TPU v7x, 32 devices: a whole 2x2x4 slice. The times are simulated.
32 devices in a mesh: dp: 2 (over core), seq: 16 (over z, y, x).
Axes of the slice: x: 2, y: 2, z: 4, core: 2. Of those that a mesh axis runs over, the one named last changes fastest.
Arguments:
- byte_ids: int32 [2, 2304], P('dp', 'seq'), may hold values from 0 to 255
- targets: int32 [2, 2304], P('dp', 'seq'), may hold values from 0 to 255
- item_lengths: int32 [2, 8], P('dp'), may hold values from 1 to 576, 2304 in all within a row
- w_qkv: float32 [2, 512, 1536], P(None, ('dp', 'seq')), may hold values from -0.25 to 0.25
- w_out: float32 [2, 512, 512], P(None, ('dp', 'seq')), may hold values from -2 to 2
- w_up: float32 [2, 512, 2048], P(None, ('dp', 'seq')), may hold values from -0.25 to 0.25
- w_down: float32 [2, 2048, 512], P(None, ('dp', 'seq')), may hold values from -0.125 to 0.125
- embed: float32 [256, 512], P(('dp', 'seq')), may hold values from -6 to 6
- head: float32 [512, 256], P(('dp', 'seq')), may hold values from -0.25 to 0.25
- gains: float32 [5, 512], P(None, ('dp', 'seq')), may hold values from 0.35 to 3.25
- mom_qkv: float32 [2, 512, 1536], P(None, ('dp', 'seq')), may hold values from -4.7683716e-06 to 4.7683716e-06
- mom_out: float32 [2, 512, 512], P(None, ('dp', 'seq')), may hold values from -4.7683716e-06 to 4.7683716e-06
- mom_up: float32 [2, 512, 2048], P(None, ('dp', 'seq')), may hold values from -4.7683716e-06 to 4.7683716e-06
- mom_down: float32 [2, 2048, 512], P(None, ('dp', 'seq')), may hold values from -4.7683716e-06 to 4.7683716e-06
- mom_embed: float32 [256, 512], P(('dp', 'seq')), may hold values from -4.7683716e-06 to 4.7683716e-06
- mom_head: float32 [512, 256], P(('dp', 'seq')), may hold values from -4.7683716e-06 to 4.7683716e-06
- mom_gains: float32 [5, 512], P(None, ('dp', 'seq')), may hold values from -7.6293945e-05 to 7.6293945e-05
- sec_qkv: float32 [2, 512, 1536], P(None, ('dp', 'seq')), may hold values from 3.2030945e-12 to 1.2812378e-11
- sec_out: float32 [2, 512, 512], P(None, ('dp', 'seq')), may hold values from 3.2030945e-12 to 1.2812378e-11
- sec_up: float32 [2, 512, 2048], P(None, ('dp', 'seq')), may hold values from 3.2030945e-12 to 1.2812378e-11
- sec_down: float32 [2, 2048, 512], P(None, ('dp', 'seq')), may hold values from 3.2030945e-12 to 1.2812378e-11
- sec_embed: float32 [256, 512], P(('dp', 'seq')), may hold values from 3.2030945e-12 to 1.2812378e-11
- sec_head: float32 [512, 256], P(('dp', 'seq')), may hold values from 3.2030945e-12 to 1.2812378e-11
- sec_gains: float32 [5, 512], P(None, ('dp', 'seq')), may hold values from 3.8132077e-11 to 1.5252831e-10
Outputs:
- loss_sum: float32 [], replicated
- grad_norm: float32 [], replicated
- w_qkv_new: float32 [2, 512, 1536], P(None, ('dp', 'seq'))
- w_out_new: float32 [2, 512, 512], P(None, ('dp', 'seq'))
- w_up_new: float32 [2, 512, 2048], P(None, ('dp', 'seq'))
- w_down_new: float32 [2, 2048, 512], P(None, ('dp', 'seq'))
- embed_new: float32 [256, 512], P(('dp', 'seq'))
- head_new: float32 [512, 256], P(('dp', 'seq'))
- gains_new: float32 [5, 512], P(None, ('dp', 'seq'))
- mom_qkv_new: float32 [2, 512, 1536], P(None, ('dp', 'seq'))
- mom_out_new: float32 [2, 512, 512], P(None, ('dp', 'seq'))
- mom_up_new: float32 [2, 512, 2048], P(None, ('dp', 'seq'))
- mom_down_new: float32 [2, 2048, 512], P(None, ('dp', 'seq'))
- mom_embed_new: float32 [256, 512], P(('dp', 'seq'))
- mom_head_new: float32 [512, 256], P(('dp', 'seq'))
- mom_gains_new: float32 [5, 512], P(None, ('dp', 'seq'))
- sec_qkv_new: float32 [2, 512, 1536], P(None, ('dp', 'seq'))
- sec_out_new: float32 [2, 512, 512], P(None, ('dp', 'seq'))
- sec_up_new: float32 [2, 512, 2048], P(None, ('dp', 'seq'))
- sec_down_new: float32 [2, 2048, 512], P(None, ('dp', 'seq'))
- sec_embed_new: float32 [256, 512], P(('dp', 'seq'))
- sec_head_new: float32 [512, 256], P(('dp', 'seq'))
- sec_gains_new: float32 [5, 512], P(None, ('dp', 'seq'))
Inputs may be any that keep to these rules, and one draw needn't show every extreme that they name: `item_lengths`: the item lengths of each group add up to 2304; the longest is exactly 576.
All inputs are finite; a program needn't handle non-finite values.
Results may differ from a plain program's by a relative error of at most 0.02.
Values may be sent and summed in bfloat16 or wider, within the bound.
A program may use at most 576 MiB of HBM per device.

v0:
```python
import jax
import jax.numpy as jnp
from jax import lax
from jax.sharding import PartitionSpec as P

HEADS = 8
VOCAB = 256
RATE = 3
STEP = 10


CLIP_NORM = 0.02
BETA_ONE = 0.9
BETA_TWO = 0.95
STEP_RATES = (0.03, 0.2, 0.03, 0.03, 0.6, 0.03, 0.2)
WEIGHT_DECAYS = (0.1, 0.1, 0.1, 0.1, 0.1, 0.1, 0.0)
EPSILON = 1e-08
NORM_EPS = 1e-05
MASK_FILL = -1e30


def shifted_2(value, axis, steps):
    count = lax.axis_size(axis)
    leading, last = (max(0, -steps), min(count, count - steps))
    return lax.ppermute(value, axis, [(source, source + steps) for source in range(leading, last)])


def to_low(values):
    return values.astype(jnp.bfloat16)


def layer_norm(values, gain):
    center = values - jnp.mean(values, axis=-1, keepdims=True)
    spread = jnp.mean(center * center, axis=-1, keepdims=True)
    return center * lax.rsqrt(spread + NORM_EPS) * gain


def rotate(joined, positions, num_heads):
    parts = joined.reshape(joined.shape[0], 3, num_heads, -1)
    half_size = parts.shape[-1] // 2
    freqs = 10000.0 ** (-jnp.arange(half_size, dtype=jnp.float32) / half_size)
    angles = positions.astype(jnp.float32)[:, None] * freqs[None, :]
    cosine = jnp.cos(angles)[:, None, :]
    sine = jnp.sin(angles)[:, None, :]

    def rotate_half(values):
        first_half = values[..., :half_size]
        second_half = values[..., half_size:]
        return jnp.concatenate(
            [first_half * cosine - second_half * sine, first_half * sine + second_half * cosine],
            axis=-1,
        )

    return (rotate_half(parts[:, 0]), rotate_half(parts[:, 1]), parts[:, 2])


def scores_for(q_low, k_low, query_pos, key_pos):
    scores = jnp.einsum(
        "rhe,phe->hrp", q_low, k_low, preferred_element_type=jnp.float32
    ) * q_low.shape[-1] ** (-0.5)
    causal = query_pos[:, None] >= key_pos[None, :]
    return (scores, causal)


def attend(q_low, k_low, v_low, query_pos):
    num_rows, num_heads, head_size = q_low.shape
    key_piece = (
        lax.all_gather(k_low, "seq", axis=0, tiled=True),
        lax.all_gather(v_low, "seq", axis=0, tiled=True),
    )
    running_max = jnp.full((num_heads, num_rows), MASK_FILL, jnp.float32)
    accum = jnp.zeros((num_rows, num_heads, head_size), jnp.float32)
    key_pos = jnp.arange(key_piece[0].shape[0], dtype=jnp.int32)
    scores, causal = scores_for(q_low, key_piece[0], query_pos, key_pos)
    scores = jnp.where(causal[None], scores, MASK_FILL)
    new_max = jnp.maximum(running_max, jnp.max(scores, axis=-1))
    factor = jnp.exp(running_max - new_max)
    attn_prob = jnp.where(causal[None], jnp.exp(scores - new_max[..., None]), 0.0)
    denom = jnp.sum(attn_prob, axis=-1)
    accum = accum * factor.T[:, :, None] + jnp.einsum(
        "hrp,phe->rhe", to_low(attn_prob), key_piece[1], preferred_element_type=jnp.float32
    )
    running_max, denom, accum = (new_max, denom, accum)
    return (accum / denom.T[:, :, None], (running_max + jnp.log(denom)).T)


def block_grads(q_low, grad_low, log_total, row_delta, query_pos, k_low, v_low, key_pos):
    scores, causal = scores_for(q_low, k_low, query_pos, key_pos)
    attn_prob = jnp.where(causal[None], jnp.exp(scores - log_total.T[:, :, None]), 0.0)
    grad_prob = jnp.einsum("rhe,phe->hrp", grad_low, v_low, preferred_element_type=jnp.float32)
    grad_score = to_low(attn_prob * (grad_prob - row_delta.T[:, :, None]))
    score_scale = q_low.shape[-1] ** (-0.5)
    grad_q = (
        jnp.einsum("hrp,phe->rhe", grad_score, k_low, preferred_element_type=jnp.float32)
        * score_scale
    )
    grad_k = (
        jnp.einsum("hrp,rhe->phe", grad_score, q_low, preferred_element_type=jnp.float32)
        * score_scale
    )
    grad_v = jnp.einsum(
        "hrp,rhe->phe", to_low(attn_prob), grad_low, preferred_element_type=jnp.float32
    )
    return (grad_q, grad_k, grad_v)


def attend_back(q_low, k_low, v_low, grad_low, log_total, row_delta, query_pos):
    key_piece = (
        lax.all_gather(k_low, "seq", axis=0, tiled=True),
        lax.all_gather(v_low, "seq", axis=0, tiled=True),
    )
    key_pos = jnp.arange(key_piece[0].shape[0], dtype=jnp.int32)
    grad_q = block_grads(
        q_low, grad_low, log_total, row_delta, query_pos, key_piece[0], key_piece[1], key_pos
    )[0]
    all_totals, all_deltas = (
        lax.all_gather(log_total, "seq", axis=0, tiled=True),
        lax.all_gather(row_delta, "seq", axis=0, tiled=True),
    )
    query_piece = (
        lax.all_gather(q_low, "seq", axis=0, tiled=True),
        lax.all_gather(grad_low, "seq", axis=0, tiled=True),
    )
    piece_rows = query_piece[0].shape[0]
    piece_pos = jnp.arange(piece_rows, dtype=jnp.int32)
    unused_q, grad_k_blk, grad_v_blk = block_grads(
        query_piece[0], query_piece[1], all_totals, all_deltas, piece_pos, k_low, v_low, query_pos
    )
    return (grad_q, grad_k_blk, grad_v_blk)


def layer_forward(hidden, weights, gain_pair, positions):
    w_joined, w_proj, w_rise, w_fall = weights
    num_rows = hidden.shape[0]
    normed = to_low(layer_norm(hidden, gain_pair[0]))
    joined = jnp.dot(normed, w_joined, preferred_element_type=jnp.float32)
    queries, keys, values = rotate(joined, positions, HEADS)
    q_low, k_low, v_low = (to_low(queries), to_low(keys), to_low(values))
    attended, log_total = attend(q_low, k_low, v_low, positions)
    flat_low = to_low(attended.reshape(num_rows, -1))
    middle = hidden + jnp.dot(flat_low, w_proj, preferred_element_type=jnp.float32)
    second = to_low(layer_norm(middle, gain_pair[1]))
    pre_act = jnp.dot(second, w_rise, preferred_element_type=jnp.float32)
    activated = to_low(jax.nn.gelu(pre_act))
    output = middle + jnp.dot(activated, w_fall, preferred_element_type=jnp.float32)
    saved = (
        normed,
        joined,
        q_low,
        k_low,
        v_low,
        attended,
        log_total,
        flat_low,
        middle,
        second,
        pre_act,
        activated,
    )
    return (output, saved)


def layer_backward(hidden, weights, gain_pair, positions, grad_out):
    w_joined, w_proj, w_rise, w_fall = weights
    unused_out, saved = layer_forward(hidden, weights, gain_pair, positions)
    (
        normed,
        joined,
        q_low,
        k_low,
        v_low,
        attended,
        log_total,
        flat_low,
        middle,
        second,
        pre_act,
        activated,
    ) = saved
    fall_low = to_low(grad_out)
    grad_fall = jnp.dot(activated.T, fall_low, preferred_element_type=jnp.float32)
    grad_act = jnp.dot(fall_low, w_fall.T, preferred_element_type=jnp.float32)
    grad_pre = to_low(jax.vjp(jax.nn.gelu, pre_act)[1](grad_act)[0])
    grad_rise = jnp.dot(second.T, grad_pre, preferred_element_type=jnp.float32)
    grad_second = jnp.dot(grad_pre, w_rise.T, preferred_element_type=jnp.float32)
    grad_middle_n, grad_gain_ffn = jax.vjp(layer_norm, middle, gain_pair[1])[1](grad_second)
    grad_middle = grad_out + grad_middle_n
    proj_low = to_low(grad_middle)
    grad_proj = jnp.dot(flat_low.T, proj_low, preferred_element_type=jnp.float32)
    grad_att = to_low(
        jnp.dot(proj_low, w_proj.T, preferred_element_type=jnp.float32).reshape(attended.shape)
    )
    row_delta = jnp.sum(grad_att.astype(jnp.float32) * attended, axis=-1)
    grad_q, grad_k, grad_v = attend_back(
        q_low, k_low, v_low, grad_att, log_total, row_delta, positions
    )

    def rotate_joined(joined_in):
        return rotate(joined_in, positions, HEADS)

    grad_joined = to_low(jax.vjp(rotate_joined, joined)[1]((grad_q, grad_k, grad_v))[0])
    grad_w_joined = jnp.dot(normed.T, grad_joined, preferred_element_type=jnp.float32)
    grad_normed = jnp.dot(grad_joined, w_joined.T, preferred_element_type=jnp.float32)
    grad_in_n, grad_gain_attn = jax.vjp(layer_norm, hidden, gain_pair[0])[1](grad_normed)
    return (
        grad_middle + grad_in_n,
        (grad_w_joined, grad_proj, grad_rise, grad_fall),
        jnp.stack([grad_gain_attn, grad_gain_ffn]),
    )


def adam_update(weight, gradient, moment_one, moment_two, step_rate, decay_rate):
    moment_one = BETA_ONE * moment_one + (1.0 - BETA_ONE) * gradient
    moment_two = BETA_TWO * moment_two + (1.0 - BETA_TWO) * gradient * gradient
    first_hat = moment_one / (1.0 - BETA_ONE**STEP)
    second_hat = moment_two / (1.0 - BETA_TWO**STEP)
    weight = weight - step_rate * (
        first_hat / (jnp.sqrt(second_hat) + EPSILON) + decay_rate * weight
    )
    return (weight, moment_one, moment_two)


def on_device(
    byte_ids,
    targets,
    item_lengths,
    w_qkv,
    w_out,
    w_up,
    w_down,
    embed,
    head,
    gains,
    mom_qkv,
    mom_out,
    mom_up,
    mom_down,
    mom_embed,
    mom_head,
    mom_gains,
    sec_qkv,
    sec_out,
    sec_up,
    sec_down,
    sec_embed,
    sec_head,
    sec_gains,
):
    low_qkv, low_out, low_up, low_down, low_embed, low_head, low_gains = (
        lax.all_gather(to_low(w_qkv), ("dp", "seq"), axis=1, tiled=True),
        lax.all_gather(to_low(w_out), ("dp", "seq"), axis=1, tiled=True),
        lax.all_gather(to_low(w_up), ("dp", "seq"), axis=1, tiled=True),
        lax.all_gather(to_low(w_down), ("dp", "seq"), axis=1, tiled=True),
        lax.all_gather(to_low(embed), ("dp", "seq"), axis=0, tiled=True),
        lax.all_gather(to_low(head), ("dp", "seq"), axis=0, tiled=True),
        lax.all_gather(to_low(gains), ("dp", "seq"), axis=1, tiled=True),
    )
    gain_rows = low_gains.astype(jnp.float32)
    byte_row = byte_ids[0]
    num_rows = byte_row.shape[0]
    short_rows = num_rows // RATE
    seq_place = lax.axis_index("seq")
    positions = seq_place * num_rows + jnp.arange(num_rows, dtype=jnp.int32)
    short_pos = seq_place * short_rows + jnp.arange(short_rows, dtype=jnp.int32)
    vocab_ids = jnp.arange(VOCAB, dtype=jnp.int32)
    one_hot_in = (byte_row[:, None] == vocab_ids[None, :]).astype(jnp.float32)
    embedded = jnp.dot(
        one_hot_in.astype(jnp.bfloat16), low_embed, preferred_element_type=jnp.float32
    )
    lower_weights = (low_qkv[0], low_out[0], low_up[0], low_down[0])
    upper_weights = (low_qkv[1], low_out[1], low_up[1], low_down[1])
    first_out, unused_first = layer_forward(embedded, lower_weights, gain_rows[0:2], positions)
    left_rim = shifted_2(first_out[num_rows - RATE + 1 :], "seq", 1)
    shifted = jnp.concatenate([left_rim, first_out[: num_rows - RATE + 1]], axis=0)
    pooled = jnp.mean(shifted.reshape(short_rows, RATE, -1), axis=1)
    short_out, unused_short = layer_forward(pooled, upper_weights, gain_rows[2:4], short_pos)
    upsampled = first_out + jnp.repeat(short_out, RATE, axis=0)
    top_gain = gain_rows[gain_rows.shape[0] - 1]
    final_low = to_low(layer_norm(upsampled, top_gain))
    logits = jnp.dot(final_low, low_head, preferred_element_type=jnp.float32)
    row_max = jnp.max(logits, axis=-1, keepdims=True)
    log_total = row_max[:, 0] + jnp.log(jnp.sum(jnp.exp(logits - row_max), axis=-1))
    one_hot_out = (targets[0][:, None] == vocab_ids[None, :]).astype(jnp.float32)
    picked = jnp.sum(one_hot_out * logits, axis=-1)
    lengths = item_lengths[0]
    ends = jnp.cumsum(lengths)
    doc_index = jnp.sum((positions[:, None] >= ends[None, :]).astype(jnp.int32), axis=1)
    item_ids = jnp.arange(lengths.shape[0], dtype=jnp.int32)
    doc_length = jnp.sum(
        jnp.where(item_ids[None, :] == doc_index[:, None], lengths[None, :], 0), axis=1
    ).astype(jnp.float32)
    loss_local = jnp.sum((log_total - picked) / doc_length)
    loss_sum = lax.psum(loss_local, ("dp", "seq"))
    grad_logits = to_low((jnp.exp(logits - log_total[:, None]) - one_hot_out) / doc_length[:, None])
    grad_head = jnp.dot(final_low.T, grad_logits, preferred_element_type=jnp.float32)
    grad_final = jnp.dot(grad_logits, low_head.T, preferred_element_type=jnp.float32)
    grad_upsampled, grad_gain_top = jax.vjp(layer_norm, upsampled, top_gain)[1](grad_final)
    grad_short = jnp.sum(grad_upsampled.reshape(short_rows, RATE, -1), axis=1)
    grad_pooled, upper_grads, upper_gain_grads = layer_backward(
        pooled, upper_weights, gain_rows[2:4], short_pos, grad_short
    )
    grad_shifted = jnp.repeat(grad_pooled / RATE, RATE, axis=0)
    rim_grad = shifted_2(grad_shifted[: RATE - 1], "seq", -1)
    grad_first = grad_upsampled + jnp.concatenate([grad_shifted[RATE - 1 :], rim_grad], axis=0)
    grad_embedded, lower_grads, lower_gain_grads = layer_backward(
        embedded, lower_weights, gain_rows[0:2], positions, grad_first
    )
    grad_embed = jnp.dot(one_hot_in.T, grad_embedded, precision=lax.Precision.HIGHEST)
    grad_gains = jnp.concatenate(
        [lower_gain_grads, upper_gain_grads, grad_gain_top[None, :]], axis=0
    )
    shard_grads = (
        lax.psum_scatter(
            jnp.stack([lower_grads[0], upper_grads[0]]),
            ("dp", "seq"),
            scatter_dimension=1,
            tiled=True,
        ),
        lax.psum_scatter(
            jnp.stack([lower_grads[1], upper_grads[1]]),
            ("dp", "seq"),
            scatter_dimension=1,
            tiled=True,
        ),
        lax.psum_scatter(
            jnp.stack([lower_grads[2], upper_grads[2]]),
            ("dp", "seq"),
            scatter_dimension=1,
            tiled=True,
        ),
        lax.psum_scatter(
            jnp.stack([lower_grads[3], upper_grads[3]]),
            ("dp", "seq"),
            scatter_dimension=1,
            tiled=True,
        ),
        lax.psum_scatter(grad_embed, ("dp", "seq"), scatter_dimension=0, tiled=True),
        lax.psum_scatter(grad_head, ("dp", "seq"), scatter_dimension=0, tiled=True),
        lax.psum_scatter(grad_gains, ("dp", "seq"), scatter_dimension=1, tiled=True),
    )
    squares = sum((jnp.sum(piece_grad * piece_grad) for piece_grad in shard_grads))
    total_squares = lax.psum(squares, ("dp", "seq"))
    grad_norm = jnp.sqrt(total_squares)
    clip_factor = jnp.minimum(1.0, CLIP_NORM / grad_norm)
    masters = (w_qkv, w_out, w_up, w_down, embed, head, gains)
    firsts = (mom_qkv, mom_out, mom_up, mom_down, mom_embed, mom_head, mom_gains)
    seconds = (sec_qkv, sec_out, sec_up, sec_down, sec_embed, sec_head, sec_gains)
    results = []
    for slot_index in range(7):
        results.append(
            adam_update(
                masters[slot_index],
                shard_grads[slot_index] * clip_factor,
                firsts[slot_index],
                seconds[slot_index],
                STEP_RATES[slot_index],
                WEIGHT_DECAYS[slot_index],
            )
        )
    return (
        loss_sum,
        grad_norm,
        results[0][0],
        results[1][0],
        results[2][0],
        results[3][0],
        results[4][0],
        results[5][0],
        results[6][0],
        results[0][1],
        results[1][1],
        results[2][1],
        results[3][1],
        results[4][1],
        results[5][1],
        results[6][1],
        results[0][2],
        results[1][2],
        results[2][2],
        results[3][2],
        results[4][2],
        results[5][2],
        results[6][2],
    )


def solution(mesh):
    return jax.shard_map(
        on_device,
        mesh=mesh,
        in_specs=(
            P("dp", "seq"),
            P("dp", "seq"),
            P("dp", None),
            P(None, ("dp", "seq"), None),
            P(None, ("dp", "seq"), None),
            P(None, ("dp", "seq"), None),
            P(None, ("dp", "seq"), None),
            P(("dp", "seq"), None),
            P(("dp", "seq"), None),
            P(None, ("dp", "seq")),
            P(None, ("dp", "seq"), None),
            P(None, ("dp", "seq"), None),
            P(None, ("dp", "seq"), None),
            P(None, ("dp", "seq"), None),
            P(("dp", "seq"), None),
            P(("dp", "seq"), None),
            P(None, ("dp", "seq")),
            P(None, ("dp", "seq"), None),
            P(None, ("dp", "seq"), None),
            P(None, ("dp", "seq"), None),
            P(None, ("dp", "seq"), None),
            P(("dp", "seq"), None),
            P(("dp", "seq"), None),
            P(None, ("dp", "seq")),
        ),
        out_specs=(
            P(),
            P(),
            P(None, ("dp", "seq"), None),
            P(None, ("dp", "seq"), None),
            P(None, ("dp", "seq"), None),
            P(None, ("dp", "seq"), None),
            P(("dp", "seq"), None),
            P(("dp", "seq"), None),
            P(None, ("dp", "seq")),
            P(None, ("dp", "seq"), None),
            P(None, ("dp", "seq"), None),
            P(None, ("dp", "seq"), None),
            P(None, ("dp", "seq"), None),
            P(("dp", "seq"), None),
            P(("dp", "seq"), None),
            P(None, ("dp", "seq")),
            P(None, ("dp", "seq"), None),
            P(None, ("dp", "seq"), None),
            P(None, ("dp", "seq"), None),
            P(None, ("dp", "seq"), None),
            P(("dp", "seq"), None),
            P(("dp", "seq"), None),
            P(None, ("dp", "seq")),
        ),
        check_vma=False,
    )
```

profile of v0, /device:TPU:0, one launch (start us, length us, event | category | flops | bytes accessed | tf_op | source)
XLA Modules:
  0.0 1994.6 jit_solution(5919763779874701490)
XLA Ops:
  11.2 72.1 %all_gather.65 = bf16[256,512]{1,0:T(8,128)(2,1)S(1)} all-gather(bf16[8,512]{1,0:T(8,128)(2,1)S(1)} %convert_element_type.197), channel_id=1, replica_groups=mesh['dp'=2,'seq'=16] {'dp','seq'}, dimensions={0}, use_global_device_ids=true | all-gather | bytes 270336 | tf_op jit(solution)/shard_map/all_gather | solution.py:254
  85.8 63.9 %all-gather.2 = bf16[32,16,5]{1,2,0:T(8,128)(2,1)S(1)} all-gather(bf16[1,16,5]{1,2,0:T(8,128)(2,1)S(1)} %convert_bitcast_fusion), channel_id=1, replica_groups=mesh['dp'=2,'seq'=16] {'dp','seq'}, dimensions={0}, use_global_device_ids=true | all-gather | bytes 5280 | tf_op jit(solution)/shard_map/all_gather | solution.py:256
  161.1 74.7 %all_gather.75 = bf16[512,256]{1,0:T(8,128)(2,1)} all-gather(bf16[16,256]{1,0:T(8,128)(2,1)S(1)} %convert_element_type.221), channel_id=1, replica_groups=mesh['dp'=2,'seq'=16] {'dp','seq'}, dimensions={0}, use_global_device_ids=true | all-gather | bytes 270336 | tf_op jit(solution)/shard_map/all_gather | solution.py:255
  240.6 5.6 copy.104
  246.2 74.9 %all-gather.30.cloned.1.call-done = bf16[2304,1,8,64]{3,2,1,0:T(8,128)(2,1)} async-done(((bf16[144,1,8,64]{3,2,1,0:T(8,128)(2,1)}), bf16[2304,1,8,64]{3,2,1,0:T(8,128)(2,1)}) %all-gather.30.cloned.1.call-update) | async-done | bytes 2359312 | tf_op jit(solution)/shard_map/all_gather | solution.py:69
  321.2 6.6 copy.106
  338.7 46.4 %all-gather.22.cloned.1.call-done = bf16[2,512,2048]{2,1,0:T(8,128)(2,1)} async-done(((bf16[2,16,2048]{2,1,0:T(8,128)(2,1)}), bf16[2,512,2048]{2,1,0:T(8,128)(2,1)}) %all-gather.22.cloned.1.call-update) | async-done | bytes 4194320 | tf_op jit(solution)/shard_map/all_gather | solution.py:252
  387.3 61.7 %all-gather.24.cloned.1.call-done = bf16[2,2048,512]{2,1,0:T(8,128)(2,1)} async-done(((bf16[2,64,512]{2,1,0:T(8,128)(2,1)}), bf16[2,2048,512]{2,1,0:T(8,128)(2,1)}) %all-gather.24.cloned.1.call-update) | async-done | bytes 4194320 | tf_op jit(solution)/shard_map/all_gather | solution.py:253
  461.3 57.7 %all_gather.73 = bf16[768,8,64]{2,0,1:T(8,128)(2,1)S(1)} all-gather(bf16[48,8,64]{2,0,1:T(8,128)(2,1)S(1)} %pad_maximum_fusion.8), channel_id=1, replica_groups=mesh['dp'=2,'seq'=16] {'seq'}, dimensions={0}, use_global_device_ids=true | all-gather | bytes 835584 | tf_op jit(solution)/shard_map/all_gather | solution.py:68
  519.1 67.4 %all_gather.77 = bf16[768,8,64]{2,0,1:T(8,128)(2,1)} all-gather(bf16[48,8,64]{2,0,1:T(8,128)(2,1)S(1)} %pad_maximum_fusion.7), channel_id=1, replica_groups=mesh['dp'=2,'seq'=16] {'seq'}, dimensions={0}, use_global_device_ids=true | all-gather | bytes 835584 | tf_op jit(solution)/shard_map/all_gather | solution.py:121
  588.9 46.8 %all-gather.1 = bf16[768,1,8,64]{3,0,2,1:T(8,128)(2,1)S(1)} all-gather(bf16[48,1,8,64]{3,0,2,1:T(8,128)(2,1)S(1)} %slice.248), channel_id=3, replica_groups=mesh['dp'=2,'seq'=16] {'seq'}, dimensions={0}, use_global_device_ids=true | all-gather | bytes 835584 | tf_op jit(solution)/shard_map/all_gather | solution.py:69
  659.6 47.1 %all_gather.76 = bf16[768,8,64]{2,0,1:T(8,128)(2,1)S(1)} all-gather(bf16[48,8,64]{2,0,1:T(8,128)(2,1)S(1)} %get-tuple-element.136), channel_id=1, replica_groups=mesh['dp'=2,'seq'=16] {'seq'}, dimensions={0}, use_global_device_ids=true | all-gather | bytes 835584 | tf_op jit(solution)/shard_map/all_gather | solution.py:122
  706.7 37.4 %all-gather.3 = f32[16,48,8]{1,2,0:T(8,128)S(1)} all-gather(f32[1,48,8]{1,2,0:T(8,128)S(1)} %copy-done.119), channel_id=1, replica_groups=mesh['dp'=2,'seq'=16] {'seq'}, dimensions={0}, use_global_device_ids=true | all-gather | bytes 26112 | tf_op jit(solution)/shard_map/all_gather | solution.py:117
  746.3 36.4 %all-gather.4 = f32[16,48,8]{1,2,0:T(8,128)S(1)} all-gather(f32[1,48,8]{1,2,0:T(8,128)} %bitcast.315), channel_id=1, replica_groups=mesh['dp'=2,'seq'=16] {'seq'}, dimensions={0}, use_global_device_ids=true | all-gather | bytes 26112 | tf_op jit(solution)/shard_map/all_gather | solution.py:118
  802.3 4.0 collective-permute-done.1
  815.1 38.9 %all-gather.5 = f32[16,144,8]{1,2,0:T(8,128)S(1)} all-gather(f32[1,144,8]{1,2,0:T(8,128)S(1)} %copy-done.96), channel_id=1, replica_groups=mesh['dp'=2,'seq'=16] {'seq'}, dimensions={0}, use_global_device_ids=true | all-gather | bytes 78336 | tf_op jit(solution)/shard_map/all_gather | solution.py:117
  854.8 5.6 copy.116
  860.4 6.7 fusion.187
  869.3 11.0 fusion.67
  880.2 36.8 %all-gather.6 = f32[16,144,8]{1,2,0:T(8,128)S(1)} all-gather(f32[1,144,8]{1,2,0:T(8,128)S(1)} %bitcast.326), channel_id=1, replica_groups=mesh['dp'=2,'seq'=16] {'seq'}, dimensions={0}, use_global_device_ids=true | all-gather | bytes 78336 | tf_op jit(solution)/shard_map/all_gather | solution.py:118
  919.4 6.6 copy.118
  926.0 10.4 fusion.71
  938.4 6.5 fusion.56
  962.8 4.3 pad_maximum_fusion.1
  967.3 63.3 %reduce-scatter.20.cloned.1.call-done = f32[16,256]{1,0:T(8,128)} async-done(((f32[512,256]{1,0:T(8,128)}), f32[16,256]{1,0:T(8,128)}) %reduce-scatter.20.cloned.1.call-update) | async-done | bytes 16400 | tf_op jit(solution)/shard_map/reduce_scatter | solution.py:338
  1031.9 140.3 %reduce-scatter.12.cloned.1.call-done = f32[2,16,512]{2,1,0:T(8,128)} async-done(((f32[2,512,512]{2,1,0:T(8,128)}), f32[2,16,512]{2,1,0:T(8,128)}) %reduce-scatter.12.cloned.1.call-update) | async-done | bytes 65552 | tf_op jit(solution)/shard_map/reduce_scatter | solution.py:319
  1173.6 135.1 %reduce-scatter.22.cloned.1.call-done = f32[16,5]{1,0:T(8,128)} async-done(((f32[512,5]{1,0:T(8,128)}), f32[16,5]{1,0:T(8,128)}) %reduce-scatter.22.cloned.1.call-update) | async-done | bytes 336
  1310.1 134.8 %reduce-scatter.18.cloned.1.call-done = f32[8,512]{1,0:T(8,128)} async-done(((f32[256,512]{1,0:T(8,128)}), f32[8,512]{1,0:T(8,128)}) %reduce-scatter.18.cloned.1.call-update) | async-done | bytes 16400 | tf_op jit(solution)/shard_map/reduce_scatter | solution.py:337
  1446.1 115.3 %reduce-scatter.10.cloned.1.call-done = f32[2,16,1536]{2,1,0:T(8,128)} async-done(((f32[2,512,1536]{2,1,0:T(8,128)}), f32[2,16,1536]{2,1,0:T(8,128)}) %reduce-scatter.10.cloned.1.call-update) | async-done | bytes 196624 | tf_op jit(solution)/shard_map/reduce_scatter | solution.py:313
  1564.3 182.6 %reduce-scatter.14.cloned.1.call-done = f32[2,16,2048]{2,1,0:T(8,128)} async-done(((f32[2,512,2048]{2,1,0:T(8,128)}), f32[2,16,2048]{2,1,0:T(8,128)}) %reduce-scatter.14.cloned.1.call-update) | async-done | bytes 262160 | tf_op jit(solution)/shard_map/reduce_scatter | solution.py:325
  1749.3 184.5 %reduce-scatter.16.cloned.1.call-done = f32[2,64,512]{2,1,0:T(8,128)} async-done(((f32[2,2048,512]{2,1,0:T(8,128)}), f32[2,64,512]{2,1,0:T(8,128)}) %reduce-scatter.16.cloned.1.call-update) | async-done | bytes 262160 | tf_op jit(solution)/shard_map/reduce_scatter | solution.py:331
  1938.0 39.9 %all-reduce.14 = (f32[]{:T(128)}, f32[]{:T(128)}) all-reduce(f32[]{:T(128)} %get-tuple-element.68, f32[]{:T(128)S(6)} %add.406), channel_id=1, replica_groups=mesh['dp'=2,'seq'=16] {'dp','seq'}, use_global_device_ids=true, to_apply=%region_22.23 | all-reduce | flops 2 | bytes 16 | tf_op jit(solution)/shard_map/psum | solution.py:293
  (533 shorter events, 146.8 us)
Async XLA Ops:
  7.2 143.7 %all-gather.16.cloned.1.call-start = ((), (), s32[]{:S(2)}) async-start(), calls=%async_computation.7 | async-start | bytes 3244032 | tf_op jit(solution)/shard_map/all_gather | solution.py:250
  8.8 229.4 %all-gather.20.cloned.1.call-start = ((), (), s32[]{:S(2)}) async-start(), calls=%async_computation.9 | async-start | bytes 1081344 | tf_op jit(solution)/shard_map/all_gather | solution.py:251
  10.4 230.3 %all-gather.18.cloned.1.call-start = ((), (), s32[]{:S(2)}) async-start(), calls=%async_computation.8 | async-start | bytes 5013504 | tf_op jit(solution)/shard_map/all_gather | solution.py:68
  157.5 163.7 %all-gather.30.cloned.1.call-start = ((), (), s32[]{:S(2)}) async-start(), calls=%async_computation.20 | async-start | bytes 5013504 | tf_op jit(solution)/shard_map/all_gather | solution.py:69
  158.5 226.6 %all-gather.22.cloned.1.call-start = ((), (), s32[]{:S(2)}) async-start(), calls=%async_computation.10 | async-start | bytes 4325376 | tf_op jit(solution)/shard_map/all_gather | solution.py:252
  159.3 289.7 %all-gather.24.cloned.1.call-start = ((), (), s32[]{:S(2)}) async-start(), calls=%async_computation.11 | async-start | bytes 4325376 | tf_op jit(solution)/shard_map/all_gather | solution.py:253
  160.0 694.8 %all-gather.28.cloned.1.call-start = ((), (), s32[]{:S(2)}) async-start(), calls=%async_computation.13 | async-start | bytes 5013504 | tf_op jit(solution)/shard_map/all_gather | solution.py:121
  451.3 6.9 collective-permute-start
  458.0 461.4 %all-gather.26.cloned.1.call-start = ((), (), s32[]{:S(2)}) async-start(), calls=%async_computation.12 | async-start | bytes 5013504 | tf_op jit(solution)/shard_map/all_gather | solution.py:122
  800.7 5.5 collective-permute-start.1
  812.7 217.9 %reduce-scatter.20.cloned.1.call-start = ((), (), s32[]{:S(2)}) async-start(), calls=%async_computation.19 | async-start | bytes 540672 | tf_op jit(solution)/shard_map/reduce_scatter | solution.py:338
  815.0 357.1 %reduce-scatter.12.cloned.1.call-start = ((), (), s32[]{:S(2)}) async-start(), calls=%async_computation.15 | async-start | bytes 2162688 | tf_op jit(solution)/shard_map/reduce_scatter | solution.py:319
  869.2 439.4 %reduce-scatter.22.cloned.1.call-start = ((), (), s32[]{:S(2)}) async-start(), calls=%async_computation.21 | async-start | bytes 270336
  947.6 497.2 %reduce-scatter.18.cloned.1.call-start = ((), (), s32[]{:S(2)}) async-start(), calls=%async_computation.18 | async-start | bytes 540672 | tf_op jit(solution)/shard_map/reduce_scatter | solution.py:337
  949.1 612.4 %reduce-scatter.10.cloned.1.call-start = ((), (), s32[]{:S(2)}) async-start(), calls=%async_computation.14 | async-start | bytes 6488064 | tf_op jit(solution)/shard_map/reduce_scatter | solution.py:313
  953.7 793.2 %reduce-scatter.14.cloned.1.call-start = ((), (), s32[]{:S(2)}) async-start(), calls=%async_computation.16 | async-start | bytes 8650752 | tf_op jit(solution)/shard_map/reduce_scatter | solution.py:325
  960.3 973.5 %reduce-scatter.16.cloned.1.call-start = ((), (), s32[]{:S(2)}) async-start(), calls=%async_computation.17 | async-start | bytes 8650752 | tf_op jit(solution)/shard_map/reduce_scatter | solution.py:331
  967.1 1011.5 %copy-start.118 = (f32[5,16]{1,0:T(8,128)S(1)}, f32[5,16]{1,0:T(8,128)}, u32[]{:S(2)}) copy-start(f32[5,16]{1,0:T(8,128)} %param.33) | copy-start | bytes 964
  967.1 1011.5 %copy-start.142 = (f32[5,16]{1,0:T(8,128)S(1)}, f32[5,16]{1,0:T(8,128)}, u32[]{:S(2)}) copy-start(f32[5,16]{1,0:T(8,128)} %param.40) | copy-start | bytes 964
  967.1 1011.6 %copy-start.143 = (f32[5,16]{1,0:T(8,128)S(1)}, f32[5,16]{1,0:T(8,128)}, u32[]{:S(2)}) copy-start(f32[5,16]{1,0:T(8,128)} %param.47) | copy-start | bytes 964
  967.1 1012.2 %copy-start.88 = (f32[16,256]{1,0:T(8,128)S(1)}, f32[16,256]{1,0:T(8,128)}, u32[]{:S(2)}) copy-start(f32[16,256]{1,0:T(8,128)} %param.32) | copy-start | bytes 49156
  967.1 1012.2 %copy-start.114 = (f32[16,256]{1,0:T(8,128)S(1)}, f32[16,256]{1,0:T(8,128)}, u32[]{:S(2)}) copy-start(f32[16,256]{1,0:T(8,128)} %param.39) | copy-start | bytes 49156
  967.1 1012.2 %copy-start.115 = (f32[16,256]{1,0:T(8,128)S(1)}, f32[16,256]{1,0:T(8,128)}, u32[]{:S(2)}) copy-start(f32[16,256]{1,0:T(8,128)} %param.46) | copy-start | bytes 49156
  967.2 1013.5 %copy-start.89 = (f32[8,512]{1,0:T(8,128)S(1)}, f32[8,512]{1,0:T(8,128)}, u32[]{:S(2)}) copy-start(f32[8,512]{1,0:T(8,128)} %param.31) | copy-start | bytes 49156
  967.2 1013.5 %copy-start.116 = (f32[8,512]{1,0:T(8,128)S(1)}, f32[8,512]{1,0:T(8,128)}, u32[]{:S(2)}) copy-start(f32[8,512]{1,0:T(8,128)} %param.38) | copy-start | bytes 49156
  967.2 1013.5 %copy-start.117 = (f32[8,512]{1,0:T(8,128)S(1)}, f32[8,512]{1,0:T(8,128)}, u32[]{:S(2)}) copy-start(f32[8,512]{1,0:T(8,128)} %param.45) | copy-start | bytes 49156
  967.2 1015.0 %copy-start.46 = (f32[2,64,512]{2,1,0:T(8,128)S(1)}, f32[2,64,512]{2,1,0:T(8,128)}, u32[]{:S(2)}) copy-start(f32[2,64,512]{2,1,0:T(8,128)} %param.30) | copy-start | bytes 786436
  967.2 1015.0 %copy-start.75 = (f32[2,64,512]{2,1,0:T(8,128)S(1)}, f32[2,64,512]{2,1,0:T(8,128)}, u32[]{:S(2)}) copy-start(f32[2,64,512]{2,1,0:T(8,128)} %param.37) | copy-start | bytes 786436
  967.2 1014.9 %copy-start.76 = (f32[2,64,512]{2,1,0:T(8,128)S(1)}, f32[2,64,512]{2,1,0:T(8,128)}, u32[]{:S(2)}) copy-start(f32[2,64,512]{2,1,0:T(8,128)} %param.44) | copy-start | bytes 786436
  967.3 1016.9 %copy-start.48 = (f32[2,16,2048]{2,1,0:T(8,128)S(1)}, f32[2,16,2048]{2,1,0:T(8,128)}, u32[]{:S(2)}) copy-start(f32[2,16,2048]{2,1,0:T(8,128)} %param.29) | copy-start | bytes 786436
  967.3 1016.9 %copy-start.77 = (f32[2,16,2048]{2,1,0:T(8,128)S(1)}, f32[2,16,2048]{2,1,0:T(8,128)}, u32[]{:S(2)}) copy-start(f32[2,16,2048]{2,1,0:T(8,128)} %param.36) | copy-start | bytes 786436
  967.3 1016.9 %copy-start.78 = (f32[2,16,2048]{2,1,0:T(8,128)S(1)}, f32[2,16,2048]{2,1,0:T(8,128)}, u32[]{:S(2)}) copy-start(f32[2,16,2048]{2,1,0:T(8,128)} %param.43) | copy-start | bytes 786436
  (143 other events, 3703.9 us)
Sparse Core Ops, SparseCore 0:
  11.5 62.6 all-gather.15
  77.8 52.1 all-gather.19
  157.6 81.2 all-gather.17
  241.5 79.6 all-gather.29
  324.5 60.5 all-gather.21
  388.5 60.4 all-gather.23
  458.1 107.5 all-gather.27
  812.8 80.0 all-gather.25
  895.2 135.3 reduce-scatter.19
  1032.8 139.3 reduce-scatter.11
  1175.0 133.6 reduce-scatter.21
  1310.9 133.9 reduce-scatter.17
  1450.5 110.9 reduce-scatter.9
  1563.7 183.1 reduce-scatter.13
  1749.2 184.5 reduce-scatter.15
where the time goes:
time: 2000 us; the launch traced here: 1990 us
  waiting for transfers between devices  1140 us (57%)
  blocking collectives  619 us (31%)
  matrix products  90.2 us (5%)
  other arithmetic  58.7 us (3%)
  local copies, waits for them, and re-layouts  54.8 us (3%)
  between operations  22.8 us (1%)
    reduce_scatter x1, waiting for transfers between devices, on_device(): lax.psum_scatter(jnp.stack([lower_grads[3], upper_grads[3]]), ('dp', 'seq...  184 us
    reduce_scatter x1, waiting for transfers between devices, on_device(): lax.psum_scatter(jnp.stack([lower_grads[2], upper_grads[2]]), ('dp', 'seq...  183 us
    reduce_scatter x1, waiting for transfers between devices, on_device(): lax.psum_scatter(jnp.stack([lower_grads[1], upper_grads[1]]), ('dp', 'seq...  140 us
    unnamed x16, waiting for transfers between devices  135 us
    reduce_scatter x1, waiting for transfers between devices, on_device(): lax.psum_scatter(grad_embed, ('dp', 'seq'), scatter_dimension=0, tiled=True)  135 us
    reduce_scatter x1, waiting for transfers between devices, on_device(): lax.psum_scatter(jnp.stack([lower_grads[0], upper_grads[0]]), ('dp', 'seq...  115 us
    all_gather x2, blocking collectives, attend_back(): lax.all_gather(log_total, 'seq', axis=0, tiled=True)  76.3 us
    all_gather x1, waiting for transfers between devices, attend(): lax.all_gather(v_low, 'seq', axis=0, tiled=True)  74.9 us
  transfers between devices with their start and end apart: 17, of which 11 were waited for; matrix products, arithmetic and copies ran while one was open for 9% of the time, Pallas kernels for 0%

commit v1 on v0

--- a/solution.py
+++ b/solution.py
@@ -1,13 +1,16 @@
+import functools
+
 import jax
 import jax.numpy as jnp
 from jax import lax
+from jax.experimental import pallas as pl
+from jax.experimental.pallas import tpu as pltpu
 from jax.sharding import PartitionSpec as P
 
 HEADS = 8
 VOCAB = 256
 RATE = 3
 STEP = 10
-
 
 CLIP_NORM = 0.02
 BETA_ONE = 0.9
@@ -220,7 +223,7 @@
     return (weight, moment_one, moment_two)
 
 
-def on_device(
+def on_device_general(
     byte_ids,
     targets,
     item_lengths,
@@ -384,60 +387,861 @@
     )
 
 
+LOW = jnp.bfloat16
+F32 = jnp.float32
+MESH = pl.DeviceIdType.MESH
+D = 512
+
+EH, GN, LAYER0, LAYER_ROWS = 0, 16, 32, 192
+QKV, OUT, UP, DOWN = 0, 48, 64, 128
+ROWS = LAYER0 + 2 * LAYER_ROWS
+
+
+def dot(a, b):
+    return jnp.dot(a, b, preferred_element_type=F32)
+
+
+def dot_nt(a, b):
+    return lax.dot_general(a, b, (((1,), (1,)), ((), ())), preferred_element_type=F32)
+
+
+def dot_tn(a, b):
+    return lax.dot_general(a, b, (((0,), (0,)), ((), ())), preferred_element_type=F32)
+
+
+def low(v):
+    return v.astype(LOW)
+
+
+def lanes(shape):
+    return lax.broadcasted_iota(jnp.int32, shape, len(shape) - 1)
+
+
+def roll64(v):
+    return pltpu.roll(v, 64, 1)
+
+
+def swap32(v):
+    return jnp.where(lanes(v.shape) % 64 < 32, pltpu.roll(v, 96, 1), pltpu.roll(v, 32, 1))
+
+
+def norm_parts(v):
+    center = v - jnp.mean(v, axis=-1, keepdims=True)
+    scale = lax.rsqrt(jnp.mean(center * center, axis=-1, keepdims=True) + NORM_EPS)
+    return center * scale, scale
+
+
+def norm_back(v, gain, grad):
+    unit, scale = norm_parts(v)
+    g = grad * gain
+    out = scale * (g - jnp.mean(g, axis=-1, keepdims=True) - unit * jnp.mean(g * unit, axis=-1, keepdims=True))
+    return out, jnp.sum(grad * unit, axis=0, keepdims=True)
+
+
+GELU_A, GELU_B = 0.7978845608028654, 0.044715
+
+
+def gelu(v):
+    return 0.5 * v * (1.0 + jnp.tanh(GELU_A * (v + GELU_B * v * v * v)))
+
+
+def gelu_grad(v):
+    t = jnp.tanh(GELU_A * (v + GELU_B * v * v * v))
+    return 0.5 * (1.0 + t) + 0.5 * v * (1.0 - t * t) * (GELU_A * (1.0 + 3.0 * GELU_B * v * v))
+
+
+class Bag:
+    pass
+
+
+def remote(src, dst, send, recv, device):
+    return pltpu.make_async_remote_copy(
+        src_ref=src, dst_ref=dst, send_sem=send, recv_sem=recv, device_id=device, device_id_type=MESH
+    )
+
+
+def pack_pair(block, odd):
+    half = block.shape[0] // 2
+    top, bottom = block[:half], block[half:]
+    if odd:
+        top = roll64(top)
+    else:
+        bottom = roll64(bottom)
+    return jnp.where(lanes(top.shape) < 64, top, bottom)
+
+
+def unpack_pair(even, odd):
+    left = lanes(even.shape) < 64
+    top = jnp.where(left, even, roll64(odd))
+    bottom = jnp.where(left, roll64(even), odd)
+    return jnp.concatenate([top, bottom], axis=0)
+
+
+def unpack_left(x):
+    left = lanes(x.shape) < 64
+    return jnp.concatenate([jnp.where(left, x, 0.0), jnp.where(left, roll64(x), 0.0)], axis=0)
+
+
+def unpack_right(x):
+    left = lanes(x.shape) < 64
+    return jnp.concatenate([jnp.where(left, 0.0, roll64(x)), jnp.where(left, 0.0, x)], axis=0)
+
+
+def pack_left(x):
+    half = x.shape[0] // 2
+    return jnp.where(lanes((half, 128)) < 64, x[:half], roll64(x[half:]))
+
+
+def pack_right(x):
+    half = x.shape[0] // 2
+    return jnp.where(lanes((half, 128)) < 64, roll64(x[:half]), x[half:])
+
+
+def kernel(*refs):
+    k = Bag()
+    names = IN_NAMES + OUT_NAMES + tuple(SCRATCH)
+    for name, ref in zip(names, refs[:-2]):
+        setattr(k, name, ref)
+    k.ss, k.rs = refs[-2:]
+    for name in PER_LAYER:
+        setattr(k, name, [getattr(k, name + "0"), getattr(k, name + "1")])
+    k.hold = []
+    for layer in range(2):
+        hold = Bag()
+        for name in HELD:
+            setattr(hold, name, getattr(k, "h_" + name + str(layer)))
+        k.hold.append(hold)
+    g = lax.axis_index("dp")
+    s = lax.axis_index("seq")
+    z, y, x = s // 4, lax.rem(s // 2, 2), lax.rem(s, 2)
+    k.g, k.s, k.z, k.y, k.x = g, s, z, y, x
+    k.side = lax.rem(x + y, 2)
+    k.cursor = 0
+
+    def dev(g, z, y, x):
+        return (g, z * 4 + y * 2 + x)
+
+    k.dev = dev
+
+    barrier = pltpu.get_barrier_semaphore()
+    me = g * 16 + s
+
+    @pl.loop(1, 32)
+    def _(i):
+        t = lax.rem(me + i, 32)
+        pl.semaphore_signal(barrier, inc=1, device_id=(t // 16, lax.rem(t, 16)), device_id_type=MESH)
+
+    own = k.pk.at[g, z, y, x]
+    own[EH : EH + 16, 0:256] = low(k.head[...])
+    own[EH : EH + 16, 256:512] = low(jnp.concatenate([k.embed[:, 0:256], k.embed[:, 256:512]], axis=0))
+    own[GN : GN + 16, :] = low(k.gains[...])
+    for layer in range(2):
+        base = LAYER0 + layer * LAYER_ROWS
+        own[base + QKV : base + QKV + 16, :] = low(k.w_qkv[layer, :, 0:512])
+        for pair in range(4):
+            keys = k.w_qkv[layer, :, 512 + 128 * pair : 640 + 128 * pair]
+            vals = k.w_qkv[layer, :, 1024 + 128 * pair : 1152 + 128 * pair]
+            left = lanes(keys.shape) < 64
+            row = base + QKV + 16 + 16 * (pair // 2)
+            col = 256 * (pair % 2)
+            own[row : row + 16, col : col + 128] = low(jnp.where(left, keys, roll64(vals)))
+            own[row : row + 16, col + 128 : col + 256] = low(jnp.where(left, roll64(keys), vals))
+        own[base + OUT : base + OUT + 16, :] = low(k.w_out[layer])
+        for j in range(4):
+            own[base + UP + 16 * j : base + UP + 16 * j + 16, :] = low(k.w_up[layer, :, 512 * j : 512 * j + 512])
+        own[base + DOWN : base + DOWN + 64, :] = low(k.w_down[layer])
+
+    pl.semaphore_wait(barrier, 31)
+    gather_weights(k)
+    forward_backward(k)
+    reduce_grads(k)
+
+
+def sem(k, count=1):
+    at = k.cursor
+    k.cursor += count
+    assert k.cursor <= SEMS
+    return at
+
+
+def start_all(copies):
+    for copy in copies:
+        copy.start()
+
+
+def wait_all(copies):
+    for copy in copies:
+        copy.wait()
+
+
+def gather_piece(k, r0, rm, r1):
+    g, z, y, x, dev, pk = k.g, k.z, k.y, k.x, k.dev, k.pk
+
+    def send(ref, device):
+        i = sem(k)
+        return remote(ref, ref, k.ss.at[i], k.rs.at[i], device)
+
+    stage = [
+        send(pk.at[g, z, y, x, pl.ds(r0, r1 - r0)], dev(g, lax.rem(z + hop, 4), y, x)) for hop in (1, 2, 3)
+    ]
+    start_all(stage)
+    wait_all(stage)
+    stage = [
+        send(pk.at[g, :, y, x, pl.ds(r0, rm - r0)], dev(g, z, 1 - y, x)),
+        send(pk.at[g, :, y, x, pl.ds(rm, r1 - rm)], dev(g, z, y, 1 - x)),
+    ]
+    start_all(stage)
+    wait_all(stage)
+    stage = [
+        send(pk.at[g, :, :, x, pl.ds(r0, rm - r0)], dev(g, z, y, 1 - x)),
+        send(pk.at[g, :, y, :, pl.ds(rm, r1 - rm)], dev(g, z, 1 - y, x)),
+    ]
+    start_all(stage)
+    wait_all(stage)
+    stage = [send(pk.at[g, :, :, :, pl.ds(r0, r1 - r0)], dev(1 - g, z, y, x))]
+    start_all(stage)
+    wait_all(stage)
+
+
+def gather_weights(k):
+    gather_piece(k, 0, ROWS // 2, ROWS)
+
+
+def block(ref, row):
+    return ref[:, :, :, :, row : row + 16, :].reshape(512, 512)
+
+
+def put_block(ref, row, value):
+    ref[:, :, :, :, row : row + 16, :] = low(value).reshape(2, 4, 2, 2, 16, 512)
+
+
+def down_block(ref, row, c):
+    return ref[c // 2, (c % 2) * 2 : (c % 2) * 2 + 2, :, :, row : row + 64, :].reshape(512, 512)
+
+
+def put_down(ref, row, c, value):
+    ref[c // 2, (c % 2) * 2 : (c % 2) * 2 + 2, :, :, row : row + 64, :] = low(value).reshape(2, 2, 2, 64, 512)
+
+
+def my_blocks(k):
+    return [4 * j + (k.side_own if half == 0 else 3 - k.side_own) for j in range(4) for half in range(2)]
+
+
+def to_heads(k, source, target, after=None):
+    base = sem(k, 16)
+    out = sem(k, 8)
+    selves = []
+    for h in range(8):
+        chip = k.g * 8 + h
+        is_self = jnp.logical_and(chip == k.s, k.side == k.g)
+        copy = remote(source.at[h], target.at[k.s], k.ss.at[out + h], k.rs.at[base + k.s], (k.side, chip))
+        selves.append((is_self, copy))
+
+        @pl.when(is_self)
+        def _():
+            pltpu.make_async_copy(source.at[h], target.at[k.s], k.rs.at[base + k.s]).start()
+
+        @pl.when(jnp.logical_not(is_self))
+        def _():
+            copy.start()
+
+    for b in my_blocks(k):
+        pltpu.make_async_copy(target.at[b], target.at[b], k.rs.at[base + b]).wait()
+        if after is not None:
+            after(b)
+    return selves
+
+
+def from_heads(k, source, target):
+    base = sem(k, 8)
+    out = sem(k, 8)
+    selves = []
+    group, head = k.s // 8, lax.rem(k.s, 8)
+    for i, b in enumerate(my_blocks(k)):
+        is_self = jnp.logical_and(group == k.g, b == k.s)
+        copy = remote(source.at[i], target.at[head], k.ss.at[out + i], k.rs.at[base + head], (group, b))
+        selves.append((is_self, copy))
+
+        @pl.when(is_self)
+        def _():
+            pltpu.make_async_copy(source.at[i], target.at[head], k.rs.at[base + head]).start()
+
+        @pl.when(jnp.logical_not(is_self))
+        def _():
+            copy.start()
+
+    for h in range(8):
+        pltpu.make_async_copy(target.at[h], target.at[h], k.rs.at[base + h]).wait()
+    return selves
+
+
+def finish(selves):
+    for is_self, copy in selves:
+        @pl.when(jnp.logical_not(is_self))
+        def _():
+            copy.wait_send()
+
+
+def rotate_block(v, cosine, sine):
+    return v * cosine + swap32(v) * sine
+
+
+def layer_sizes(layer):
+    rows = 144 if layer == 0 else 48
+    return rows, (rows // 2 + 15) // 16 * 16
+
+
+def attend_loop(k, layer, body):
+    for part in range(2):
+        @pl.loop(0, 4)
+        def _(n):
+            i = part * 4 + n
+            j, half = i // 2, lax.rem(i, 2)
+            b = 4 * j + jnp.where(half == 0, k.side_own, 3 - k.side_own)
+            body(i, b, 8 * (part + 1))
+
+
+def masked_scores(k, layer, b, q, kv):
+    rows, _ = layer_sizes(layer)
+    scores = dot_nt(q, kv)
+    shape = scores.shape
+    visible = lanes(shape) <= b * rows + lax.broadcasted_iota(jnp.int32, shape, 0)
+    return jnp.where(visible, scores, MASK_FILL)
+
+
+def queries(inbox, b, rows):
+    return low(unpack_left(inbox[b, 0 : (rows // 2 + 15) // 16 * 16, :].astype(F32)[: rows // 2]) * 0.125)
+
+
+def attention_forward(k, layer):
+    rows, pad = layer_sizes(layer)
+    inbox, outbox, lse, keep = k.inbox[layer], k.abox[layer], k.lse[layer], k.att[layer]
+
+    def body(i, b, blocks):
+        q = queries(inbox, b, rows)
+        kv = inbox[0:blocks, pad : pad + rows, :].reshape(blocks * rows, 128)
+        scores = masked_scores(k, layer, b, q, kv)
+        top = jnp.max(scores, axis=-1, keepdims=True)
+        prob = jnp.exp(scores - top)
+        total = jnp.sum(prob, axis=-1, keepdims=True)
+        out = dot(low(prob), kv) / total
+        lse[i] = jnp.broadcast_to(top + jnp.log(total), (rows, 128))
+        keep[i] = out
+        outbox[i, 0 : rows // 2, :] = low(pack_right(out))
+
+    attend_loop(k, layer, body)
+
+
+def attention_backward(k, layer):
+    rows, pad = layer_sizes(layer)
+    inbox, gradbox, lse, keep = k.inbox[layer], k.gbox[layer], k.lse[layer], k.att[layer]
+    dkvt, outbox = k.dkvt[layer], k.dbox[layer]
+    dkvt[...] = jnp.zeros_like(dkvt)
+
+    def body(i, b, blocks):
+        q = queries(inbox, b, rows)
+        kv = inbox[0:blocks, pad : pad + rows, :].reshape(blocks * rows, 128)
+        grad = unpack_right(gradbox[b].astype(F32)[: rows // 2])
+        delta = jnp.sum(grad * keep[i], axis=-1, keepdims=True)
+        grad = low(grad)
+        prob = jnp.exp(masked_scores(k, layer, b, q, kv) - lse[i][:, 0:1])
+        grad_prob = dot_nt(grad, kv)
+        ds = low(prob * (grad_prob - delta))
+        dq = dot(ds, kv) * 0.125
+        outbox[i, 0 : rows // 2, :] = low(pack_left(dq))
+        both = dot_tn(q, ds) + dot_tn(grad, low(prob))
+        dkvt[:, 0 : blocks * rows] += both
+
+    attend_loop(k, layer, body)
+    dkv, theirs, got = k.dkv[layer], k.dkv_out[layer], k.dkv_in[layer]
+    dkv[...] = dkvt[...].T.reshape(16, rows, 128)
+    mine = my_blocks(k)
+    for i in range(8):
+        j, half = i // 2, i % 2
+        other = 4 * j + ((1 - k.side_own) if half == 0 else 2 + k.side_own)
+        theirs[i] = dkv[other]
+    at = sem(k)
+    copy = remote(theirs, got, k.ss.at[at], k.rs.at[at], k.dev(1 - k.g, k.z, k.y, k.x))
+    copy.start()
+    copy.wait()
+    for i, b in enumerate(mine):
+        outbox[i, pad : pad + rows, :] = low(dkv[b] + got[i])
+
+
+def layer_ahead(k, layer, hidden):
+    rows, pad = layer_sizes(layer)
+    base = LAYER0 + layer * LAYER_ROWS
+    hold = k.hold[layer]
+    hold.hidden[...] = hidden
+    unit, _ = norm_parts(hidden)
+    normed = low(unit * k.gain[2 * layer : 2 * layer + 1, :])
+    hold.normed[...] = normed
+    cosine, sine = k.cos[layer][...], k.sin[layer][...]
+    left = lanes(cosine.shape) < 64
+    cos_kv, sin_kv = jnp.where(left, cosine, 1.0), jnp.where(left, sine, 0.0)
+    sendbox = k.sendbox[layer]
+    for part in range(3):
+        joined = dot(normed, block(k.pk, base + QKV + 16 * part))
+        for n in range(4):
+            piece = joined[:, 128 * n : 128 * n + 128]
+            if part == 0:
+                piece = rotate_block(piece, cosine, sine)
+                sendbox[2 * n, 0 : rows // 2, :] = low(pack_pair(piece, 0))
+                sendbox[2 * n + 1, 0 : rows // 2, :] = low(pack_pair(piece, 1))
+            else:
+                sendbox[4 * part - 4 + n, pad : pad + rows, :] = low(rotate_block(piece, cos_kv, sin_kv))
+    inbox = k.inbox[layer]
+    at = sem(k, 16)
+    share = sem(k, 16)
+    passed = []
+
+    def pass_on(b):
+        copy = remote(
+            inbox.at[b, pl.ds(pad, rows)],
+            inbox.at[b, pl.ds(pad, rows)],
+            k.ss.at[share + b],
+            k.rs.at[at + b],
+            k.dev(1 - k.g, k.z, k.y, k.x),
+        )
+        copy.start()
+        passed.append(copy)
+
+    selves = to_heads(k, sendbox, inbox, pass_on)
+    for i in range(8):
+        j, half = i // 2, i % 2
+        other = 4 * j + ((1 - k.side_own) if half == 0 else 2 + k.side_own)
+        ref = inbox.at[other, pl.ds(pad, rows)]
+        pltpu.make_async_copy(ref, ref, k.rs.at[at + other]).wait()
+    attention_forward(k, layer)
+    home = k.home[layer]
+    selves = selves + from_heads(k, k.abox[layer], home)
+    for n in range(4):
+        pair = unpack_pair(
+            home[2 * n].astype(F32)[: rows // 2], home[2 * n + 1].astype(F32)[: rows // 2]
+        )
+        hold.flat[:, 128 * n : 128 * n + 128] = low(pair)
+    middle = hidden + dot(hold.flat[...], block(k.pk, base + OUT))
+    hold.middle[...] = middle
+    unit, _ = norm_parts(middle)
+    second = low(unit * k.gain[2 * layer + 1 : 2 * layer + 2, :])
+    hold.second[...] = second
+    for j in range(4):
+        pre = dot(second, block(k.pk, base + UP + 16 * j))
+        hold.pre[:, 512 * j : 512 * j + 512] = pre
+        hold.act[:, 512 * j : 512 * j + 512] = low(gelu(pre))
+    output = middle
+    for c in range(4):
+        output = output + dot(hold.act[:, 512 * c : 512 * c + 512], down_block(k.pk, base + DOWN, c))
+    finish(selves)
+    for copy in passed:
+        copy.wait_send()
+    return output
+
+
+def layer_back(k, layer, grad_out):
+    rows, pad = layer_sizes(layer)
+    base = LAYER0 + layer * LAYER_ROWS
+    hold = k.hold[layer]
+    fall = low(grad_out)
+    grad_second = jnp.zeros((rows, D), F32)
+    second = hold.second[...]
+    for c in range(4):
+        cols = slice(512 * c, 512 * c + 512)
+        put_down(k.gr, base + DOWN, c, dot_tn(hold.act[:, cols], fall))
+        grad_act = dot_nt(fall, down_block(k.pk, base + DOWN, c))
+        grad_pre = low(grad_act * gelu_grad(hold.pre[:, cols]))
+        put_block(k.gr, base + UP + 16 * c, dot_tn(second, grad_pre))
+        grad_second = grad_second + dot_nt(grad_pre, block(k.pk, base + UP + 16 * c))
+    gain = k.gain[2 * layer + 1 : 2 * layer + 2, :]
+    grad_mid, k.gain_grads[2 * layer + 1] = norm_back(hold.middle[...], gain, grad_second)
+    grad_middle = grad_out + grad_mid
+    hold.middle[...] = grad_middle
+    proj = low(grad_middle)
+    put_block(k.gr, base + OUT, dot_tn(hold.flat[...], proj))
+    grad_att = dot_nt(proj, block(k.pk, base + OUT))
+    gsend = k.gsend[layer]
+    for n in range(4):
+        piece = grad_att[:, 128 * n : 128 * n + 128]
+        gsend[2 * n, 0 : rows // 2, :] = low(pack_pair(piece, 0))
+        gsend[2 * n + 1, 0 : rows // 2, :] = low(pack_pair(piece, 1))
+    selves = to_heads(k, gsend, k.gbox[layer])
+    attention_backward(k, layer)
+    back = k.back[layer]
+    selves = selves + from_heads(k, k.dbox[layer], back)
+    cosine, sine = k.cos[layer][...], k.sin[layer][...]
+    left = lanes(cosine.shape) < 64
+    cos_kv, sin_kv = jnp.where(left, cosine, 1.0), jnp.where(left, sine, 0.0)
+    normed = hold.normed[...]
+    grad_normed = jnp.zeros((rows, D), F32)
+    for part in range(3):
+        for n in range(4):
+            if part == 0:
+                piece = unpack_pair(
+                    back[2 * n, 0:pad, :].astype(F32)[: rows // 2],
+                    back[2 * n + 1, 0:pad, :].astype(F32)[: rows // 2],
+                )
+                piece = rotate_block(piece, cosine, -sine)
+            else:
+                piece = back[4 * part - 4 + n, pad : pad + rows, :].astype(F32)
+                piece = rotate_block(piece, cos_kv, -sin_kv)
+            hold.gj[:, 128 * n : 128 * n + 128] = low(piece)
+        gj = hold.gj[...]
+        put_block(k.gr, base + QKV + 16 * part, dot_tn(normed, gj))
+        grad_normed = grad_normed + dot_nt(gj, block(k.pk, base + QKV + 16 * part))
+    gain = k.gain[2 * layer : 2 * layer + 1, :]
+    grad_in, k.gain_grads[2 * layer] = norm_back(hold.hidden[...], gain, grad_normed)
+    finish(selves)
+    return hold.middle[...] + grad_in
+
+
+def byte_matrix(ids, half):
+    n = lanes((ids.shape[0], 512))
+    return low(jnp.where((n // 16 * 8 + n % 8 == ids) & (n // 8 % 2 == half), 1.0, 0.0))
+
+
+def forward_backward(k):
+    k.side_own = k.g
+    rows, short = 144, 48
+    k.gain[...] = jnp.sum(k.pk[:, :, :, :, GN : GN + 16, :].astype(F32).reshape(32, 16, 512), axis=0)
+    k.gain_grads = [None] * 5
+    table = k.pk[:, :, :, :, EH : EH + 16, 256:512].reshape(512, 256)
+    ids = k.ids[...]
+    first_in = jnp.concatenate([dot(byte_matrix(ids, 0), table), dot(byte_matrix(ids, 1), table)], axis=1)
+    first = layer_ahead(k, 0, first_in)
+    k.shift[8 : 8 + rows, :] = first
+    at = sem(k)
+    rim = remote(
+        k.shift.at[pl.ds(rows, 8)], k.shift.at[pl.ds(0, 8)], k.ss.at[at], k.rs.at[at], (k.g, lax.rem(k.s + 1, 16))
+    )
+
+    @pl.when(k.s < 15)
+    def _():
+        rim.start()
+
+    @pl.when(k.s > 0)
+    def _():
+        rim.wait_recv()
+
+    @pl.when(k.s == 0)
+    def _():
+        k.shift[0:8, :] = jnp.zeros((8, D), F32)
+
+    @pl.when(k.s < 15)
+    def _():
+        rim.wait_send()
+
+    def pool_matrix(shape, offset, axis):
+        j = lax.broadcasted_iota(jnp.int32, shape, axis)
+        t = lax.broadcasted_iota(jnp.int32, shape, 1 - axis) - offset
+        return jnp.where((t >= 3 * j) & (t < 3 * j + 3), 1.0, 0.0)
+
+    exact = functools.partial(jnp.dot, preferred_element_type=F32, precision=lax.Precision.HIGHEST)
+    pooled = exact(pool_matrix((short, rows + 8), 6, 0), k.shift[...]) / 3.0
+    short_out = layer_ahead(k, 1, pooled)
+    upsampled = k.shift[8 : 8 + rows, :] + exact(pool_matrix((rows, short), 0, 1), short_out)
+    gain = k.gain[4:5, :]
+    unit, _ = norm_parts(upsampled)
+    final = low(unit * gain)
+    head = k.pk[:, :, :, :, EH : EH + 16, 0:256].reshape(512, 256)
+    logits = dot(final, head)
+    top = jnp.max(logits, axis=-1, keepdims=True)
+    log_total = top + jnp.log(jnp.sum(jnp.exp(logits - top), axis=-1, keepdims=True))
+    hot = jnp.where(lanes((rows, 256)) == k.targets[...], 1.0, 0.0)
+    picked = jnp.sum(hot * logits, axis=-1, keepdims=True)
+    position = k.s * rows + lax.broadcasted_iota(jnp.int32, (rows, 1), 0)
+    length = jnp.zeros((rows, 1), F32)
+    begin = jnp.int32(0)
+    for i in range(8):
+        size = k.lengths[0, i]
+        inside = (position >= begin) & (position < begin + size)
+        length = jnp.where(inside, size.astype(F32), length)
+        begin = begin + size
+    k.loss = jnp.sum((log_total - picked) / length, axis=0, keepdims=True)
+    grad_logits = low((jnp.exp(logits - log_total) - hot) / length)
+    k.gr[:, :, :, :, EH : EH + 16, 0:256] = low(dot_tn(final, grad_logits)).reshape(2, 4, 2, 2, 16, 256)
+    grad_final = dot_nt(grad_logits, head)
+    grad_up, k.gain_grads[4] = norm_back(upsampled, gain, grad_final)
+    k.up[...] = grad_up
+    grad_short = exact(pool_matrix((short, rows), 0, 0), grad_up)
+    grad_pooled = layer_back(k, 1, grad_short)
+    k.pool[0:short, :] = grad_pooled
+    at = sem(k)
+    rim2 = remote(
+        k.pool.at[pl.ds(0, 8)], k.pool.at[pl.ds(short, 8)], k.ss.at[at], k.rs.at[at], (k.g, lax.rem(k.s + 15, 16))
+    )
+
+    @pl.when(k.s > 0)
+    def _():
+        rim2.start()
+
+    @pl.when(k.s < 15)
+    def _():
+        rim2.wait_recv()
+
+    @pl.when(k.s == 15)
+    def _():
+        k.pool[short : short + 8, :] = jnp.zeros((8, D), F32)
+
+    @pl.when(k.s > 0)
+    def _():
+        rim2.wait_send()
+
+    t = lax.broadcasted_iota(jnp.int32, (rows, short + 8), 0)
+    j = lax.broadcasted_iota(jnp.int32, (rows, short + 8), 1)
+    spread = jnp.where((t + 2 >= 3 * j) & (t + 2 < 3 * j + 3), 1.0, 0.0)
+    grad_first = k.up[...] + exact(spread, k.pool[...] / 3.0)
+    grad_in = layer_back(k, 0, grad_first)
+    table_grad = dot_tn(byte_matrix(ids, 0), low(grad_in[:, 0:256])) + dot_tn(
+        byte_matrix(ids, 1), low(grad_in[:, 256:512])
+    )
+    k.gr[:, :, :, :, EH : EH + 16, 256:512] = low(table_grad).reshape(2, 4, 2, 2, 16, 256)
+    gains = jnp.concatenate(k.gain_grads + [jnp.zeros((11, D), F32)], axis=0)
+    k.gr[:, :, :, :, GN : GN + 16, :] = low(jnp.broadcast_to(gains[None], (32, 16, 512))).reshape(2, 4, 2, 2, 16, 512)
+
+
+def add_into(ref, other):
+    ref[...] = low(ref[...].astype(F32) + other[...].astype(F32))
+
+
+def reduce_grads(k):
+    g, z, y, x, dev, gr = k.g, k.z, k.y, k.x, k.dev, k.gr
+    half = ROWS // 2
+    a, b = pl.ds(0, half), pl.ds(half, half)
+
+    def send(src, dst, device):
+        i = sem(k)
+        return remote(src, dst, k.ss.at[i], k.rs.at[i], device)
+
+    copy = send(gr.at[1 - g], k.rc, dev(1 - g, z, y, x))
+    copy.start()
+    copy.wait()
+
+    @pl.loop(0, 16)
+    def _(n):
+        add_into(gr.at[g, n // 4, lax.rem(n // 2, 2), lax.rem(n, 2)], k.rc.at[n // 4, lax.rem(n // 2, 2), lax.rem(n, 2)])
+
+    stage = [
+        send(gr.at[g, :, :, 1 - x, a], k.r2.at[:, :, a], dev(g, z, y, 1 - x)),
+        send(gr.at[g, :, 1 - y, :, b], k.r2.at[:, :, b], dev(g, z, 1 - y, x)),
+    ]
+    start_all(stage)
+    wait_all(stage)
+
+    @pl.loop(0, 8)
+    def _(n):
+        add_into(gr.at[g, n // 2, lax.rem(n, 2), x, a], k.r2.at[n // 2, lax.rem(n, 2), a])
+        add_into(gr.at[g, n // 2, y, lax.rem(n, 2), b], k.r2.at[n // 2, lax.rem(n, 2), b])
+
+    stage = [
+        send(gr.at[g, :, 1 - y, x, a], k.r1.at[:, a], dev(g, z, 1 - y, x)),
+        send(gr.at[g, :, y, 1 - x, b], k.r1.at[:, b], dev(g, z, y, 1 - x)),
+    ]
+    start_all(stage)
+    wait_all(stage)
+
+    @pl.loop(0, 4)
+    def _(n):
+        add_into(gr.at[g, n, y, x], k.r1.at[n])
+
+    stage = []
+    for hop in (1, 2, 3):
+        to = lax.rem(z + hop, 4)
+        stage.append(send(gr.at[g, to, y, x], k.rz.at[hop - 1], dev(g, to, y, x)))
+    start_all(stage)
+    wait_all(stage)
+    k.sq = jnp.zeros((1, 1), F32)
+
+    def total(row, count):
+        rows = pl.ds(row, count)
+        v = gr[g, z, y, x, rows].astype(F32)
+        for i in range(3):
+            v = v + k.rz[i, rows].astype(F32)
+        return v
+
+    def square(v):
+        k.sq = k.sq + jnp.sum(jnp.sum(v * v, axis=1, keepdims=True), axis=0, keepdims=True)
+
+    v = total(EH, 16)
+    square(v)
+    k.g_head[...] = v[:, 0:256]
+    k.g_embed[:, 0:256] = v[0:8, 256:512]
+    k.g_embed[:, 256:512] = v[8:16, 256:512]
+    v = total(GN, 16)
+    pick = (
+        lax.broadcasted_iota(jnp.int32, (D, 16), 0) - 16 * (g * 16 + k.s)
+        == lax.broadcasted_iota(jnp.int32, (D, 16), 1)
+    )
+    v = jnp.dot(v, jnp.where(pick, 1.0, 0.0), preferred_element_type=F32, precision=lax.Precision.HIGHEST)
+    square(v)
+    k.g_gains[...] = v[0:5]
+    for layer in range(2):
+        base = LAYER0 + layer * LAYER_ROWS
+        v = total(base + QKV, 48)
+        square(v)
+        k.g_qkv[layer, :, 0:512] = v[0:16]
+        for pair in range(4):
+            row, col = 16 + 16 * (pair // 2), 256 * (pair % 2)
+            even = v[row : row + 16, col : col + 128]
+            odd = v[row : row + 16, col + 128 : col + 256]
+            left = lanes(even.shape) < 64
+            k.g_qkv[layer, :, 512 + 128 * pair : 640 + 128 * pair] = jnp.where(left, even, roll64(odd))
+            k.g_qkv[layer, :, 1024 + 128 * pair : 1152 + 128 * pair] = jnp.where(left, roll64(even), odd)
+        v = total(base + OUT, 16)
+        square(v)
+        k.g_out[layer] = v
+        v = total(base + UP, 64)
+        square(v)
+        for j in range(4):
+            k.g_up[layer, :, 512 * j : 512 * j + 512] = v[16 * j : 16 * j + 16]
+        v = total(base + DOWN, 64)
+        square(v)
+        k.g_down[layer] = v
+
+    lane = lanes((8, 128))
+    k.stat[0] = jnp.where(lane == 0, k.sq, jnp.where(lane == 1, k.loss, 0.0))
+    me = g * 16 + k.s
+    base, out = sem(k, 32), sem(k, 32)
+
+    def stat_copy(i):
+        t = lax.rem(me + i, 32)
+        return remote(
+            k.stat.at[0], k.stat.at[i], k.ss.at[out + i], k.rs.at[base + i], (t // 16, lax.rem(t, 16))
+        )
+
+    @pl.loop(1, 32)
+    def _(i):
+        stat_copy(i).start()
+
+    @pl.loop(1, 32)
+    def _(i):
+        stat_copy(i).wait()
+
+    k.stats[...] = jnp.sum(k.stat[...], axis=0)
+
+
+IN_NAMES = (
+    "ids", "targets", "lengths", "w_qkv", "w_out", "w_up", "w_down", "embed", "head", "gains",
+    "cos0", "sin0", "cos1", "sin1",
+)
+OUT_NAMES = ("g_qkv", "g_out", "g_up", "g_down", "g_embed", "g_head", "g_gains", "stats")
+SEMS = 384
+
+
+def scratch_shapes():
+    shapes = {
+        "pk": ((2, 4, 2, 2, ROWS, D), LOW),
+        "gr": ((2, 4, 2, 2, ROWS, D), LOW),
+        "rc": ((4, 2, 2, ROWS, D), LOW),
+        "r2": ((4, 2, ROWS, D), LOW),
+        "r1": ((4, ROWS, D), LOW),
+        "rz": ((3, ROWS, D), LOW),
+        "gain": ((16, D), F32),
+        "shift": ((152, D), F32),
+        "pool": ((56, D), F32),
+        "up": ((144, D), F32),
+        "stat": ((32, 8, 128), F32),
+    }
+    for layer in range(2):
+        rows, pad = layer_sizes(layer)
+        for name, shape, kind in (
+            ("sendbox", (8, pad + rows, 128), LOW),
+            ("inbox", (16, pad + rows, 128), LOW),
+            ("abox", (8, pad, 128), LOW),
+            ("home", (8, pad, 128), LOW),
+            ("gsend", (8, pad, 128), LOW),
+            ("gbox", (16, pad, 128), LOW),
+            ("dbox", (8, pad + rows, 128), LOW),
+            ("back", (8, pad + rows, 128), LOW),
+            ("lse", (8, rows, 128), F32),
+            ("att", (8, rows, 128), F32),
+            ("dkvt", (128, 16 * rows), F32),
+            ("dkv", (16, rows, 128), F32),
+            ("dkv_out", (8, rows, 128), F32),
+            ("dkv_in", (8, rows, 128), F32),
+            ("h_hidden", (rows, D), F32),
+            ("h_normed", (rows, D), LOW),
+            ("h_flat", (rows, D), LOW),
+            ("h_middle", (rows, D), F32),
+            ("h_second", (rows, D), LOW),
+            ("h_pre", (rows, 4 * D), F32),
+            ("h_act", (rows, 4 * D), LOW),
+            ("h_gj", (rows, D), LOW),
+        ):
+            shapes[name + str(layer)] = (shape, kind)
+    return shapes
+
+
+SCRATCH = scratch_shapes()
+PER_LAYER = (
+    "cos", "sin", "sendbox", "inbox", "abox", "home", "gsend", "gbox", "dbox", "back", "lse", "att", "dkvt", "dkv",
+    "dkv_out", "dkv_in",
+)
+HELD = ("hidden", "normed", "flat", "middle", "second", "pre", "act", "gj")
+
+
+def update_kernel(*refs):
+    stats, grads, masters, firsts, seconds = refs[0], refs[1:8], refs[8:15], refs[15:22], refs[22:29]
+    outs = refs[29:]
+    norm = jnp.sqrt(stats[0:1, 0:1])
+    clip = jnp.minimum(1.0, CLIP_NORM / norm)
+    for i in range(7):
+        results = adam_update(
+            masters[i][...], grads[i][...] * clip, firsts[i][...], seconds[i][...], STEP_RATES[i], WEIGHT_DECAYS[i]
+        )
+        for j in range(3):
+            outs[7 * j + i][...] = results[j]
+
+
+def on_device_fast(byte_ids, targets, item_lengths, *arrays):
+    masters, firsts, seconds = arrays[0:7], arrays[7:14], arrays[14:21]
+    gains = masters[6]
+    rows = byte_ids.shape[1]
+    place = lax.axis_index("seq")
+    own = lax.axis_index("dp") * lax.axis_size("seq") + place
+    lane = jnp.arange(D, dtype=jnp.int32)
+    spread = jnp.where(lane[None, :] // gains.shape[1] == own, jnp.tile(gains, (1, D // gains.shape[1])), 0.0)
+    spread = jnp.pad(spread, ((0, 16 - gains.shape[0]), (0, 0)))
+    freqs = 10000.0 ** (-jnp.arange(32, dtype=jnp.float32) / 32)
+    freqs = jnp.tile(freqs, 4)
+    sign = jnp.where(jnp.arange(128) % 64 < 32, -1.0, 1.0)
+    tables = []
+    for count in (rows, rows // RATE):
+        positions = place * count + jnp.arange(count, dtype=jnp.int32)
+        angles = positions.astype(jnp.float32)[:, None] * freqs[None, :]
+        tables += [jnp.cos(angles), jnp.sin(angles) * sign[None, :]]
+    vmem = pl.BlockSpec(memory_space=pltpu.VMEM)
+    shard_shapes = [jax.ShapeDtypeStruct(master.shape, F32) for master in masters]
+    outs = pl.pallas_call(
+        kernel,
+        name="step",
+        out_shape=shard_shapes + [jax.ShapeDtypeStruct((8, 128), F32)],
+        in_specs=[vmem, vmem, pl.BlockSpec(memory_space=pltpu.SMEM)] + [vmem] * 11,
+        out_specs=[vmem] * 8,
+        scratch_shapes=[pltpu.VMEM(shape, kind) for shape, kind in SCRATCH.values()]
+        + [pltpu.SemaphoreType.DMA((SEMS,)), pltpu.SemaphoreType.DMA((SEMS,))],
+        compiler_params=pltpu.CompilerParams(collective_id=0, has_side_effects=True, vmem_limit_bytes=63 << 20),
+    )(byte_ids.reshape(rows, 1), targets.reshape(rows, 1), item_lengths, *masters[:6], spread, *tables)
+    grads, stats = outs[:7], outs[7]
+    results = pl.pallas_call(
+        update_kernel,
+        name="update",
+        out_shape=shard_shapes * 3,
+        in_specs=[vmem] * 29,
+        out_specs=[vmem] * 21,
+        compiler_params=pltpu.CompilerParams(vmem_limit_bytes=32 << 20),
+    )(stats, *grads, *masters, *firsts, *seconds)
+    return (stats[0, 1], jnp.sqrt(stats[0, 0]), *results)
+
+
 def solution(mesh):
+    tuned = mesh.shape["dp"] == 2 and mesh.shape["seq"] == 16
+    row = P(None, ("dp", "seq"), None)
+    flat = P(("dp", "seq"), None)
+    shards = (row, row, row, row, flat, flat, P(None, ("dp", "seq")))
     return jax.shard_map(
-        on_device,
+        on_device_fast if tuned else on_device_general,
         mesh=mesh,
-        in_specs=(
-            P("dp", "seq"),
-            P("dp", "seq"),
-            P("dp", None),
-            P(None, ("dp", "seq"), None),
-            P(None, ("dp", "seq"), None),
-            P(None, ("dp", "seq"), None),
-            P(None, ("dp", "seq"), None),
-            P(("dp", "seq"), None),
-            P(("dp", "seq"), None),
-            P(None, ("dp", "seq")),
-            P(None, ("dp", "seq"), None),
-            P(None, ("dp", "seq"), None),
-            P(None, ("dp", "seq"), None),
-            P(None, ("dp", "seq"), None),
-            P(("dp", "seq"), None),
-            P(("dp", "seq"), None),
-            P(None, ("dp", "seq")),
-            P(None, ("dp", "seq"), None),
-            P(None, ("dp", "seq"), None),
-            P(None, ("dp", "seq"), None),
-            P(None, ("dp", "seq"), None),
-            P(("dp", "seq"), None),
-            P(("dp", "seq"), None),
-            P(None, ("dp", "seq")),
-        ),
-        out_specs=(
-            P(),
-            P(),
-            P(None, ("dp", "seq"), None),
-            P(None, ("dp", "seq"), None),
-            P(None, ("dp", "seq"), None),
-            P(None, ("dp", "seq"), None),
-            P(("dp", "seq"), None),
-            P(("dp", "seq"), None),
-            P(None, ("dp", "seq")),
-            P(None, ("dp", "seq"), None),
-            P(None, ("dp", "seq"), None),
-            P(None, ("dp", "seq"), None),
-            P(None, ("dp", "seq"), None),
-            P(("dp", "seq"), None),
-            P(("dp", "seq"), None),
-            P(None, ("dp", "seq")),
-            P(None, ("dp", "seq"), None),
-            P(None, ("dp", "seq"), None),
-            P(None, ("dp", "seq"), None),
-            P(None, ("dp", "seq"), None),
-            P(("dp", "seq"), None),
-            P(("dp", "seq"), None),
-            P(None, ("dp", "seq")),
-        ),
+        in_specs=(P("dp", "seq"), P("dp", "seq"), P("dp", None)) + shards * 3,
+        out_specs=(P(), P()) + shards * 3,
         check_vma=False,
     )

time: 2000 us -> 375 us (0.19)
  waiting for transfers between devices: 1140 us -> 0 us
  blocking collectives: 619 us -> 0 us
  Pallas kernels: 0 us -> 346 us
  matrix products: 90.2 us -> 0 us
  other arithmetic: 58.7 us -> 1.83 us
  local copies, waits for them, and re-layouts: 54.8 us -> 23.6 us
  between operations: 22.8 us -> 2.62 us
    reduce_scatter x6 -> x0, waiting for transfers between devices: 821 us -> none  [the longest x1 184 us: on_device(): lax.psum_scatter(jnp.stack([lower_grads[3], upper_grads[3]]), ('dp', 'seq...]
    all_gather x11 -> x0, blocking collectives: 579 us -> none  [the longest x2 76.3 us: attend_back(): lax.all_gather(log_total, 'seq', axis=0, tiled=True)]
    pallas_call x0 -> x2, Pallas kernels: none -> 346 us  [the longest x1 344 us: on_device_fast(): pl.pallas_call(kernel, name='step', out_shape=shard_shapes + [jax.ShapeDt...]
    all_gather x8 -> x0, waiting for transfers between devices: 183 us -> none  [the longest x1 74.9 us: attend(): lax.all_gather(v_low, 'seq', axis=0, tiled=True)]
    unnamed x16 -> x0, waiting for transfers between devices: 135 us -> none
    dot_general x41 -> x0, matrix products: 90.2 us -> none  [the longest x2 14.3 us: block_grads(): jnp.einsum('hrp,phe->rhe', grad_score, k_low, preferred_element_type=jnp....]
    psum x1 -> x0, blocking collectives: 39.9 us -> none  [on_device(): loss_sum = lax.psum(loss_local, ('dp', 'seq'))]
    all_gather x9 -> x0, local copies, waits for them, and re-layouts: 26.4 us -> none  [the longest x1 6.57 us: attend_back(): lax.all_gather(grad_low, 'seq', axis=0, tiled=True)]
  transfers between devices with their start and end apart: 17 -> 0, of which waited for: 11 -> 0; matrix products, arithmetic and copies ran while one was open for 9% -> 0% of each run, Pallas kernels for 0% -> 0%
where the time goes in v1:
time: 375 us; the launch traced here: 374 us
  Pallas kernels  346 us (92%)
  local copies, waits for them, and re-layouts  23.6 us (6%)
    pallas_call x1, Pallas kernels, on_device_fast(): pl.pallas_call(kernel, name='step', out_shape=shard_shapes + [jax.ShapeDt...  344 us
    unnamed x64, local copies, waits for them, and re-layouts  20.7 us

profile of v1, /device:TPU:0, one launch (start us, length us, event | category | flops | bytes accessed | tf_op | source)
XLA Modules:
  0.0 374.0 jit_solution(13874234663278854025)
XLA Ops:
  0.8 1.0 fusion
  1.8 0.8 fusion.1
  2.6 0.7 copy-done.24
  3.4 0.6 pad.4.refs_9_
  4.0 0.7 copy-done.30
  4.7 0.7 copy.47.refs_0_
  5.4 0.7 copy-done.31
  6.1 0.7 copy.48.refs_1_
  6.9 344.1 %step.1 = (f32[2,16,1536]{2,1,0:T(8,128)}, f32[2,16,512]{2,1,0:T(8,128)}, f32[2,16,2048]{2,1,0:T(8,128)}, f32[2,64,512]{2,1,0:T(8,128)}, f32[8,512]{1,0:T(8,128)...) custom-call(s32[144,1]{1,0:T(8,128)} %copy.47.refs_0_, s32[144,1]{1,0:T(8,128)} %copy.48.refs_1_, ...), custom_call_target="tpu_custom_call" | custom-call | tf_op jit(solution)/shard_map/step/pallas_call | solution.py:1214
  351.7 0.9 copy-done.4
  352.6 0.9 copy-done.5
  353.6 0.9 copy-done.6
  354.5 0.9 copy-done.7
  355.5 0.9 copy-done.8
  356.4 0.8 copy-done.9
  357.3 0.9 copy-done.10
  358.2 0.9 copy-done.11
  359.1 0.9 copy-done.12
  360.1 0.7 copy-done.13
  360.8 0.7 copy-done.14
  361.5 0.8 copy-done.15
  362.3 0.8 copy-done.16
  363.2 0.8 copy-done.17
  364.0 0.7 copy-done.18
  364.7 0.7 copy-done.19
  365.4 0.7 copy-done.20
  366.2 0.7 copy-done.21
  366.9 0.7 copy-done.22
  367.6 0.7 copy-done.23
  368.3 0.7 copy-done.28
  369.0 0.7 copy-done.29
  369.7 1.9 update.1
  (50 shorter events, 1.5 us)
Async XLA Ops:
  2.6 0.7 copy-start.24
  4.0 0.7 copy-start.30
  5.4 0.7 copy-start.31
  6.9 344.1 %copy-start = (f32[2,16,2048]{2,1,0:T(8,128)S(1)}, f32[2,16,2048]{2,1,0:T(8,128)}, u32[]{:S(2)}) copy-start(f32[2,16,2048]{2,1,0:T(8,128)} %refs_10_.1) | copy-start | bytes 786436
  6.9 344.1 %copy-start.1 = (f32[2,64,512]{2,1,0:T(8,128)S(1)}, f32[2,64,512]{2,1,0:T(8,128)}, u32[]{:S(2)}) copy-start(f32[2,64,512]{2,1,0:T(8,128)} %refs_11_.1) | copy-start | bytes 786436
  6.9 344.1 %copy-start.2 = (f32[2,16,1536]{2,1,0:T(8,128)S(1)}, f32[2,16,1536]{2,1,0:T(8,128)}, u32[]{:S(2)}) copy-start(f32[2,16,1536]{2,1,0:T(8,128)} %refs_8_.3) | copy-start | bytes 589828
  6.9 344.2 %copy-start.3 = (f32[2,16,2048]{2,1,0:T(8,128)S(1)}, f32[2,16,2048]{2,1,0:T(8,128)}, u32[]{:S(2)}) copy-start(f32[2,16,2048]{2,1,0:T(8,128)} %refs_17_.1) | copy-start | bytes 786436
  351.0 0.7 copy-start.27
  351.0 0.7 copy-start.26
  351.0 0.7 copy-start.25
  351.7 0.9 copy-start.4
  352.6 0.9 copy-start.5
  353.6 0.9 copy-start.6
  354.5 0.9 copy-start.7
  355.5 0.9 copy-start.8
  356.4 0.8 copy-start.9
  357.3 0.9 copy-start.10
  358.2 0.9 copy-start.11
  359.1 0.9 copy-start.12
  360.0 0.7 copy-start.13
  360.8 0.7 copy-start.14
  361.5 0.8 copy-start.15
  362.3 0.8 copy-start.16
  363.2 0.8 copy-start.17
  364.0 0.7 copy-start.18
  364.7 0.7 copy-start.19
  365.4 0.7 copy-start.20
  366.2 0.7 copy-start.21
  366.9 0.7 copy-start.22
  367.6 0.7 copy-start.23
  368.3 0.7 copy-start.28
  369.0 0.7 copy-start.29

commit v2 on v1

--- a/solution.py
+++ b/solution.py
@@ -392,9 +392,41 @@
 MESH = pl.DeviceIdType.MESH
 D = 512
 
-EH, GN, LAYER0, LAYER_ROWS = 0, 16, 32, 192
+EG, LAYER0, LAYER_ROWS = 0, 16, 192
 QKV, OUT, UP, DOWN = 0, 48, 64, 128
-ROWS = LAYER0 + 2 * LAYER_ROWS
+HEAD = LAYER0 + 2 * LAYER_ROWS
+ROWS = HEAD + 16
+PIECES = {"A": (0, 32, 64), "B": (64, 144, 208), "C": (208, 240, 272), "D": (272, 336, ROWS)}
+SCHEDULE = {
+    "start": "A",
+    "packed": "ABAABCDA",
+    "f0_sent": "B",
+    "f0_got": "",
+    "f0_part0": "BC",
+    "f0_part1": "C",
+    "f0_home": "B",
+    "f0_up": "CD",
+    "f0_end": "C",
+    "f1_sent": "D",
+    "f1_got": "",
+    "f1_part0": "",
+    "f1_home": "D",
+    "f1_up": "D",
+    "f1_end": "",
+    "b1_ff": "D",
+    "b1_sent": "D",
+    "b1_part0": "D",
+    "b1_sums": "",
+    "b1_home": "D",
+    "b1_end": "C",
+    "b0_ff": "BC",
+    "b0_sent": "BD",
+    "b0_part1": "C",
+    "b0_part0": "B",
+    "b0_sums": "C",
+    "b0_home": "B",
+    "b0_end": "",
+}
 
 
 def dot(a, b):
@@ -411,6 +443,9 @@
 
 def low(v):
     return v.astype(LOW)
+
+
+exact = functools.partial(jnp.dot, preferred_element_type=F32, precision=lax.Precision.HIGHEST)
 
 
 def lanes(shape):
@@ -532,29 +567,47 @@
         pl.semaphore_signal(barrier, inc=1, device_id=(t // 16, lax.rem(t, 16)), device_id_type=MESH)
 
     own = k.pk.at[g, z, y, x]
-    own[EH : EH + 16, 0:256] = low(k.head[...])
-    own[EH : EH + 16, 256:512] = low(jnp.concatenate([k.embed[:, 0:256], k.embed[:, 256:512]], axis=0))
-    own[GN : GN + 16, :] = low(k.gains[...])
-    for layer in range(2):
-        base = LAYER0 + layer * LAYER_ROWS
-        own[base + QKV : base + QKV + 16, :] = low(k.w_qkv[layer, :, 0:512])
-        for pair in range(4):
-            keys = k.w_qkv[layer, :, 512 + 128 * pair : 640 + 128 * pair]
-            vals = k.w_qkv[layer, :, 1024 + 128 * pair : 1152 + 128 * pair]
-            left = lanes(keys.shape) < 64
-            row = base + QKV + 16 + 16 * (pair // 2)
-            col = 256 * (pair % 2)
-            own[row : row + 16, col : col + 128] = low(jnp.where(left, keys, roll64(vals)))
-            own[row : row + 16, col + 128 : col + 256] = low(jnp.where(left, roll64(keys), vals))
-        own[base + OUT : base + OUT + 16, :] = low(k.w_out[layer])
-        for j in range(4):
-            own[base + UP + 16 * j : base + UP + 16 * j + 16, :] = low(k.w_up[layer, :, 512 * j : 512 * j + 512])
-        own[base + DOWN : base + DOWN + 64, :] = low(k.w_down[layer])
-
+    own[EG : EG + 16, 0:256] = low(jnp.concatenate([k.embed[:, 0:256], k.embed[:, 256:512]], axis=0))
+    place = lanes((16, 256)) - 16 * s == lax.broadcasted_iota(jnp.int32, (16, 256), 0)
+    gains = exact(k.gains[...], jnp.where(place, 1.0, 0.0))
+    gains = jnp.concatenate([gains, jnp.zeros((3, 256), F32)], axis=0)
+    gains = jnp.concatenate([jnp.where(g == 0, gains, 0.0), jnp.where(g == 1, gains, 0.0)], axis=0)
+    own[EG : EG + 16, 256:512] = low(gains)
+    pack_layer(k, own, 0)
     pl.semaphore_wait(barrier, 31)
-    gather_weights(k)
+    k.gathers = {name: gather_piece(k, *rows) for name, rows in PIECES.items()}
+    k.reduces = {name: reduce_piece(k, *rows) for name, rows in PIECES.items()}
+    k.ready, k.summed = set(), set()
+    point(k, "start")
+    own[HEAD : HEAD + 16, 0:256] = low(k.head[...])
+    own[HEAD : HEAD + 16, 256:512] = jnp.zeros((16, 256), LOW)
+    pack_layer(k, own, 1)
+    point(k, "packed")
     forward_backward(k)
-    reduce_grads(k)
+    finish_grads(k)
+
+
+def point(k, name):
+    moving = k.gathers if name[0] in "spf" else k.reduces
+    for piece in SCHEDULE[name]:
+        next(moving[piece])
+
+
+def pack_layer(k, own, layer):
+    base = LAYER0 + layer * LAYER_ROWS
+    own[base + QKV : base + QKV + 16, :] = low(k.w_qkv[layer, :, 0:512])
+    for pair in range(4):
+        keys = k.w_qkv[layer, :, 512 + 128 * pair : 640 + 128 * pair]
+        vals = k.w_qkv[layer, :, 1024 + 128 * pair : 1152 + 128 * pair]
+        left = lanes(keys.shape) < 64
+        row = base + QKV + 16 + 16 * (pair // 2)
+        col = 256 * (pair % 2)
+        own[row : row + 16, col : col + 128] = low(jnp.where(left, keys, roll64(vals)))
+        own[row : row + 16, col + 128 : col + 256] = low(jnp.where(left, roll64(keys), vals))
+    own[base + OUT : base + OUT + 16, :] = low(k.w_out[layer])
+    for j in range(4):
+        own[base + UP + 16 * j : base + UP + 16 * j + 16, :] = low(k.w_up[layer, :, 512 * j : 512 * j + 512])
+    own[base + DOWN : base + DOWN + 64, :] = low(k.w_down[layer])
 
 
 def sem(k, count=1):
@@ -574,49 +627,57 @@
         copy.wait()
 
 
+def hop(k, src, dst, device):
+    at = sem(k)
+    return remote(src, dst, k.ss.at[at], k.rs.at[at], device)
+
+
 def gather_piece(k, r0, rm, r1):
     g, z, y, x, dev, pk = k.g, k.z, k.y, k.x, k.dev, k.pk
+    a, b, every = pl.ds(r0, rm - r0), pl.ds(rm, r1 - rm), pl.ds(r0, r1 - r0)
 
     def send(ref, device):
-        i = sem(k)
-        return remote(ref, ref, k.ss.at[i], k.rs.at[i], device)
-
-    stage = [
-        send(pk.at[g, z, y, x, pl.ds(r0, r1 - r0)], dev(g, lax.rem(z + hop, 4), y, x)) for hop in (1, 2, 3)
-    ]
-    start_all(stage)
-    wait_all(stage)
-    stage = [
-        send(pk.at[g, :, y, x, pl.ds(r0, rm - r0)], dev(g, z, 1 - y, x)),
-        send(pk.at[g, :, y, x, pl.ds(rm, r1 - rm)], dev(g, z, y, 1 - x)),
-    ]
-    start_all(stage)
-    wait_all(stage)
-    stage = [
-        send(pk.at[g, :, :, x, pl.ds(r0, rm - r0)], dev(g, z, y, 1 - x)),
-        send(pk.at[g, :, y, :, pl.ds(rm, r1 - rm)], dev(g, z, 1 - y, x)),
-    ]
-    start_all(stage)
-    wait_all(stage)
-    stage = [send(pk.at[g, :, :, :, pl.ds(r0, r1 - r0)], dev(1 - g, z, y, x))]
-    start_all(stage)
-    wait_all(stage)
-
-
-def gather_weights(k):
-    gather_piece(k, 0, ROWS // 2, ROWS)
-
-
-def block(ref, row):
-    return ref[:, :, :, :, row : row + 16, :].reshape(512, 512)
+        return hop(k, ref, ref, device)
+
+    stages = (
+        lambda: [send(pk.at[g, z, y, x, every], dev(g, lax.rem(z + n, 4), y, x)) for n in (2, 1, 3)],
+        lambda: [
+            send(pk.at[g, :, y, x, a], dev(g, z, 1 - y, x)),
+            send(pk.at[g, :, y, x, b], dev(g, z, y, 1 - x)),
+        ],
+        lambda: [
+            send(pk.at[g, :, :, x, a], dev(g, z, y, 1 - x)),
+            send(pk.at[g, :, y, :, b], dev(g, z, 1 - y, x)),
+        ],
+        lambda: [send(pk.at[g, :, :, :, every], dev(1 - g, z, y, x))],
+    )
+    waiting = []
+    for stage in stages:
+        wait_all(waiting)
+        waiting = stage()
+        start_all(waiting)
+        yield
+    wait_all(waiting)
+    k.ready.update(range(r0, r1, 16))
+    yield
+
+
+def need(k, row, count=16):
+    assert k.ready.issuperset(range(row, row + count, 16)), row
+
+
+def block(k, row):
+    need(k, row)
+    return k.pk[:, :, :, :, row : row + 16, :].reshape(512, 512)
 
 
 def put_block(ref, row, value):
     ref[:, :, :, :, row : row + 16, :] = low(value).reshape(2, 4, 2, 2, 16, 512)
 
 
-def down_block(ref, row, c):
-    return ref[c // 2, (c % 2) * 2 : (c % 2) * 2 + 2, :, :, row : row + 64, :].reshape(512, 512)
+def down_block(k, row, c):
+    need(k, row, 64)
+    return k.pk[c // 2, (c % 2) * 2 : (c % 2) * 2 + 2, :, :, row : row + 64, :].reshape(512, 512)
 
 
 def put_down(ref, row, c, value):
@@ -624,66 +685,105 @@
 
 
 def my_blocks(k):
-    return [4 * j + (k.side_own if half == 0 else 3 - k.side_own) for j in range(4) for half in range(2)]
-
-
-def to_heads(k, source, target, after=None):
-    base = sem(k, 16)
-    out = sem(k, 8)
-    selves = []
-    for h in range(8):
-        chip = k.g * 8 + h
-        is_self = jnp.logical_and(chip == k.s, k.side == k.g)
-        copy = remote(source.at[h], target.at[k.s], k.ss.at[out + h], k.rs.at[base + k.s], (k.side, chip))
-        selves.append((is_self, copy))
+    return [4 * j + (k.g if half == 0 else 3 - k.g) for j in range(4) for half in range(2)]
+
+
+def other_blocks(k):
+    return [4 * j + (1 - k.g if half == 0 else 2 + k.g) for j in range(4) for half in range(2)]
+
+
+def my_block(k, i):
+    return 4 * (i // 2) + jnp.where(lax.rem(i, 2) == 0, k.g, 3 - k.g)
+
+
+class Post:
+    def __init__(self, k, sends, receives):
+        self.k, self.out, self.base = k, sem(k, sends), sem(k, receives)
+        self.sent = []
+
+    def copy(self, src, dst, i, slot, device):
+        k = self.k
+        is_self = jnp.logical_and(device[0] == k.g, device[1] == k.s)
+        return is_self, remote(src, dst, k.ss.at[self.out + i], k.rs.at[self.base + slot], device)
+
+    def start(self, src, dst, i, slot, device):
+        k = self.k
+        is_self, copy = self.copy(src, dst, i, slot, device)
 
         @pl.when(is_self)
         def _():
-            pltpu.make_async_copy(source.at[h], target.at[k.s], k.rs.at[base + k.s]).start()
+            pltpu.make_async_copy(src, dst, k.rs.at[self.base + slot]).start()
 
         @pl.when(jnp.logical_not(is_self))
         def _():
             copy.start()
 
-    for b in my_blocks(k):
-        pltpu.make_async_copy(target.at[b], target.at[b], k.rs.at[base + b]).wait()
-        if after is not None:
-            after(b)
-    return selves
-
-
-def from_heads(k, source, target):
-    base = sem(k, 8)
-    out = sem(k, 8)
-    selves = []
-    group, head = k.s // 8, lax.rem(k.s, 8)
-    for i, b in enumerate(my_blocks(k)):
-        is_self = jnp.logical_and(group == k.g, b == k.s)
-        copy = remote(source.at[i], target.at[head], k.ss.at[out + i], k.rs.at[base + head], (group, b))
-        selves.append((is_self, copy))
-
-        @pl.when(is_self)
-        def _():
-            pltpu.make_async_copy(source.at[i], target.at[head], k.rs.at[base + head]).start()
-
-        @pl.when(jnp.logical_not(is_self))
-        def _():
-            copy.start()
-
-    for h in range(8):
-        pltpu.make_async_copy(target.at[h], target.at[h], k.rs.at[base + h]).wait()
-    return selves
-
-
-def finish(selves):
-    for is_self, copy in selves:
+    def wait(self, dst, slot):
+        pltpu.make_async_copy(dst, dst, self.k.rs.at[self.base + slot]).wait()
+
+    def finish(self, src, dst, i, slot, device):
+        is_self, copy = self.copy(src, dst, i, slot, device)
+
         @pl.when(jnp.logical_not(is_self))
         def _():
             copy.wait_send()
 
 
+class ToHeads(Post):
+    def __init__(self, k, source, target):
+        super().__init__(k, 8, 16)
+        self.source, self.target = source, target
+
+    def each(self, act):
+        k = self.k
+        for h in range(8):
+            act(self.source.at[h], self.target.at[k.s], h, k.s, (k.side, k.g * 8 + h))
+
+    def send(self):
+        self.each(self.start)
+
+    def take(self, b):
+        self.wait(self.target.at[b], b)
+
+    def done(self):
+        self.each(self.finish)
+
+
+class FromHeads(Post):
+    def __init__(self, k, source, target, rows):
+        super().__init__(k, 8, 8)
+        self.source, self.target, self.rows = source, target, rows
+
+    def args(self, i, b):
+        k = self.k
+        head = lax.rem(k.s, 8)
+        return self.source.at[i, self.rows], self.target.at[head, self.rows], i, head, (k.s // 8, b)
+
+    def send(self, i, b):
+        self.start(*self.args(i, b))
+
+    def take(self, h):
+        self.wait(self.target.at[h, self.rows], h)
+
+    def done(self):
+        for i, b in enumerate(my_blocks(self.k)):
+            self.finish(*self.args(i, b))
+
+
 def rotate_block(v, cosine, sine):
     return v * cosine + swap32(v) * sine
+
+
+def rotary_tables(k, layer):
+    rows, _ = layer_sizes(layer)
+    lane = lanes((1, 128))
+    freqs = jnp.zeros((1, 128), F32)
+    for i in range(32):
+        freqs = jnp.where(lane % 32 == i, 10000.0 ** (-i / 32), freqs)
+    position = k.s * rows + lax.broadcasted_iota(jnp.int32, (rows, 1), 0)
+    angles = position.astype(F32) * freqs
+    k.cos[layer][...] = jnp.cos(angles)
+    k.sin[layer][...] = jnp.sin(angles) * jnp.where(lane % 64 < 32, -1.0, 1.0)
 
 
 def layer_sizes(layer):
@@ -691,81 +791,106 @@
     return rows, (rows // 2 + 15) // 16 * 16
 
 
-def attend_loop(k, layer, body):
-    for part in range(2):
-        @pl.loop(0, 4)
+def attend_loop(layer, part, body, between=None):
+    if layer == 1:
+        body(list(range(8)), 16)
+        return
+    for first in (0, 2):
+        @pl.loop(first, first + 2)
         def _(n):
-            i = part * 4 + n
-            j, half = i // 2, lax.rem(i, 2)
-            b = 4 * j + jnp.where(half == 0, k.side_own, 3 - k.side_own)
-            body(i, b, 8 * (part + 1))
-
-
-def masked_scores(k, layer, b, q, kv):
-    rows, _ = layer_sizes(layer)
+            body([part * 4 + n], 8 * (part + 1))
+
+        if between is not None and first == 0:
+            between()
+
+
+def stack(pieces):
+    return pieces[0] if len(pieces) == 1 else jnp.concatenate(pieces, axis=0)
+
+
+def masked_scores(q, kv, places):
     scores = dot_nt(q, kv)
-    shape = scores.shape
-    visible = lanes(shape) <= b * rows + lax.broadcasted_iota(jnp.int32, shape, 0)
-    return jnp.where(visible, scores, MASK_FILL)
-
-
-def queries(inbox, b, rows):
-    return low(unpack_left(inbox[b, 0 : (rows // 2 + 15) // 16 * 16, :].astype(F32)[: rows // 2]) * 0.125)
-
-
-def attention_forward(k, layer):
+    return jnp.where(lanes(scores.shape) <= places, scores, MASK_FILL)
+
+
+def stacked_queries(k, layer, items):
+    rows, pad = layer_sizes(layer)
+    blocks = [my_block(k, i) for i in items]
+    q = stack([unpack_left(k.inbox[layer][b, 0:pad, :].astype(F32)[: rows // 2]) for b in blocks])
+    places = stack([b * rows + lax.broadcasted_iota(jnp.int32, (rows, 1), 0) for b in blocks])
+    return low(q * 0.125), blocks, places
+
+
+def attention_forward(k, layer, part, post):
     rows, pad = layer_sizes(layer)
     inbox, outbox, lse, keep = k.inbox[layer], k.abox[layer], k.lse[layer], k.att[layer]
 
-    def body(i, b, blocks):
-        q = queries(inbox, b, rows)
-        kv = inbox[0:blocks, pad : pad + rows, :].reshape(blocks * rows, 128)
-        scores = masked_scores(k, layer, b, q, kv)
+    def body(items, count):
+        q, blocks, places = stacked_queries(k, layer, items)
+        kv = inbox[0:count, pad : pad + rows, :].reshape(count * rows, 128)
+        scores = masked_scores(q, kv, places)
         top = jnp.max(scores, axis=-1, keepdims=True)
         prob = jnp.exp(scores - top)
         total = jnp.sum(prob, axis=-1, keepdims=True)
         out = dot(low(prob), kv) / total
-        lse[i] = jnp.broadcast_to(top + jnp.log(total), (rows, 128))
-        keep[i] = out
-        outbox[i, 0 : rows // 2, :] = low(pack_right(out))
-
-    attend_loop(k, layer, body)
-
-
-def attention_backward(k, layer):
+        stat = jnp.broadcast_to(top + jnp.log(total), out.shape)
+        for n, (i, b) in enumerate(zip(items, blocks)):
+            span = slice(n * rows, (n + 1) * rows)
+            lse[i] = stat[span]
+            keep[i] = out[span]
+            outbox[i, 0 : rows // 2, :] = low(pack_right(out[span]))
+            post.send(i, b)
+
+    attend_loop(layer, part, body)
+
+
+def attention_backward(k, layer, part, post, between=None):
     rows, pad = layer_sizes(layer)
     inbox, gradbox, lse, keep = k.inbox[layer], k.gbox[layer], k.lse[layer], k.att[layer]
     dkvt, outbox = k.dkvt[layer], k.dbox[layer]
-    dkvt[...] = jnp.zeros_like(dkvt)
-
-    def body(i, b, blocks):
-        q = queries(inbox, b, rows)
-        kv = inbox[0:blocks, pad : pad + rows, :].reshape(blocks * rows, 128)
-        grad = unpack_right(gradbox[b].astype(F32)[: rows // 2])
-        delta = jnp.sum(grad * keep[i], axis=-1, keepdims=True)
+
+    def body(items, count):
+        q, blocks, places = stacked_queries(k, layer, items)
+        kv = inbox[0:count, pad : pad + rows, :].reshape(count * rows, 128)
+        grad = stack([unpack_right(gradbox[b].astype(F32)[: rows // 2]) for b in blocks])
+        delta = jnp.sum(grad * stack([keep[i] for i in items]), axis=-1, keepdims=True)
         grad = low(grad)
-        prob = jnp.exp(masked_scores(k, layer, b, q, kv) - lse[i][:, 0:1])
+        prob = jnp.exp(masked_scores(q, kv, places) - stack([lse[i] for i in items])[:, 0:1])
         grad_prob = dot_nt(grad, kv)
         ds = low(prob * (grad_prob - delta))
         dq = dot(ds, kv) * 0.125
-        outbox[i, 0 : rows // 2, :] = low(pack_left(dq))
-        both = dot_tn(q, ds) + dot_tn(grad, low(prob))
-        dkvt[:, 0 : blocks * rows] += both
-
-    attend_loop(k, layer, body)
-    dkv, theirs, got = k.dkv[layer], k.dkv_out[layer], k.dkv_in[layer]
-    dkv[...] = dkvt[...].T.reshape(16, rows, 128)
-    mine = my_blocks(k)
-    for i in range(8):
-        j, half = i // 2, i % 2
-        other = 4 * j + ((1 - k.side_own) if half == 0 else 2 + k.side_own)
-        theirs[i] = dkv[other]
-    at = sem(k)
-    copy = remote(theirs, got, k.ss.at[at], k.rs.at[at], k.dev(1 - k.g, k.z, k.y, k.x))
-    copy.start()
-    copy.wait()
-    for i, b in enumerate(mine):
-        outbox[i, pad : pad + rows, :] = low(dkv[b] + got[i])
+        for n, (i, b) in enumerate(zip(items, blocks)):
+            outbox[i, 0 : rows // 2, :] = low(pack_left(dq[n * rows : (n + 1) * rows]))
+            post.send(i, b)
+        dkvt[:, 0 : count * rows] += dot_tn(q, ds) + dot_tn(grad, low(prob))
+
+    attend_loop(layer, part, body, between)
+
+
+class KeySums:
+    def __init__(self, k, layer, part, post):
+        rows, _ = layer_sizes(layer)
+        self.k, self.layer, self.post = k, layer, post
+        self.items = range(8) if layer == 1 else range(4 * part, 4 * part + 4)
+        first, count = (0, 16) if layer == 1 else (8 * part, 8)
+        k.dkv[layer][first : first + count] = (
+            k.dkvt[layer][:, first * rows : (first + count) * rows].T.reshape(count, rows, 128)
+        )
+        others = other_blocks(k)
+        for i in self.items:
+            k.dkv_out[layer][i] = k.dkv[layer][others[i]]
+        span = pl.ds(self.items[0], len(self.items))
+        self.copy = hop(k, k.dkv_out[layer].at[span], k.dkv_in[layer].at[span], k.dev(1 - k.g, k.z, k.y, k.x))
+        self.copy.start()
+
+    def send(self):
+        k, layer = self.k, self.layer
+        rows, pad = layer_sizes(layer)
+        self.copy.wait()
+        mine = my_blocks(k)
+        for i in self.items:
+            k.dbox[layer][i, pad : pad + rows, :] = low(k.dkv[layer][mine[i]] + k.dkv_in[layer][i])
+            self.post.send(i, mine[i])
 
 
 def layer_ahead(k, layer, hidden):
@@ -781,7 +906,7 @@
     cos_kv, sin_kv = jnp.where(left, cosine, 1.0), jnp.where(left, sine, 0.0)
     sendbox = k.sendbox[layer]
     for part in range(3):
-        joined = dot(normed, block(k.pk, base + QKV + 16 * part))
+        joined = dot(normed, block(k, base + QKV + 16 * part))
         for n in range(4):
             piece = joined[:, 128 * n : 128 * n + 128]
             if part == 0:
@@ -791,50 +916,52 @@
             else:
                 sendbox[4 * part - 4 + n, pad : pad + rows, :] = low(rotate_block(piece, cos_kv, sin_kv))
     inbox = k.inbox[layer]
-    at = sem(k, 16)
-    share = sem(k, 16)
+    out = ToHeads(k, sendbox, inbox)
+    out.send()
+    point(k, f"f{layer}_sent")
+    share, shared = sem(k, 16), sem(k, 16)
     passed = []
-
-    def pass_on(b):
-        copy = remote(
-            inbox.at[b, pl.ds(pad, rows)],
-            inbox.at[b, pl.ds(pad, rows)],
-            k.ss.at[share + b],
-            k.rs.at[at + b],
-            k.dev(1 - k.g, k.z, k.y, k.x),
-        )
-        copy.start()
-        passed.append(copy)
-
-    selves = to_heads(k, sendbox, inbox, pass_on)
-    for i in range(8):
-        j, half = i // 2, i % 2
-        other = 4 * j + ((1 - k.side_own) if half == 0 else 2 + k.side_own)
-        ref = inbox.at[other, pl.ds(pad, rows)]
-        pltpu.make_async_copy(ref, ref, k.rs.at[at + other]).wait()
-    attention_forward(k, layer)
+    for b in my_blocks(k):
+        out.take(b)
+        ref = inbox.at[b, pl.ds(pad, rows)]
+        passed.append(remote(ref, ref, k.ss.at[share + b], k.rs.at[shared + b], k.dev(1 - k.g, k.z, k.y, k.x)))
+        passed[-1].start()
+    point(k, f"f{layer}_got")
     home = k.home[layer]
-    selves = selves + from_heads(k, k.abox[layer], home)
+    back = FromHeads(k, k.abox[layer], home, pl.ds(0, pad))
+    others = other_blocks(k)
+    for part in range(2 - layer):
+        for b in others if layer == 1 else others[4 * part : 4 * part + 4]:
+            ref = inbox.at[b, pl.ds(pad, rows)]
+            pltpu.make_async_copy(ref, ref, k.rs.at[shared + b]).wait()
+        attention_forward(k, layer, part, back)
+        point(k, f"f{layer}_part{part}")
+    for h in range(8):
+        back.take(h)
+    point(k, f"f{layer}_home")
     for n in range(4):
         pair = unpack_pair(
             home[2 * n].astype(F32)[: rows // 2], home[2 * n + 1].astype(F32)[: rows // 2]
         )
         hold.flat[:, 128 * n : 128 * n + 128] = low(pair)
-    middle = hidden + dot(hold.flat[...], block(k.pk, base + OUT))
+    middle = hidden + dot(hold.flat[...], block(k, base + OUT))
+    point(k, f"f{layer}_up")
     hold.middle[...] = middle
     unit, _ = norm_parts(middle)
     second = low(unit * k.gain[2 * layer + 1 : 2 * layer + 2, :])
     hold.second[...] = second
     for j in range(4):
-        pre = dot(second, block(k.pk, base + UP + 16 * j))
+        pre = dot(second, block(k, base + UP + 16 * j))
         hold.pre[:, 512 * j : 512 * j + 512] = pre
         hold.act[:, 512 * j : 512 * j + 512] = low(gelu(pre))
     output = middle
     for c in range(4):
-        output = output + dot(hold.act[:, 512 * c : 512 * c + 512], down_block(k.pk, base + DOWN, c))
-    finish(selves)
+        output = output + dot(hold.act[:, 512 * c : 512 * c + 512], down_block(k, base + DOWN, c))
+    out.done()
+    back.done()
     for copy in passed:
         copy.wait_send()
+    point(k, f"f{layer}_end")
     return output
 
 
@@ -848,32 +975,55 @@
     for c in range(4):
         cols = slice(512 * c, 512 * c + 512)
         put_down(k.gr, base + DOWN, c, dot_tn(hold.act[:, cols], fall))
-        grad_act = dot_nt(fall, down_block(k.pk, base + DOWN, c))
+        grad_act = dot_nt(fall, down_block(k, base + DOWN, c))
         grad_pre = low(grad_act * gelu_grad(hold.pre[:, cols]))
         put_block(k.gr, base + UP + 16 * c, dot_tn(second, grad_pre))
-        grad_second = grad_second + dot_nt(grad_pre, block(k.pk, base + UP + 16 * c))
+        grad_second = grad_second + dot_nt(grad_pre, block(k, base + UP + 16 * c))
+    if layer == 1:
+        point(k, "b1_ff")
     gain = k.gain[2 * layer + 1 : 2 * layer + 2, :]
     grad_mid, k.gain_grads[2 * layer + 1] = norm_back(hold.middle[...], gain, grad_second)
     grad_middle = grad_out + grad_mid
     hold.middle[...] = grad_middle
     proj = low(grad_middle)
     put_block(k.gr, base + OUT, dot_tn(hold.flat[...], proj))
-    grad_att = dot_nt(proj, block(k.pk, base + OUT))
+    grad_att = dot_nt(proj, block(k, base + OUT))
     gsend = k.gsend[layer]
     for n in range(4):
         piece = grad_att[:, 128 * n : 128 * n + 128]
         gsend[2 * n, 0 : rows // 2, :] = low(pack_pair(piece, 0))
         gsend[2 * n + 1, 0 : rows // 2, :] = low(pack_pair(piece, 1))
-    selves = to_heads(k, gsend, k.gbox[layer])
-    attention_backward(k, layer)
+    out = ToHeads(k, gsend, k.gbox[layer])
+    out.send()
+    if layer == 0:
+        point(k, "b0_ff")
     back = k.back[layer]
-    selves = selves + from_heads(k, k.dbox[layer], back)
+    home_q = FromHeads(k, k.dbox[layer], back, pl.ds(0, pad))
+    home_kv = FromHeads(k, k.dbox[layer], back, pl.ds(pad, rows))
+    k.dkvt[layer][...] = jnp.zeros_like(k.dkvt[layer])
+    point(k, f"b{layer}_sent")
+    mine = my_blocks(k)
+    sums = None
+    for part in reversed(range(2 - layer)):
+        for b in mine if layer == 1 else mine[4 * part : 4 * part + 4]:
+            out.take(b)
+        attention_backward(k, layer, part, home_q, None if sums is None else sums.send)
+        sums = KeySums(k, layer, part, home_kv)
+        point(k, f"b{layer}_part{part}")
+    sums.send()
+    point(k, f"b{layer}_sums")
+    for h in range(8):
+        home_q.take(h)
     cosine, sine = k.cos[layer][...], k.sin[layer][...]
     left = lanes(cosine.shape) < 64
     cos_kv, sin_kv = jnp.where(left, cosine, 1.0), jnp.where(left, sine, 0.0)
     normed = hold.normed[...]
     grad_normed = jnp.zeros((rows, D), F32)
     for part in range(3):
+        if part == 1:
+            for h in range(8):
+                home_kv.take(h)
+            point(k, f"b{layer}_home")
         for n in range(4):
             if part == 0:
                 piece = unpack_pair(
@@ -887,10 +1037,14 @@
             hold.gj[:, 128 * n : 128 * n + 128] = low(piece)
         gj = hold.gj[...]
         put_block(k.gr, base + QKV + 16 * part, dot_tn(normed, gj))
-        grad_normed = grad_normed + dot_nt(gj, block(k.pk, base + QKV + 16 * part))
+        grad_normed = grad_normed + dot_nt(gj, block(k, base + QKV + 16 * part))
     gain = k.gain[2 * layer : 2 * layer + 1, :]
     grad_in, k.gain_grads[2 * layer] = norm_back(hold.hidden[...], gain, grad_normed)
-    finish(selves)
+    out.done()
+    home_q.done()
+    home_kv.done()
+    if layer == 1:
+        point(k, "b1_end")
     return hold.middle[...] + grad_in
 
 
@@ -900,12 +1054,19 @@
 
 
 def forward_backward(k):
-    k.side_own = k.g
     rows, short = 144, 48
-    k.gain[...] = jnp.sum(k.pk[:, :, :, :, GN : GN + 16, :].astype(F32).reshape(32, 16, 512), axis=0)
+    need(k, EG)
+    gains = jnp.sum(k.pk[:, :, :, :, EG : EG + 16, 256:512].astype(F32).reshape(32, 16, 256), axis=0)
+    k.gain[:, 0:256] = gains[0:8]
+    k.gain[:, 256:512] = gains[8:16]
     k.gain_grads = [None] * 5
-    table = k.pk[:, :, :, :, EH : EH + 16, 256:512].reshape(512, 256)
-    ids = k.ids[...]
+    table = k.pk[:, :, :, :, EG : EG + 16, 0:256].reshape(512, 256)
+    k.columns[0:1, 0:rows] = k.ids[...].astype(F32)
+    k.columns[1:2, 0:rows] = k.targets[...].astype(F32)
+    columns = k.columns[...].T
+    ids, targets = columns[0:rows, 0:1].astype(jnp.int32), columns[0:rows, 1:2].astype(jnp.int32)
+    for layer in range(2):
+        rotary_tables(k, layer)
     first_in = jnp.concatenate([dot(byte_matrix(ids, 0), table), dot(byte_matrix(ids, 1), table)], axis=1)
     first = layer_ahead(k, 0, first_in)
     k.shift[8 : 8 + rows, :] = first
@@ -935,18 +1096,18 @@
         t = lax.broadcasted_iota(jnp.int32, shape, 1 - axis) - offset
         return jnp.where((t >= 3 * j) & (t < 3 * j + 3), 1.0, 0.0)
 
-    exact = functools.partial(jnp.dot, preferred_element_type=F32, precision=lax.Precision.HIGHEST)
     pooled = exact(pool_matrix((short, rows + 8), 6, 0), k.shift[...]) / 3.0
     short_out = layer_ahead(k, 1, pooled)
     upsampled = k.shift[8 : 8 + rows, :] + exact(pool_matrix((rows, short), 0, 1), short_out)
     gain = k.gain[4:5, :]
     unit, _ = norm_parts(upsampled)
     final = low(unit * gain)
-    head = k.pk[:, :, :, :, EH : EH + 16, 0:256].reshape(512, 256)
+    need(k, HEAD)
+    head = k.pk[:, :, :, :, HEAD : HEAD + 16, 0:256].reshape(512, 256)
     logits = dot(final, head)
     top = jnp.max(logits, axis=-1, keepdims=True)
     log_total = top + jnp.log(jnp.sum(jnp.exp(logits - top), axis=-1, keepdims=True))
-    hot = jnp.where(lanes((rows, 256)) == k.targets[...], 1.0, 0.0)
+    hot = jnp.where(lanes((rows, 256)) == targets, 1.0, 0.0)
     picked = jnp.sum(hot * logits, axis=-1, keepdims=True)
     position = k.s * rows + lax.broadcasted_iota(jnp.int32, (rows, 1), 0)
     length = jnp.zeros((rows, 1), F32)
@@ -958,7 +1119,8 @@
         begin = begin + size
     k.loss = jnp.sum((log_total - picked) / length, axis=0, keepdims=True)
     grad_logits = low((jnp.exp(logits - log_total) - hot) / length)
-    k.gr[:, :, :, :, EH : EH + 16, 0:256] = low(dot_tn(final, grad_logits)).reshape(2, 4, 2, 2, 16, 256)
+    k.gr[:, :, :, :, HEAD : HEAD + 16, 0:256] = low(dot_tn(final, grad_logits)).reshape(2, 4, 2, 2, 16, 256)
+    k.gr[:, :, :, :, HEAD : HEAD + 16, 256:512] = jnp.zeros((2, 4, 2, 2, 16, 256), LOW)
     grad_final = dot_nt(grad_logits, head)
     grad_up, k.gain_grads[4] = norm_back(upsampled, gain, grad_final)
     k.up[...] = grad_up
@@ -994,109 +1156,152 @@
     table_grad = dot_tn(byte_matrix(ids, 0), low(grad_in[:, 0:256])) + dot_tn(
         byte_matrix(ids, 1), low(grad_in[:, 256:512])
     )
-    k.gr[:, :, :, :, EH : EH + 16, 256:512] = low(table_grad).reshape(2, 4, 2, 2, 16, 256)
-    gains = jnp.concatenate(k.gain_grads + [jnp.zeros((11, D), F32)], axis=0)
-    k.gr[:, :, :, :, GN : GN + 16, :] = low(jnp.broadcast_to(gains[None], (32, 16, 512))).reshape(2, 4, 2, 2, 16, 512)
+    k.gr[:, :, :, :, EG : EG + 16, 0:256] = low(table_grad).reshape(2, 4, 2, 2, 16, 256)
+    fill = [jnp.zeros((3, 256), F32)]
+    gains = jnp.concatenate(
+        [v[:, 0:256] for v in k.gain_grads] + fill + [v[:, 256:512] for v in k.gain_grads] + fill, axis=0
+    )
+    gains = jnp.broadcast_to(low(gains)[None], (32, 16, 256))
+    k.gr[:, :, :, :, EG : EG + 16, 256:512] = gains.reshape(2, 4, 2, 2, 16, 256)
+    point(k, "b0_end")
 
 
 def add_into(ref, other):
     ref[...] = low(ref[...].astype(F32) + other[...].astype(F32))
 
 
-def reduce_grads(k):
+def reduce_piece(k, r0, rm, r1):
     g, z, y, x, dev, gr = k.g, k.z, k.y, k.x, k.dev, k.gr
-    half = ROWS // 2
-    a, b = pl.ds(0, half), pl.ds(half, half)
-
-    def send(src, dst, device):
-        i = sem(k)
-        return remote(src, dst, k.ss.at[i], k.rs.at[i], device)
-
-    copy = send(gr.at[1 - g], k.rc, dev(1 - g, z, y, x))
-    copy.start()
-    copy.wait()
+    a, b, every = pl.ds(r0, rm - r0), pl.ds(rm, r1 - rm), pl.ds(r0, r1 - r0)
+    waiting = [hop(k, gr.at[1 - g, :, :, :, every], k.rc.at[:, :, :, every], dev(1 - g, z, y, x))]
+    start_all(waiting)
+    yield
+    wait_all(waiting)
 
     @pl.loop(0, 16)
     def _(n):
-        add_into(gr.at[g, n // 4, lax.rem(n // 2, 2), lax.rem(n, 2)], k.rc.at[n // 4, lax.rem(n // 2, 2), lax.rem(n, 2)])
-
-    stage = [
-        send(gr.at[g, :, :, 1 - x, a], k.r2.at[:, :, a], dev(g, z, y, 1 - x)),
-        send(gr.at[g, :, 1 - y, :, b], k.r2.at[:, :, b], dev(g, z, 1 - y, x)),
+        place = (n // 4, lax.rem(n // 2, 2), lax.rem(n, 2), every)
+        add_into(gr.at[(g,) + place], k.rc.at[place])
+
+    waiting = [
+        hop(k, gr.at[g, :, :, 1 - x, a], k.r2.at[:, :, a], dev(g, z, y, 1 - x)),
+        hop(k, gr.at[g, :, 1 - y, :, b], k.r2.at[:, :, b], dev(g, z, 1 - y, x)),
     ]
-    start_all(stage)
-    wait_all(stage)
+    start_all(waiting)
+    yield
+    wait_all(waiting)
 
     @pl.loop(0, 8)
     def _(n):
         add_into(gr.at[g, n // 2, lax.rem(n, 2), x, a], k.r2.at[n // 2, lax.rem(n, 2), a])
         add_into(gr.at[g, n // 2, y, lax.rem(n, 2), b], k.r2.at[n // 2, lax.rem(n, 2), b])
 
-    stage = [
-        send(gr.at[g, :, 1 - y, x, a], k.r1.at[:, a], dev(g, z, 1 - y, x)),
-        send(gr.at[g, :, y, 1 - x, b], k.r1.at[:, b], dev(g, z, y, 1 - x)),
+    waiting = [
+        hop(k, gr.at[g, :, 1 - y, x, a], k.r1.at[:, a], dev(g, z, 1 - y, x)),
+        hop(k, gr.at[g, :, y, 1 - x, b], k.r1.at[:, b], dev(g, z, y, 1 - x)),
     ]
-    start_all(stage)
-    wait_all(stage)
+    start_all(waiting)
+    yield
+    wait_all(waiting)
 
     @pl.loop(0, 4)
     def _(n):
-        add_into(gr.at[g, n, y, x], k.r1.at[n])
-
-    stage = []
-    for hop in (1, 2, 3):
-        to = lax.rem(z + hop, 4)
-        stage.append(send(gr.at[g, to, y, x], k.rz.at[hop - 1], dev(g, to, y, x)))
-    start_all(stage)
-    wait_all(stage)
+        add_into(gr.at[g, n, y, x, every], k.r1.at[n, every])
+
+    waiting = []
+    for n in (2, 1, 3):
+        to = lax.rem(z + n, 4)
+        waiting.append(hop(k, gr.at[g, to, y, x, every], k.rz.at[n - 1, every], dev(g, to, y, x)))
+    start_all(waiting)
+    yield
+    wait_all(waiting)
+    k.summed.update(range(r0, r1, 16))
+    yield
+
+
+def own_sum(k, row, count):
+    assert k.summed.issuperset(range(row, row + count, 16))
+    rows = pl.ds(row, count)
+    v = k.gr[k.g, k.z, k.y, k.x, rows].astype(F32)
+    for i in range(3):
+        v = v + k.rz[i, rows].astype(F32)
+    return v
+
+
+def square(k, v):
+    k.sq = k.sq + jnp.sum(jnp.sum(v * v, axis=1, keepdims=True), axis=0, keepdims=True)
+
+
+def store_qkv(k, layer):
+    v = own_sum(k, LAYER0 + layer * LAYER_ROWS + QKV, 48)
+    square(k, v)
+    k.g_qkv[layer, :, 0:512] = v[0:16]
+    for pair in range(4):
+        row, col = 16 + 16 * (pair // 2), 256 * (pair % 2)
+        even = v[row : row + 16, col : col + 128]
+        odd = v[row : row + 16, col + 128 : col + 256]
+        left = lanes(even.shape) < 64
+        k.g_qkv[layer, :, 512 + 128 * pair : 640 + 128 * pair] = jnp.where(left, even, roll64(odd))
+        k.g_qkv[layer, :, 1024 + 128 * pair : 1152 + 128 * pair] = jnp.where(left, roll64(even), odd)
+
+
+def store_out(k, layer):
+    v = own_sum(k, LAYER0 + layer * LAYER_ROWS + OUT, 16)
+    square(k, v)
+    k.g_out[layer] = v
+
+
+def store_ff(k, layer):
+    v = own_sum(k, LAYER0 + layer * LAYER_ROWS + UP, 64)
+    square(k, v)
+    for j in range(4):
+        k.g_up[layer, :, 512 * j : 512 * j + 512] = v[16 * j : 16 * j + 16]
+    v = own_sum(k, LAYER0 + layer * LAYER_ROWS + DOWN, 64)
+    square(k, v)
+    k.g_down[layer] = v
+
+
+def store_head(k):
+    v = own_sum(k, HEAD, 16)[:, 0:256]
+    square(k, v)
+    k.g_head[...] = v
+
+
+def store_rest(k):
+    v = own_sum(k, EG, 16)
+    square(k, v[:, 0:256])
+    k.g_embed[:, 0:256] = v[0:8, 0:256]
+    k.g_embed[:, 256:512] = v[8:16, 0:256]
+    gains = jnp.where(k.g == 0, v[0:8, 256:512], v[8:16, 256:512])
+    row, column = lax.broadcasted_iota(jnp.int32, (256, 16), 0), lax.broadcasted_iota(jnp.int32, (256, 16), 1)
+    gains = exact(gains, jnp.where(row - 16 * k.s == column, 1.0, 0.0))[0:5]
+    square(k, gains)
+    k.g_gains[...] = gains
+
+
+def finish_grads(k):
+    g = k.g
     k.sq = jnp.zeros((1, 1), F32)
 
-    def total(row, count):
-        rows = pl.ds(row, count)
-        v = gr[g, z, y, x, rows].astype(F32)
-        for i in range(3):
-            v = v + k.rz[i, rows].astype(F32)
-        return v
-
-    def square(v):
-        k.sq = k.sq + jnp.sum(jnp.sum(v * v, axis=1, keepdims=True), axis=0, keepdims=True)
-
-    v = total(EH, 16)
-    square(v)
-    k.g_head[...] = v[:, 0:256]
-    k.g_embed[:, 0:256] = v[0:8, 256:512]
-    k.g_embed[:, 256:512] = v[8:16, 256:512]
-    v = total(GN, 16)
-    pick = (
-        lax.broadcasted_iota(jnp.int32, (D, 16), 0) - 16 * (g * 16 + k.s)
-        == lax.broadcasted_iota(jnp.int32, (D, 16), 1)
-    )
-    v = jnp.dot(v, jnp.where(pick, 1.0, 0.0), preferred_element_type=F32, precision=lax.Precision.HIGHEST)
-    square(v)
-    k.g_gains[...] = v[0:5]
-    for layer in range(2):
-        base = LAYER0 + layer * LAYER_ROWS
-        v = total(base + QKV, 48)
-        square(v)
-        k.g_qkv[layer, :, 0:512] = v[0:16]
-        for pair in range(4):
-            row, col = 16 + 16 * (pair // 2), 256 * (pair % 2)
-            even = v[row : row + 16, col : col + 128]
-            odd = v[row : row + 16, col + 128 : col + 256]
-            left = lanes(even.shape) < 64
-            k.g_qkv[layer, :, 512 + 128 * pair : 640 + 128 * pair] = jnp.where(left, even, roll64(odd))
-            k.g_qkv[layer, :, 1024 + 128 * pair : 1152 + 128 * pair] = jnp.where(left, roll64(even), odd)
-        v = total(base + OUT, 16)
-        square(v)
-        k.g_out[layer] = v
-        v = total(base + UP, 64)
-        square(v)
-        for j in range(4):
-            k.g_up[layer, :, 512 * j : 512 * j + 512] = v[16 * j : 16 * j + 16]
-        v = total(base + DOWN, 64)
-        square(v)
-        k.g_down[layer] = v
-
+    def complete(name):
+        for _ in k.reduces[name]:
+            pass
+
+    next(k.reduces["A"])
+    complete("D")
+    store_ff(k, 1)
+    store_head(k)
+    next(k.reduces["A"])
+    complete("C")
+    store_qkv(k, 1)
+    store_out(k, 1)
+    next(k.reduces["A"])
+    complete("B")
+    store_out(k, 0)
+    store_ff(k, 0)
+    complete("A")
+    store_qkv(k, 0)
+    store_rest(k)
     lane = lanes((8, 128))
     k.stat[0] = jnp.where(lane == 0, k.sq, jnp.where(lane == 1, k.loss, 0.0))
     me = g * 16 + k.s
@@ -1121,10 +1326,9 @@
 
 IN_NAMES = (
     "ids", "targets", "lengths", "w_qkv", "w_out", "w_up", "w_down", "embed", "head", "gains",
-    "cos0", "sin0", "cos1", "sin1",
 )
 OUT_NAMES = ("g_qkv", "g_out", "g_up", "g_down", "g_embed", "g_head", "g_gains", "stats")
-SEMS = 384
+SEMS = 512
 
 
 def scratch_shapes():
@@ -1135,15 +1339,18 @@
         "r2": ((4, 2, ROWS, D), LOW),
         "r1": ((4, ROWS, D), LOW),
         "rz": ((3, ROWS, D), LOW),
-        "gain": ((16, D), F32),
+        "gain": ((8, D), F32),
         "shift": ((152, D), F32),
         "pool": ((56, D), F32),
         "up": ((144, D), F32),
         "stat": ((32, 8, 128), F32),
+        "columns": ((128, 256), F32),
     }
     for layer in range(2):
         rows, pad = layer_sizes(layer)
         for name, shape, kind in (
+            ("cos", (rows, 128), F32),
+            ("sin", (rows, 128), F32),
             ("sendbox", (8, pad + rows, 128), LOW),
             ("inbox", (16, pad + rows, 128), LOW),
             ("abox", (8, pad, 128), LOW),
@@ -1180,13 +1387,17 @@
 
 
 def update_kernel(*refs):
-    stats, grads, masters, firsts, seconds = refs[0], refs[1:8], refs[8:15], refs[15:22], refs[22:29]
-    outs = refs[29:]
+    stats, grads, state, outs = refs[0], refs[1:8], refs[8:29], refs[29:50]
+    held, got, sems = refs[50:57], refs[57:78], refs[78]
+    copies = [pltpu.make_async_copy(src, dst, sems.at[i]) for i, (src, dst) in enumerate(zip(grads + state, held + got))]
+    start_all(copies)
     norm = jnp.sqrt(stats[0:1, 0:1])
     clip = jnp.minimum(1.0, CLIP_NORM / norm)
     for i in range(7):
+        for j in range(4):
+            copies[7 * j + i].wait()
         results = adam_update(
-            masters[i][...], grads[i][...] * clip, firsts[i][...], seconds[i][...], STEP_RATES[i], WEIGHT_DECAYS[i]
+            got[i][...], held[i][...] * clip, got[7 + i][...], got[14 + i][...], STEP_RATES[i], WEIGHT_DECAYS[i]
         )
         for j in range(3):
             outs[7 * j + i][...] = results[j]
@@ -1194,41 +1405,27 @@
 
 def on_device_fast(byte_ids, targets, item_lengths, *arrays):
     masters, firsts, seconds = arrays[0:7], arrays[7:14], arrays[14:21]
-    gains = masters[6]
-    rows = byte_ids.shape[1]
-    place = lax.axis_index("seq")
-    own = lax.axis_index("dp") * lax.axis_size("seq") + place
-    lane = jnp.arange(D, dtype=jnp.int32)
-    spread = jnp.where(lane[None, :] // gains.shape[1] == own, jnp.tile(gains, (1, D // gains.shape[1])), 0.0)
-    spread = jnp.pad(spread, ((0, 16 - gains.shape[0]), (0, 0)))
-    freqs = 10000.0 ** (-jnp.arange(32, dtype=jnp.float32) / 32)
-    freqs = jnp.tile(freqs, 4)
-    sign = jnp.where(jnp.arange(128) % 64 < 32, -1.0, 1.0)
-    tables = []
-    for count in (rows, rows // RATE):
-        positions = place * count + jnp.arange(count, dtype=jnp.int32)
-        angles = positions.astype(jnp.float32)[:, None] * freqs[None, :]
-        tables += [jnp.cos(angles), jnp.sin(angles) * sign[None, :]]
     vmem = pl.BlockSpec(memory_space=pltpu.VMEM)
     shard_shapes = [jax.ShapeDtypeStruct(master.shape, F32) for master in masters]
     outs = pl.pallas_call(
         kernel,
         name="step",
         out_shape=shard_shapes + [jax.ShapeDtypeStruct((8, 128), F32)],
-        in_specs=[vmem, vmem, pl.BlockSpec(memory_space=pltpu.SMEM)] + [vmem] * 11,
+        in_specs=[vmem, vmem, pl.BlockSpec(memory_space=pltpu.SMEM)] + [vmem] * 7,
         out_specs=[vmem] * 8,
         scratch_shapes=[pltpu.VMEM(shape, kind) for shape, kind in SCRATCH.values()]
         + [pltpu.SemaphoreType.DMA((SEMS,)), pltpu.SemaphoreType.DMA((SEMS,))],
         compiler_params=pltpu.CompilerParams(collective_id=0, has_side_effects=True, vmem_limit_bytes=63 << 20),
-    )(byte_ids.reshape(rows, 1), targets.reshape(rows, 1), item_lengths, *masters[:6], spread, *tables)
+    )(byte_ids, targets, item_lengths, *masters)
     grads, stats = outs[:7], outs[7]
     results = pl.pallas_call(
         update_kernel,
         name="update",
         out_shape=shard_shapes * 3,
-        in_specs=[vmem] * 29,
+        in_specs=[vmem] + [pl.BlockSpec(memory_space=pl.ANY)] * 28,
         out_specs=[vmem] * 21,
-        compiler_params=pltpu.CompilerParams(vmem_limit_bytes=32 << 20),
+        scratch_shapes=[pltpu.VMEM(shard.shape, F32) for shard in shard_shapes * 4] + [pltpu.SemaphoreType.DMA((28,))],
+        compiler_params=pltpu.CompilerParams(vmem_limit_bytes=63 << 20),
     )(stats, *grads, *masters, *firsts, *seconds)
     return (stats[0, 1], jnp.sqrt(stats[0, 0]), *results)
 

time: 375 us -> 245 us (0.65)
  Pallas kernels: 346 us -> 241 us
  local copies, waits for them, and re-layouts: 23.6 us -> 1.34 us
    pallas_call x1, Pallas kernels: 344 us -> 236 us  [on_device_fast(): pl.pallas_call(kernel, name='step', out_shape=shard_shapes + [jax.ShapeDt...]
    unnamed x64 -> x0, local copies, waits for them, and re-layouts: 20.7 us -> none
where the time goes in v2:
time: 245 us
  Pallas kernels  241 us (98%)
  between operations  2.49 us (1%)
    pallas_call x1, Pallas kernels, on_device_fast(): pl.pallas_call(kernel, name='step', out_shape=shard_shapes + [jax.ShapeDt...  236 us
    pallas_call x1, Pallas kernels, on_device_fast(): pl.pallas_call(update_kernel, name='update', out_shape=shard_shapes * 3,...  5.14 us

profile of v2, /device:TPU:0, one launch (start us, length us, event | category | flops | bytes accessed | tf_op | source)
XLA Modules:
  0.0 245.2 jit_solution(17090861892827893986)
XLA Ops:
  0.7 236.2 %step.1 = (f32[2,16,1536]{2,1,0:T(8,128)}, f32[2,16,512]{2,1,0:T(8,128)}, f32[2,16,2048]{2,1,0:T(8,128)}, f32[2,64,512]{2,1,0:T(8,128)}, f32[8,512]{1,0:T(8,128)...) custom-call(s32[1,144]{1,0:T(1,128)} %refs_0_.1, s32[1,144]{1,0:T(1,128)} %refs_1_.1, s32[1,8]{1,0:T(1,128)} %refs_2_.1, ...), custom_call_target="tpu_custom_call" | custom-call | tf_op jit(solution)/shard_map/step/pallas_call | solution.py:1410
  236.9 5.1 %update.1 = (f32[2,16,1536]{2,1,0:T(8,128)}, f32[2,16,512]{2,1,0:T(8,128)}, f32[2,16,2048]{2,1,0:T(8,128)}, f32[2,64,512]{2,1,0:T(8,128)}, f32[8,512]{1,0:T(8,12...) custom-call(f32[8,128]{1,0:T(8,128)} %get-tuple-element.52.refs_0_, ...), custom_call_target="tpu_custom_call" | custom-call | tf_op jit(solution)/shard_map/update/pallas_call | solution.py:1421
  242.0 1.3 fusion

commit v3 on v2

--- a/solution.py
+++ b/solution.py
@@ -1,3 +1,4 @@
+import contextlib
 import functools
 
 import jax
@@ -396,36 +397,52 @@
 QKV, OUT, UP, DOWN = 0, 48, 64, 128
 HEAD = LAYER0 + 2 * LAYER_ROWS
 ROWS = HEAD + 16
-PIECES = {"A": (0, 32, 64), "B": (64, 144, 208), "C": (208, 240, 272), "D": (272, 336, ROWS)}
+PIECES = {
+    "A": (0, 16, 32),
+    "a": (32, 48, 64),
+    "B": (64, 96, 144),
+    "b": (144, 176, 208),
+    "C": (208, 240, 272),
+    "D": (272, 304, 336),
+    "d": (336, 384, ROWS),
+}
 SCHEDULE = {
-    "start": "A",
-    "packed": "ABAABCDA",
-    "f0_sent": "B",
-    "f0_got": "",
-    "f0_part0": "BC",
+    "start": "Aa",
+    "packed": "AaBAabCAaBAa",
+    "f0_sent": "Bb",
+    "f0_got": "CDd",
+    "f0_part0": "bB",
     "f0_part1": "C",
     "f0_home": "B",
-    "f0_up": "CD",
+    "f0_up": "Dbb",
+    "f0_rim": "Cd",
     "f0_end": "C",
     "f1_sent": "D",
     "f1_got": "",
-    "f1_part0": "",
-    "f1_home": "D",
-    "f1_up": "D",
-    "f1_end": "",
-    "b1_ff": "D",
+    "f1_part0": "dD",
+    "f1_home": "",
+    "f1_out": "D",
+    "f1_up": "dd",
+    "b1_ff": "dD",
     "b1_sent": "D",
-    "b1_part0": "D",
-    "b1_sums": "",
-    "b1_home": "D",
+    "b1_part0": "",
+    "b1_sums": "d",
+    "b1_home": "",
     "b1_end": "C",
-    "b0_ff": "BC",
-    "b0_sent": "BD",
-    "b0_part1": "C",
-    "b0_part0": "B",
-    "b0_sums": "C",
+    "b1_rim": "D",
+    "b0_ff": "BbCd",
+    "b0_sent": "D",
+    "b0_part1": "Bd",
+    "b0_part0": "",
+    "b0_sums": "bC",
     "b0_home": "B",
-    "b0_end": "",
+    "b0_kv": "a",
+    "b0_end": "A",
+    "tail0": "aA",
+    "tail1": "b",
+    "tail2": "aA",
+    "tail3": "b",
+    "tail4": "aA",
 }
 
 
@@ -487,6 +504,10 @@
 
 class Bag:
     pass
+
+
+def scope(name):
+    return contextlib.nullcontext()
 
 
 def remote(src, dst, send, recv, device):
@@ -535,9 +556,9 @@
 def kernel(*refs):
     k = Bag()
     names = IN_NAMES + OUT_NAMES + tuple(SCRATCH)
-    for name, ref in zip(names, refs[:-2]):
+    for name, ref in zip(names, refs[:-1]):
         setattr(k, name, ref)
-    k.ss, k.rs = refs[-2:]
+    k.sems = refs[-1]
     for name in PER_LAYER:
         setattr(k, name, [getattr(k, name + "0"), getattr(k, name + "1")])
     k.hold = []
@@ -574,9 +595,10 @@
     gains = jnp.concatenate([jnp.where(g == 0, gains, 0.0), jnp.where(g == 1, gains, 0.0)], axis=0)
     own[EG : EG + 16, 256:512] = low(gains)
     pack_layer(k, own, 0)
-    pl.semaphore_wait(barrier, 31)
-    k.gathers = {name: gather_piece(k, *rows) for name, rows in PIECES.items()}
-    k.reduces = {name: reduce_piece(k, *rows) for name, rows in PIECES.items()}
+    with scope("barrier"):
+        pl.semaphore_wait(barrier, 31)
+    k.gathers = {name: gather_piece(k, name, *rows) for name, rows in PIECES.items()}
+    k.reduces = {name: reduce_piece(k, name, *rows) for name, rows in PIECES.items()}
     k.ready, k.summed = set(), set()
     point(k, "start")
     own[HEAD : HEAD + 16, 0:256] = low(k.head[...])
@@ -610,11 +632,10 @@
     own[base + DOWN : base + DOWN + 64, :] = low(k.w_down[layer])
 
 
-def sem(k, count=1):
-    at = k.cursor
-    k.cursor += count
+def sem(k):
+    k.cursor += 1
     assert k.cursor <= SEMS
-    return at
+    return k.sems.at[k.cursor - 1]
 
 
 def start_all(copies):
@@ -627,37 +648,53 @@
         copy.wait()
 
 
-def hop(k, src, dst, device):
-    at = sem(k)
-    return remote(src, dst, k.ss.at[at], k.rs.at[at], device)
-
-
-def gather_piece(k, r0, rm, r1):
+def drain(semaphore, ref):
+    pltpu.make_async_copy(ref, ref, semaphore).wait()
+
+
+class Stage:
+    def __init__(self, k, total, moves):
+        self.total, self.sent, self.got = total, sem(k), sem(k)
+        start_all([remote(src, dst, self.sent, self.got, device) for src, dst, device in moves])
+
+    def wait(self):
+        drain(self.got, self.total)
+        drain(self.sent, self.total)
+
+
+def gather_piece(k, name, r0, rm, r1):
     g, z, y, x, dev, pk = k.g, k.z, k.y, k.x, k.dev, k.pk
     a, b, every = pl.ds(r0, rm - r0), pl.ds(rm, r1 - rm), pl.ds(r0, r1 - r0)
 
-    def send(ref, device):
-        return hop(k, ref, ref, device)
+    def stage(total, *moves):
+        return Stage(k, total, [(ref, ref, device) for ref, device in moves])
 
     stages = (
-        lambda: [send(pk.at[g, z, y, x, every], dev(g, lax.rem(z + n, 4), y, x)) for n in (2, 1, 3)],
-        lambda: [
-            send(pk.at[g, :, y, x, a], dev(g, z, 1 - y, x)),
-            send(pk.at[g, :, y, x, b], dev(g, z, y, 1 - x)),
-        ],
-        lambda: [
-            send(pk.at[g, :, :, x, a], dev(g, z, y, 1 - x)),
-            send(pk.at[g, :, y, :, b], dev(g, z, 1 - y, x)),
-        ],
-        lambda: [send(pk.at[g, :, :, :, every], dev(1 - g, z, y, x))],
-    )
-    waiting = []
-    for stage in stages:
-        wait_all(waiting)
-        waiting = stage()
-        start_all(waiting)
+        lambda: stage(
+            pk.at[g, pl.ds(0, 3), y, x, every],
+            *[(pk.at[g, z, y, x, every], dev(g, lax.rem(z + n, 4), y, x)) for n in (2, 1, 3)],
+        ),
+        lambda: stage(
+            pk.at[g, :, y, x, every],
+            (pk.at[g, :, y, x, a], dev(g, z, 1 - y, x)),
+            (pk.at[g, :, y, x, b], dev(g, z, y, 1 - x)),
+        ),
+        lambda: stage(
+            pk.at[g, :, :, x, every],
+            (pk.at[g, :, :, x, a], dev(g, z, y, 1 - x)),
+            (pk.at[g, :, y, :, b], dev(g, z, 1 - y, x)),
+        ),
+        lambda: stage(pk.at[1 - g, :, :, :, every], (pk.at[g, :, :, :, every], dev(1 - g, z, y, x))),
+    )
+    waiting = None
+    for begin in stages:
+        if waiting is not None:
+            with scope(f"gw_{name}"):
+                waiting.wait()
+        waiting = begin()
         yield
-    wait_all(waiting)
+    with scope(f"gw_{name}"):
+        waiting.wait()
     k.ready.update(range(r0, r1, 16))
     yield
 
@@ -697,77 +734,70 @@
 
 
 class Post:
-    def __init__(self, k, sends, receives):
-        self.k, self.out, self.base = k, sem(k, sends), sem(k, receives)
-        self.sent = []
-
-    def copy(self, src, dst, i, slot, device):
+    def __init__(self, k, source, groups):
+        self.k, self.source = k, source
+        self.sent, self.got = sem(k), [sem(k) for _ in range(groups)]
+
+    def start(self, src, dst, got, device):
         k = self.k
         is_self = jnp.logical_and(device[0] == k.g, device[1] == k.s)
-        return is_self, remote(src, dst, k.ss.at[self.out + i], k.rs.at[self.base + slot], device)
-
-    def start(self, src, dst, i, slot, device):
-        k = self.k
-        is_self, copy = self.copy(src, dst, i, slot, device)
 
         @pl.when(is_self)
         def _():
-            pltpu.make_async_copy(src, dst, k.rs.at[self.base + slot]).start()
+            pltpu.make_async_copy(src, dst, got).start()
 
         @pl.when(jnp.logical_not(is_self))
         def _():
-            copy.start()
-
-    def wait(self, dst, slot):
-        pltpu.make_async_copy(dst, dst, self.k.rs.at[self.base + slot]).wait()
-
-    def finish(self, src, dst, i, slot, device):
-        is_self, copy = self.copy(src, dst, i, slot, device)
-
-        @pl.when(jnp.logical_not(is_self))
+            remote(src, dst, self.sent, got, device).start()
+
+    def finish(self, one_is_self):
+        @pl.when(one_is_self)
         def _():
-            copy.wait_send()
+            drain(self.sent, self.source.at[pl.ds(0, 7)])
+
+        @pl.when(jnp.logical_not(one_is_self))
+        def _():
+            drain(self.sent, self.source)
 
 
 class ToHeads(Post):
     def __init__(self, k, source, target):
-        super().__init__(k, 8, 16)
-        self.source, self.target = source, target
-
-    def each(self, act):
+        super().__init__(k, source, 2)
+        self.target = target
+
+    def send(self):
         k = self.k
-        for h in range(8):
-            act(self.source.at[h], self.target.at[k.s], h, k.s, (k.side, k.g * 8 + h))
-
-    def send(self):
-        self.each(self.start)
-
-    def take(self, b):
-        self.wait(self.target.at[b], b)
+        for part in range(2):
+
+            @pl.when(k.s // 8 == part)
+            def _():
+                for h in range(8):
+                    self.start(self.source.at[h], self.target.at[k.s], self.got[part], (k.side, k.g * 8 + h))
+
+    def take(self, part):
+        drain(self.got[part], self.target.at[pl.ds(0, 4)])
 
     def done(self):
-        self.each(self.finish)
+        k = self.k
+        self.finish(jnp.logical_and(k.s // 8 == k.g, k.side == k.g))
 
 
 class FromHeads(Post):
-    def __init__(self, k, source, target, rows):
-        super().__init__(k, 8, 8)
-        self.source, self.target, self.rows = source, target, rows
-
-    def args(self, i, b):
+    def __init__(self, k, source, target):
+        super().__init__(k, source, 1)
+        self.target = target
+
+    def send(self, i, b):
         k = self.k
         head = lax.rem(k.s, 8)
-        return self.source.at[i, self.rows], self.target.at[head, self.rows], i, head, (k.s // 8, b)
-
-    def send(self, i, b):
-        self.start(*self.args(i, b))
-
-    def take(self, h):
-        self.wait(self.target.at[h, self.rows], h)
+        self.start(self.source.at[i], self.target.at[head], self.got[0], (k.s // 8, b))
+
+    def take(self):
+        drain(self.got[0], self.target)
 
     def done(self):
-        for i, b in enumerate(my_blocks(self.k)):
-            self.finish(*self.args(i, b))
+        k = self.k
+        self.finish(jnp.logical_and(k.s // 8 == k.g, k.side == k.g))
 
 
 def rotate_block(v, cosine, sine):
@@ -880,16 +910,18 @@
         for i in self.items:
             k.dkv_out[layer][i] = k.dkv[layer][others[i]]
         span = pl.ds(self.items[0], len(self.items))
-        self.copy = hop(k, k.dkv_out[layer].at[span], k.dkv_in[layer].at[span], k.dev(1 - k.g, k.z, k.y, k.x))
-        self.copy.start()
+        self.copy = Stage(
+            k,
+            k.dkv_in[layer].at[span],
+            [(k.dkv_out[layer].at[span], k.dkv_in[layer].at[span], k.dev(1 - k.g, k.z, k.y, k.x))],
+        )
 
     def send(self):
         k, layer = self.k, self.layer
-        rows, pad = layer_sizes(layer)
         self.copy.wait()
         mine = my_blocks(k)
         for i in self.items:
-            k.dbox[layer][i, pad : pad + rows, :] = low(k.dkv[layer][mine[i]] + k.dkv_in[layer][i])
+            k.kvbox[layer][i] = low(k.dkv[layer][mine[i]] + k.dkv_in[layer][i])
             self.post.send(i, mine[i])
 
 
@@ -919,33 +951,35 @@
     out = ToHeads(k, sendbox, inbox)
     out.send()
     point(k, f"f{layer}_sent")
-    share, shared = sem(k, 16), sem(k, 16)
-    passed = []
-    for b in my_blocks(k):
-        out.take(b)
-        ref = inbox.at[b, pl.ds(pad, rows)]
-        passed.append(remote(ref, ref, k.ss.at[share + b], k.rs.at[shared + b], k.dev(1 - k.g, k.z, k.y, k.x)))
-        passed[-1].start()
+    sent, shared = sem(k), [sem(k), sem(k)]
+    mine, others = my_blocks(k), other_blocks(k)
+    for part in range(2):
+        with scope("take"):
+            out.take(part)
+        for b in mine[4 * part : 4 * part + 4]:
+            ref = inbox.at[b, pl.ds(pad, rows)]
+            remote(ref, ref, sent, shared[part], k.dev(1 - k.g, k.z, k.y, k.x)).start()
     point(k, f"f{layer}_got")
     home = k.home[layer]
-    back = FromHeads(k, k.abox[layer], home, pl.ds(0, pad))
-    others = other_blocks(k)
+    back = FromHeads(k, k.abox[layer], home)
     for part in range(2 - layer):
-        for b in others if layer == 1 else others[4 * part : 4 * part + 4]:
-            ref = inbox.at[b, pl.ds(pad, rows)]
-            pltpu.make_async_copy(ref, ref, k.rs.at[shared + b]).wait()
-        attention_forward(k, layer, part, back)
+        for half in range(2) if layer == 1 else [part]:
+            with scope("share"):
+                drain(shared[half], inbox.at[pl.ds(0, 4), pl.ds(pad, rows)])
+        with scope("attend"):
+            attention_forward(k, layer, part, back)
         point(k, f"f{layer}_part{part}")
-    for h in range(8):
-        back.take(h)
+    with scope("home"):
+        back.take()
     point(k, f"f{layer}_home")
+    if layer == 1:
+        point(k, "f1_out")
     for n in range(4):
         pair = unpack_pair(
             home[2 * n].astype(F32)[: rows // 2], home[2 * n + 1].astype(F32)[: rows // 2]
         )
         hold.flat[:, 128 * n : 128 * n + 128] = low(pair)
     middle = hidden + dot(hold.flat[...], block(k, base + OUT))
-    point(k, f"f{layer}_up")
     hold.middle[...] = middle
     unit, _ = norm_parts(middle)
     second = low(unit * k.gain[2 * layer + 1 : 2 * layer + 2, :])
@@ -955,13 +989,12 @@
         hold.pre[:, 512 * j : 512 * j + 512] = pre
         hold.act[:, 512 * j : 512 * j + 512] = low(gelu(pre))
     output = middle
+    point(k, f"f{layer}_up")
     for c in range(4):
         output = output + dot(hold.act[:, 512 * c : 512 * c + 512], down_block(k, base + DOWN, c))
     out.done()
     back.done()
-    for copy in passed:
-        copy.wait_send()
-    point(k, f"f{layer}_end")
+    drain(sent, inbox.at[pl.ds(0, 8), pl.ds(pad, rows)])
     return output
 
 
@@ -998,22 +1031,24 @@
     if layer == 0:
         point(k, "b0_ff")
     back = k.back[layer]
-    home_q = FromHeads(k, k.dbox[layer], back, pl.ds(0, pad))
-    home_kv = FromHeads(k, k.dbox[layer], back, pl.ds(pad, rows))
+    home_q = FromHeads(k, k.dbox[layer], back)
+    home_kv = FromHeads(k, k.kvbox[layer], k.kvback[layer])
     k.dkvt[layer][...] = jnp.zeros_like(k.dkvt[layer])
     point(k, f"b{layer}_sent")
-    mine = my_blocks(k)
     sums = None
     for part in reversed(range(2 - layer)):
-        for b in mine if layer == 1 else mine[4 * part : 4 * part + 4]:
-            out.take(b)
-        attention_backward(k, layer, part, home_q, None if sums is None else sums.send)
+        with scope("take"):
+            for half in range(2) if layer == 1 else [part]:
+                out.take(half)
+        with scope("unattend"):
+            attention_backward(k, layer, part, home_q, None if sums is None else sums.send)
         sums = KeySums(k, layer, part, home_kv)
         point(k, f"b{layer}_part{part}")
-    sums.send()
+    with scope("sums"):
+        sums.send()
     point(k, f"b{layer}_sums")
-    for h in range(8):
-        home_q.take(h)
+    with scope("home_q"):
+        home_q.take()
     cosine, sine = k.cos[layer][...], k.sin[layer][...]
     left = lanes(cosine.shape) < 64
     cos_kv, sin_kv = jnp.where(left, cosine, 1.0), jnp.where(left, sine, 0.0)
@@ -1021,23 +1056,25 @@
     grad_normed = jnp.zeros((rows, D), F32)
     for part in range(3):
         if part == 1:
-            for h in range(8):
-                home_kv.take(h)
+            with scope("home_kv"):
+                home_kv.take()
             point(k, f"b{layer}_home")
         for n in range(4):
             if part == 0:
                 piece = unpack_pair(
-                    back[2 * n, 0:pad, :].astype(F32)[: rows // 2],
-                    back[2 * n + 1, 0:pad, :].astype(F32)[: rows // 2],
+                    back[2 * n].astype(F32)[: rows // 2],
+                    back[2 * n + 1].astype(F32)[: rows // 2],
                 )
                 piece = rotate_block(piece, cosine, -sine)
             else:
-                piece = back[4 * part - 4 + n, pad : pad + rows, :].astype(F32)
+                piece = k.kvback[layer][4 * part - 4 + n].astype(F32)
                 piece = rotate_block(piece, cos_kv, -sin_kv)
             hold.gj[:, 128 * n : 128 * n + 128] = low(piece)
         gj = hold.gj[...]
         put_block(k.gr, base + QKV + 16 * part, dot_tn(normed, gj))
         grad_normed = grad_normed + dot_nt(gj, block(k, base + QKV + 16 * part))
+    if layer == 0:
+        point(k, "b0_kv")
     gain = k.gain[2 * layer : 2 * layer + 1, :]
     grad_in, k.gain_grads[2 * layer] = norm_back(hold.hidden[...], gain, grad_normed)
     out.done()
@@ -1070,14 +1107,15 @@
     first_in = jnp.concatenate([dot(byte_matrix(ids, 0), table), dot(byte_matrix(ids, 1), table)], axis=1)
     first = layer_ahead(k, 0, first_in)
     k.shift[8 : 8 + rows, :] = first
-    at = sem(k)
     rim = remote(
-        k.shift.at[pl.ds(rows, 8)], k.shift.at[pl.ds(0, 8)], k.ss.at[at], k.rs.at[at], (k.g, lax.rem(k.s + 1, 16))
+        k.shift.at[pl.ds(rows, 8)], k.shift.at[pl.ds(0, 8)], sem(k), sem(k), (k.g, lax.rem(k.s + 1, 16))
     )
 
     @pl.when(k.s < 15)
     def _():
         rim.start()
+
+    point(k, "f0_rim")
 
     @pl.when(k.s > 0)
     def _():
@@ -1097,6 +1135,7 @@
         return jnp.where((t >= 3 * j) & (t < 3 * j + 3), 1.0, 0.0)
 
     pooled = exact(pool_matrix((short, rows + 8), 6, 0), k.shift[...]) / 3.0
+    point(k, "f0_end")
     short_out = layer_ahead(k, 1, pooled)
     upsampled = k.shift[8 : 8 + rows, :] + exact(pool_matrix((rows, short), 0, 1), short_out)
     gain = k.gain[4:5, :]
@@ -1127,14 +1166,15 @@
     grad_short = exact(pool_matrix((short, rows), 0, 0), grad_up)
     grad_pooled = layer_back(k, 1, grad_short)
     k.pool[0:short, :] = grad_pooled
-    at = sem(k)
     rim2 = remote(
-        k.pool.at[pl.ds(0, 8)], k.pool.at[pl.ds(short, 8)], k.ss.at[at], k.rs.at[at], (k.g, lax.rem(k.s + 15, 16))
+        k.pool.at[pl.ds(0, 8)], k.pool.at[pl.ds(short, 8)], sem(k), sem(k), (k.g, lax.rem(k.s + 15, 16))
     )
 
     @pl.when(k.s > 0)
     def _():
         rim2.start()
+
+    point(k, "b1_rim")
 
     @pl.when(k.s < 15)
     def _():
@@ -1170,51 +1210,64 @@
     ref[...] = low(ref[...].astype(F32) + other[...].astype(F32))
 
 
-def reduce_piece(k, r0, rm, r1):
+def reduce_piece(k, name, r0, rm, r1):
     g, z, y, x, dev, gr = k.g, k.z, k.y, k.x, k.dev, k.gr
     a, b, every = pl.ds(r0, rm - r0), pl.ds(rm, r1 - rm), pl.ds(r0, r1 - r0)
-    waiting = [hop(k, gr.at[1 - g, :, :, :, every], k.rc.at[:, :, :, every], dev(1 - g, z, y, x))]
-    start_all(waiting)
+    waiting = Stage(
+        k, k.rc.at[:, :, :, every], [(gr.at[1 - g, :, :, :, every], k.rc.at[:, :, :, every], dev(1 - g, z, y, x))]
+    )
     yield
-    wait_all(waiting)
-
-    @pl.loop(0, 16)
-    def _(n):
-        place = (n // 4, lax.rem(n // 2, 2), lax.rem(n, 2), every)
-        add_into(gr.at[(g,) + place], k.rc.at[place])
-
-    waiting = [
-        hop(k, gr.at[g, :, :, 1 - x, a], k.r2.at[:, :, a], dev(g, z, y, 1 - x)),
-        hop(k, gr.at[g, :, 1 - y, :, b], k.r2.at[:, :, b], dev(g, z, 1 - y, x)),
-    ]
-    start_all(waiting)
+    with scope(f"rw_{name}"):
+        waiting.wait()
+
+    with scope("radd"):
+
+        @pl.loop(0, 16)
+        def _(n):
+            place = (n // 4, lax.rem(n // 2, 2), lax.rem(n, 2), every)
+            add_into(gr.at[(g,) + place], k.rc.at[place])
+
+    waiting = Stage(
+        k,
+        k.r2.at[:, :, every],
+        [
+            (gr.at[g, :, :, 1 - x, a], k.r2.at[:, :, a], dev(g, z, y, 1 - x)),
+            (gr.at[g, :, 1 - y, :, b], k.r2.at[:, :, b], dev(g, z, 1 - y, x)),
+        ],
+    )
     yield
-    wait_all(waiting)
+    with scope(f"rw_{name}"):
+        waiting.wait()
 
     @pl.loop(0, 8)
     def _(n):
         add_into(gr.at[g, n // 2, lax.rem(n, 2), x, a], k.r2.at[n // 2, lax.rem(n, 2), a])
         add_into(gr.at[g, n // 2, y, lax.rem(n, 2), b], k.r2.at[n // 2, lax.rem(n, 2), b])
 
-    waiting = [
-        hop(k, gr.at[g, :, 1 - y, x, a], k.r1.at[:, a], dev(g, z, 1 - y, x)),
-        hop(k, gr.at[g, :, y, 1 - x, b], k.r1.at[:, b], dev(g, z, y, 1 - x)),
-    ]
-    start_all(waiting)
+    waiting = Stage(
+        k,
+        k.r1.at[:, every],
+        [
+            (gr.at[g, :, 1 - y, x, a], k.r1.at[:, a], dev(g, z, 1 - y, x)),
+            (gr.at[g, :, y, 1 - x, b], k.r1.at[:, b], dev(g, z, y, 1 - x)),
+        ],
+    )
     yield
-    wait_all(waiting)
+    with scope(f"rw_{name}"):
+        waiting.wait()
 
     @pl.loop(0, 4)
     def _(n):
         add_into(gr.at[g, n, y, x, every], k.r1.at[n, every])
 
-    waiting = []
+    moves = []
     for n in (2, 1, 3):
         to = lax.rem(z + n, 4)
-        waiting.append(hop(k, gr.at[g, to, y, x, every], k.rz.at[n - 1, every], dev(g, to, y, x)))
-    start_all(waiting)
+        moves.append((gr.at[g, to, y, x, every], k.rz.at[n - 1, every], dev(g, to, y, x)))
+    waiting = Stage(k, k.rz.at[:, every], moves)
     yield
-    wait_all(waiting)
+    with scope(f"rw_{name}"):
+        waiting.wait()
     k.summed.update(range(r0, r1, 16))
     yield
 
@@ -1232,103 +1285,120 @@
     k.sq = k.sq + jnp.sum(jnp.sum(v * v, axis=1, keepdims=True), axis=0, keepdims=True)
 
 
+def flush(k, name, layer=None):
+    src, dst = getattr(k, "s_" + name), getattr(k, "g_" + name)
+    if layer is not None:
+        src, dst = src.at[layer], dst.at[layer]
+    copy = pltpu.make_async_copy(src, dst, sem(k))
+    copy.start()
+    k.flushed.append(copy)
+
+
 def store_qkv(k, layer):
     v = own_sum(k, LAYER0 + layer * LAYER_ROWS + QKV, 48)
     square(k, v)
-    k.g_qkv[layer, :, 0:512] = v[0:16]
+    k.s_qkv[layer, :, 0:512] = v[0:16]
     for pair in range(4):
         row, col = 16 + 16 * (pair // 2), 256 * (pair % 2)
         even = v[row : row + 16, col : col + 128]
         odd = v[row : row + 16, col + 128 : col + 256]
         left = lanes(even.shape) < 64
-        k.g_qkv[layer, :, 512 + 128 * pair : 640 + 128 * pair] = jnp.where(left, even, roll64(odd))
-        k.g_qkv[layer, :, 1024 + 128 * pair : 1152 + 128 * pair] = jnp.where(left, roll64(even), odd)
+        k.s_qkv[layer, :, 512 + 128 * pair : 640 + 128 * pair] = jnp.where(left, even, roll64(odd))
+        k.s_qkv[layer, :, 1024 + 128 * pair : 1152 + 128 * pair] = jnp.where(left, roll64(even), odd)
+    flush(k, "qkv", layer)
 
 
 def store_out(k, layer):
     v = own_sum(k, LAYER0 + layer * LAYER_ROWS + OUT, 16)
     square(k, v)
-    k.g_out[layer] = v
+    k.s_out[layer] = v
+    flush(k, "out", layer)
 
 
 def store_ff(k, layer):
     v = own_sum(k, LAYER0 + layer * LAYER_ROWS + UP, 64)
     square(k, v)
     for j in range(4):
-        k.g_up[layer, :, 512 * j : 512 * j + 512] = v[16 * j : 16 * j + 16]
+        k.s_up[layer, :, 512 * j : 512 * j + 512] = v[16 * j : 16 * j + 16]
     v = own_sum(k, LAYER0 + layer * LAYER_ROWS + DOWN, 64)
     square(k, v)
-    k.g_down[layer] = v
+    k.s_down[layer] = v
+    flush(k, "up", layer)
+    flush(k, "down", layer)
 
 
 def store_head(k):
     v = own_sum(k, HEAD, 16)[:, 0:256]
     square(k, v)
-    k.g_head[...] = v
+    k.s_head[...] = v
+    flush(k, "head")
 
 
 def store_rest(k):
     v = own_sum(k, EG, 16)
     square(k, v[:, 0:256])
-    k.g_embed[:, 0:256] = v[0:8, 0:256]
-    k.g_embed[:, 256:512] = v[8:16, 0:256]
+    k.s_embed[:, 0:256] = v[0:8, 0:256]
+    k.s_embed[:, 256:512] = v[8:16, 0:256]
     gains = jnp.where(k.g == 0, v[0:8, 256:512], v[8:16, 256:512])
     row, column = lax.broadcasted_iota(jnp.int32, (256, 16), 0), lax.broadcasted_iota(jnp.int32, (256, 16), 1)
     gains = exact(gains, jnp.where(row - 16 * k.s == column, 1.0, 0.0))[0:5]
     square(k, gains)
-    k.g_gains[...] = gains
+    k.s_gains[...] = gains
+    flush(k, "embed")
+    flush(k, "gains")
 
 
 def finish_grads(k):
     g = k.g
     k.sq = jnp.zeros((1, 1), F32)
+    k.flushed = []
 
     def complete(name):
         for _ in k.reduces[name]:
             pass
 
-    next(k.reduces["A"])
+    point(k, "tail0")
     complete("D")
+    complete("d")
     store_ff(k, 1)
     store_head(k)
-    next(k.reduces["A"])
+    point(k, "tail1")
     complete("C")
     store_qkv(k, 1)
     store_out(k, 1)
-    next(k.reduces["A"])
+    point(k, "tail2")
     complete("B")
     store_out(k, 0)
+    point(k, "tail3")
+    complete("b")
     store_ff(k, 0)
+    point(k, "tail4")
     complete("A")
+    store_rest(k)
+    complete("a")
     store_qkv(k, 0)
-    store_rest(k)
     lane = lanes((8, 128))
     k.stat[0] = jnp.where(lane == 0, k.sq, jnp.where(lane == 1, k.loss, 0.0))
     me = g * 16 + k.s
-    base, out = sem(k, 32), sem(k, 32)
-
-    def stat_copy(i):
-        t = lax.rem(me + i, 32)
-        return remote(
-            k.stat.at[0], k.stat.at[i], k.ss.at[out + i], k.rs.at[base + i], (t // 16, lax.rem(t, 16))
-        )
+    sent, got = sem(k), sem(k)
 
     @pl.loop(1, 32)
     def _(i):
-        stat_copy(i).start()
-
-    @pl.loop(1, 32)
-    def _(i):
-        stat_copy(i).wait()
-
+        t = lax.rem(me + i, 32)
+        remote(k.stat.at[0], k.stat.at[i], sent, got, (t // 16, lax.rem(t, 16))).start()
+
+    with scope("stats"):
+        drain(got, k.stat.at[pl.ds(1, 31)])
+        drain(sent, k.stat.at[pl.ds(1, 31)])
     k.stats[...] = jnp.sum(k.stat[...], axis=0)
+    wait_all(k.flushed)
 
 
 IN_NAMES = (
     "ids", "targets", "lengths", "w_qkv", "w_out", "w_up", "w_down", "embed", "head", "gains",
 )
 OUT_NAMES = ("g_qkv", "g_out", "g_up", "g_down", "g_embed", "g_head", "g_gains", "stats")
-SEMS = 512
+SEMS = 200
 
 
 def scratch_shapes():
@@ -1345,6 +1415,13 @@
         "up": ((144, D), F32),
         "stat": ((32, 8, 128), F32),
         "columns": ((128, 256), F32),
+        "s_qkv": ((2, 16, 3 * D), F32),
+        "s_out": ((2, 16, D), F32),
+        "s_up": ((2, 16, 4 * D), F32),
+        "s_down": ((2, 64, D), F32),
+        "s_embed": ((8, D), F32),
+        "s_head": ((16, 256), F32),
+        "s_gains": ((5, 16), F32),
     }
     for layer in range(2):
         rows, pad = layer_sizes(layer)
@@ -1357,8 +1434,10 @@
             ("home", (8, pad, 128), LOW),
             ("gsend", (8, pad, 128), LOW),
             ("gbox", (16, pad, 128), LOW),
-            ("dbox", (8, pad + rows, 128), LOW),
-            ("back", (8, pad + rows, 128), LOW),
+            ("dbox", (8, pad, 128), LOW),
+            ("kvbox", (8, rows, 128), LOW),
+            ("back", (8, pad, 128), LOW),
+            ("kvback", (8, rows, 128), LOW),
             ("lse", (8, rows, 128), F32),
             ("att", (8, rows, 128), F32),
             ("dkvt", (128, 16 * rows), F32),
@@ -1381,53 +1460,58 @@
 SCRATCH = scratch_shapes()
 PER_LAYER = (
     "cos", "sin", "sendbox", "inbox", "abox", "home", "gsend", "gbox", "dbox", "back", "lse", "att", "dkvt", "dkv",
-    "dkv_out", "dkv_in",
+    "dkv_out", "dkv_in", "kvbox", "kvback",
 )
 HELD = ("hidden", "normed", "flat", "middle", "second", "pre", "act", "gj")
 
 
 def update_kernel(*refs):
-    stats, grads, state, outs = refs[0], refs[1:8], refs[8:29], refs[29:50]
-    held, got, sems = refs[50:57], refs[57:78], refs[78]
-    copies = [pltpu.make_async_copy(src, dst, sems.at[i]) for i, (src, dst) in enumerate(zip(grads + state, held + got))]
-    start_all(copies)
+    stats, sources, outs, loss_ref, norm_ref = refs[0], refs[1:29], refs[29:50], refs[50], refs[51]
+    held, made, sems, out_sems = refs[52:59], refs[59:66], refs[66], refs[67]
+    order = (4, 5, 6, 1, 0, 2, 3)
+    for i in order:
+        start_all([pltpu.make_async_copy(sources[7 * j + i], held[i].at[j], sems.at[i]) for j in range(4)])
     norm = jnp.sqrt(stats[0:1, 0:1])
+    loss_ref[...] = stats[0:1, 1:2]
+    norm_ref[...] = norm
     clip = jnp.minimum(1.0, CLIP_NORM / norm)
-    for i in range(7):
-        for j in range(4):
-            copies[7 * j + i].wait()
-        results = adam_update(
-            got[i][...], held[i][...] * clip, got[7 + i][...], got[14 + i][...], STEP_RATES[i], WEIGHT_DECAYS[i]
-        )
+    for i in order:
+        drain(sems.at[i], held[i])
+        gradient, master, first, second = (held[i][j] for j in range(4))
+        results = adam_update(master, gradient * clip, first, second, STEP_RATES[i], WEIGHT_DECAYS[i])
         for j in range(3):
-            outs[7 * j + i][...] = results[j]
+            made[i][j] = results[j]
+        start_all([pltpu.make_async_copy(made[i].at[j], outs[7 * j + i], out_sems.at[i]) for j in range(3)])
+    for i in order:
+        drain(out_sems.at[i], made[i])
 
 
 def on_device_fast(byte_ids, targets, item_lengths, *arrays):
     masters, firsts, seconds = arrays[0:7], arrays[7:14], arrays[14:21]
-    vmem = pl.BlockSpec(memory_space=pltpu.VMEM)
+    vmem, anywhere = pl.BlockSpec(memory_space=pltpu.VMEM), pl.BlockSpec(memory_space=pl.ANY)
     shard_shapes = [jax.ShapeDtypeStruct(master.shape, F32) for master in masters]
     outs = pl.pallas_call(
         kernel,
         name="step",
         out_shape=shard_shapes + [jax.ShapeDtypeStruct((8, 128), F32)],
         in_specs=[vmem, vmem, pl.BlockSpec(memory_space=pltpu.SMEM)] + [vmem] * 7,
-        out_specs=[vmem] * 8,
+        out_specs=[anywhere] * 7 + [vmem],
         scratch_shapes=[pltpu.VMEM(shape, kind) for shape, kind in SCRATCH.values()]
-        + [pltpu.SemaphoreType.DMA((SEMS,)), pltpu.SemaphoreType.DMA((SEMS,))],
+        + [pltpu.SemaphoreType.DMA((SEMS,))],
         compiler_params=pltpu.CompilerParams(collective_id=0, has_side_effects=True, vmem_limit_bytes=63 << 20),
     )(byte_ids, targets, item_lengths, *masters)
     grads, stats = outs[:7], outs[7]
     results = pl.pallas_call(
         update_kernel,
         name="update",
-        out_shape=shard_shapes * 3,
-        in_specs=[vmem] + [pl.BlockSpec(memory_space=pl.ANY)] * 28,
-        out_specs=[vmem] * 21,
-        scratch_shapes=[pltpu.VMEM(shard.shape, F32) for shard in shard_shapes * 4] + [pltpu.SemaphoreType.DMA((28,))],
+        out_shape=shard_shapes * 3 + [jax.ShapeDtypeStruct((1, 1), F32)] * 2,
+        in_specs=[vmem] + [anywhere] * 28,
+        out_specs=[anywhere] * 21 + [vmem] * 2,
+        scratch_shapes=[pltpu.VMEM((count, *shard.shape), F32) for count in (4, 3) for shard in shard_shapes]
+        + [pltpu.SemaphoreType.DMA((7,)), pltpu.SemaphoreType.DMA((7,))],
         compiler_params=pltpu.CompilerParams(vmem_limit_bytes=63 << 20),
     )(stats, *grads, *masters, *firsts, *seconds)
-    return (stats[0, 1], jnp.sqrt(stats[0, 0]), *results)
+    return (results[21].reshape(()), results[22].reshape(()), *results[:21])
 
 
 def solution(mesh):

time: 245 us -> 212 us (0.87)
  Pallas kernels: 241 us -> 210 us
    pallas_call x1, Pallas kernels: 236 us -> 206 us  [on_device_fast(): pl.pallas_call(kernel, name='step', out_shape=shard_shapes + [jax.ShapeDt...]
where the time goes in v3:
time: 212 us; the launch traced here: 211 us
  Pallas kernels  210 us (99%)
    pallas_call x1, Pallas kernels, on_device_fast(): pl.pallas_call(kernel, name='step', out_shape=shard_shapes + [jax.ShapeDt...  206 us
    pallas_call x1, Pallas kernels, on_device_fast(): pl.pallas_call(update_kernel, name='update', out_shape=shard_shapes * 3 +...  4.71 us

profile of v3, /device:TPU:0, one launch (start us, length us, event | category | flops | bytes accessed | tf_op | source)
XLA Modules:
  0.0 211.3 jit_solution(3922172106416126682)
XLA Ops:
  0.7 205.7 %step.1 = (f32[2,16,1536]{2,1,0:T(8,128)}, f32[2,16,512]{2,1,0:T(8,128)}, f32[2,16,2048]{2,1,0:T(8,128)}, f32[2,64,512]{2,1,0:T(8,128)}, f32[8,512]{1,0:T(8,128)...) custom-call(s32[1,144]{1,0:T(1,128)} %refs_0_.1, s32[1,144]{1,0:T(1,128)} %refs_1_.1, s32[1,8]{1,0:T(1,128)} %refs_2_.1, ...), custom_call_target="tpu_custom_call" | custom-call | tf_op jit(solution)/shard_map/step/pallas_call | solution.py:1493
  206.4 4.7 %update.1 = (f32[2,16,1536]{2,1,0:T(8,128)}, f32[2,16,512]{2,1,0:T(8,128)}, f32[2,16,2048]{2,1,0:T(8,128)}, f32[2,64,512]{2,1,0:T(8,128)}, f32[8,512]{1,0:T(8,12...) custom-call(f32[8,128]{1,0:T(8,128)} %get-tuple-element.54.refs_0_, ...), custom_call_target="tpu_custom_call" | custom-call | tf_op jit(solution)/shard_map/update/pallas_call | solution.py:1504

commit v4 on v3

--- a/solution.py
+++ b/solution.py
@@ -404,45 +404,31 @@
     "b": (144, 176, 208),
     "C": (208, 240, 272),
     "D": (272, 304, 336),
-    "d": (336, 384, ROWS),
+    "d": (336, 384, 416),
 }
 SCHEDULE = {
-    "start": "Aa",
-    "packed": "AaBAabCAaBAa",
-    "f0_sent": "Bb",
-    "f0_got": "CDd",
-    "f0_part0": "bB",
-    "f0_part1": "C",
-    "f0_home": "B",
-    "f0_up": "Dbb",
-    "f0_rim": "Cd",
-    "f0_end": "C",
-    "f1_sent": "D",
-    "f1_got": "",
-    "f1_part0": "dD",
-    "f1_home": "",
-    "f1_out": "D",
-    "f1_up": "dd",
-    "b1_ff": "dD",
-    "b1_sent": "D",
-    "b1_part0": "",
-    "b1_sums": "d",
-    "b1_home": "",
-    "b1_end": "C",
-    "b1_rim": "D",
-    "b0_ff": "BbCd",
-    "b0_sent": "D",
-    "b0_part1": "Bd",
-    "b0_part0": "",
-    "b0_sums": "bC",
-    "b0_home": "B",
-    "b0_kv": "a",
-    "b0_end": "A",
-    "tail0": "aA",
-    "tail1": "b",
-    "tail2": "aA",
-    "tail3": "b",
-    "tail4": "aA",
+    "start": "AaBAaA",
+    "packed": "CabABaC",
+    "f0_sent": "bB",
+    "f0_take": "d",
+    "f0_got": "DbC",
+    "f0_part0": "B",
+    "f0_part1": "DbdC",
+    "f0_rim": "D",
+    "f1_sent": "d",
+    "f1_part0": "Dd",
+    "b1_ff": "D",
+    "b1_sent": "dD",
+    "b1_sums": "D",
+    "b1_rim": "dC",
+    "b0_ff": "CBb",
+    "b0_sent": "BD",
+    "b0_part1": "C",
+    "b0_sums": "CBd",
+    "b0_home": "b",
+    "b0_kv": "B",
+    "b0_end": "AAdbaab",
+    "tail": "AaAa",
 }
 
 
@@ -599,7 +585,8 @@
         pl.semaphore_wait(barrier, 31)
     k.gathers = {name: gather_piece(k, name, *rows) for name, rows in PIECES.items()}
     k.reduces = {name: reduce_piece(k, name, *rows) for name, rows in PIECES.items()}
-    k.ready, k.summed = set(), set()
+    k.made, k.summed, k.stored = set(), set(), set()
+    k.flushed, k.sq = [], jnp.zeros((1, 1), F32)
     point(k, "start")
     own[HEAD : HEAD + 16, 0:256] = low(k.head[...])
     own[HEAD : HEAD + 16, 256:512] = jnp.zeros((16, 256), LOW)
@@ -610,9 +597,15 @@
 
 
 def point(k, name):
-    moving = k.gathers if name[0] in "spf" else k.reduces
-    for piece in SCHEDULE[name]:
-        next(moving[piece])
+    coming = name[0] in "spf"
+    for piece in SCHEDULE.get(name, ""):
+        next((k.gathers if coming else k.reduces)[piece], None)
+        if not coming:
+            store_ready(k)
+
+
+def touching(rows):
+    return [name for name, (r0, _, r1) in PIECES.items() if r0 < rows.stop and r1 > rows.start]
 
 
 def pack_layer(k, own, layer):
@@ -695,12 +688,13 @@
         yield
     with scope(f"gw_{name}"):
         waiting.wait()
-    k.ready.update(range(r0, r1, 16))
     yield
 
 
 def need(k, row, count=16):
-    assert k.ready.issuperset(range(row, row + count, 16)), row
+    for name in touching(range(row, row + count)):
+        for _ in k.gathers[name]:
+            pass
 
 
 def block(k, row):
@@ -708,8 +702,9 @@
     return k.pk[:, :, :, :, row : row + 16, :].reshape(512, 512)
 
 
-def put_block(ref, row, value):
-    ref[:, :, :, :, row : row + 16, :] = low(value).reshape(2, 4, 2, 2, 16, 512)
+def put_block(k, row, value):
+    k.made.add(row)
+    k.gr[:, :, :, :, row : row + 16, :] = low(value).reshape(2, 4, 2, 2, 16, 512)
 
 
 def down_block(k, row, c):
@@ -717,8 +712,10 @@
     return k.pk[c // 2, (c % 2) * 2 : (c % 2) * 2 + 2, :, :, row : row + 64, :].reshape(512, 512)
 
 
-def put_down(ref, row, c, value):
-    ref[c // 2, (c % 2) * 2 : (c % 2) * 2 + 2, :, :, row : row + 64, :] = low(value).reshape(2, 2, 2, 64, 512)
+def put_down(k, row, c, value):
+    if c == 3:
+        k.made.update(range(row, row + 64, 16))
+    k.gr[c // 2, (c % 2) * 2 : (c % 2) * 2 + 2, :, :, row : row + 64, :] = low(value).reshape(2, 2, 2, 64, 512)
 
 
 def my_blocks(k):
@@ -771,7 +768,8 @@
 
             @pl.when(k.s // 8 == part)
             def _():
-                for h in range(8):
+                for i in range(8):
+                    h = lax.rem(k.s + i, 8)
                     self.start(self.source.at[h], self.target.at[k.s], self.got[part], (k.side, k.g * 8 + h))
 
     def take(self, part):
@@ -851,7 +849,7 @@
     return low(q * 0.125), blocks, places
 
 
-def attention_forward(k, layer, part, post):
+def attention_forward(k, layer, part, post, between):
     rows, pad = layer_sizes(layer)
     inbox, outbox, lse, keep = k.inbox[layer], k.abox[layer], k.lse[layer], k.att[layer]
 
@@ -871,7 +869,7 @@
             outbox[i, 0 : rows // 2, :] = low(pack_right(out[span]))
             post.send(i, b)
 
-    attend_loop(layer, part, body)
+    attend_loop(layer, part, body, between)
 
 
 def attention_backward(k, layer, part, post, between=None):
@@ -954,6 +952,8 @@
     sent, shared = sem(k), [sem(k), sem(k)]
     mine, others = my_blocks(k), other_blocks(k)
     for part in range(2):
+        if part == 1:
+            point(k, f"f{layer}_take")
         with scope("take"):
             out.take(part)
         for b in mine[4 * part : 4 * part + 4]:
@@ -967,7 +967,7 @@
             with scope("share"):
                 drain(shared[half], inbox.at[pl.ds(0, 4), pl.ds(pad, rows)])
         with scope("attend"):
-            attention_forward(k, layer, part, back)
+            attention_forward(k, layer, part, back, lambda: point(k, f"f0_mid{part}"))
         point(k, f"f{layer}_part{part}")
     with scope("home"):
         back.take()
@@ -1007,10 +1007,10 @@
     second = hold.second[...]
     for c in range(4):
         cols = slice(512 * c, 512 * c + 512)
-        put_down(k.gr, base + DOWN, c, dot_tn(hold.act[:, cols], fall))
+        put_down(k, base + DOWN, c, dot_tn(hold.act[:, cols], fall))
         grad_act = dot_nt(fall, down_block(k, base + DOWN, c))
         grad_pre = low(grad_act * gelu_grad(hold.pre[:, cols]))
-        put_block(k.gr, base + UP + 16 * c, dot_tn(second, grad_pre))
+        put_block(k, base + UP + 16 * c, dot_tn(second, grad_pre))
         grad_second = grad_second + dot_nt(grad_pre, block(k, base + UP + 16 * c))
     if layer == 1:
         point(k, "b1_ff")
@@ -1019,7 +1019,7 @@
     grad_middle = grad_out + grad_mid
     hold.middle[...] = grad_middle
     proj = low(grad_middle)
-    put_block(k.gr, base + OUT, dot_tn(hold.flat[...], proj))
+    put_block(k, base + OUT, dot_tn(hold.flat[...], proj))
     grad_att = dot_nt(proj, block(k, base + OUT))
     gsend = k.gsend[layer]
     for n in range(4):
@@ -1041,7 +1041,12 @@
             for half in range(2) if layer == 1 else [part]:
                 out.take(half)
         with scope("unattend"):
-            attention_backward(k, layer, part, home_q, None if sums is None else sums.send)
+            def between(part=part, sums=sums):
+                if sums is not None:
+                    sums.send()
+                point(k, f"b0_mid{part}")
+
+            attention_backward(k, layer, part, home_q, between)
         sums = KeySums(k, layer, part, home_kv)
         point(k, f"b{layer}_part{part}")
     with scope("sums"):
@@ -1056,6 +1061,8 @@
     grad_normed = jnp.zeros((rows, D), F32)
     for part in range(3):
         if part == 1:
+            if layer == 0:
+                point(k, "b0_q")
             with scope("home_kv"):
                 home_kv.take()
             point(k, f"b{layer}_home")
@@ -1071,7 +1078,7 @@
                 piece = rotate_block(piece, cos_kv, -sin_kv)
             hold.gj[:, 128 * n : 128 * n + 128] = low(piece)
         gj = hold.gj[...]
-        put_block(k.gr, base + QKV + 16 * part, dot_tn(normed, gj))
+        put_block(k, base + QKV + 16 * part, dot_tn(normed, gj))
         grad_normed = grad_normed + dot_nt(gj, block(k, base + QKV + 16 * part))
     if layer == 0:
         point(k, "b0_kv")
@@ -1159,6 +1166,7 @@
     k.loss = jnp.sum((log_total - picked) / length, axis=0, keepdims=True)
     grad_logits = low((jnp.exp(logits - log_total) - hot) / length)
     k.gr[:, :, :, :, HEAD : HEAD + 16, 0:256] = low(dot_tn(final, grad_logits)).reshape(2, 4, 2, 2, 16, 256)
+    k.made.add(HEAD)
     k.gr[:, :, :, :, HEAD : HEAD + 16, 256:512] = jnp.zeros((2, 4, 2, 2, 16, 256), LOW)
     grad_final = dot_nt(grad_logits, head)
     grad_up, k.gain_grads[4] = norm_back(upsampled, gain, grad_final)
@@ -1203,6 +1211,7 @@
     )
     gains = jnp.broadcast_to(low(gains)[None], (32, 16, 256))
     k.gr[:, :, :, :, EG : EG + 16, 256:512] = gains.reshape(2, 4, 2, 2, 16, 256)
+    k.made.add(EG)
     point(k, "b0_end")
 
 
@@ -1213,6 +1222,7 @@
 def reduce_piece(k, name, r0, rm, r1):
     g, z, y, x, dev, gr = k.g, k.z, k.y, k.x, k.dev, k.gr
     a, b, every = pl.ds(r0, rm - r0), pl.ds(rm, r1 - rm), pl.ds(r0, r1 - r0)
+    assert k.made.issuperset(range(r0, r1, 16)), name
     waiting = Stage(
         k, k.rc.at[:, :, :, every], [(gr.at[1 - g, :, :, :, every], k.rc.at[:, :, :, every], dev(1 - g, z, y, x))]
     )
@@ -1273,7 +1283,6 @@
 
 
 def own_sum(k, row, count):
-    assert k.summed.issuperset(range(row, row + count, 16))
     rows = pl.ds(row, count)
     v = k.gr[k.g, k.z, k.y, k.x, rows].astype(F32)
     for i in range(3):
@@ -1315,15 +1324,18 @@
     flush(k, "out", layer)
 
 
-def store_ff(k, layer):
+def store_up(k, layer):
     v = own_sum(k, LAYER0 + layer * LAYER_ROWS + UP, 64)
     square(k, v)
     for j in range(4):
         k.s_up[layer, :, 512 * j : 512 * j + 512] = v[16 * j : 16 * j + 16]
+    flush(k, "up", layer)
+
+
+def store_down(k, layer):
     v = own_sum(k, LAYER0 + layer * LAYER_ROWS + DOWN, 64)
     square(k, v)
     k.s_down[layer] = v
-    flush(k, "up", layer)
     flush(k, "down", layer)
 
 
@@ -1348,35 +1360,27 @@
     flush(k, "gains")
 
 
+def store_ready(k):
+    stores = [(range(EG, EG + 16), store_rest, ()), (range(HEAD, HEAD + 16), store_head, ())]
+    for layer in range(2):
+        base = LAYER0 + layer * LAYER_ROWS
+        stores.append((range(base + QKV, base + QKV + 48), store_qkv, (layer,)))
+        stores.append((range(base + OUT, base + OUT + 16), store_out, (layer,)))
+        stores.append((range(base + UP, base + UP + 64), store_up, (layer,)))
+        stores.append((range(base + DOWN, base + DOWN + 64), store_down, (layer,)))
+    for rows, store, args in stores:
+        if rows.start not in k.stored and k.summed.issuperset(range(rows.start, rows.stop, 16)):
+            k.stored.add(rows.start)
+            store(k, *args)
+
+
 def finish_grads(k):
     g = k.g
-    k.sq = jnp.zeros((1, 1), F32)
-    k.flushed = []
-
-    def complete(name):
+    point(k, "tail")
+    for name in PIECES:
         for _ in k.reduces[name]:
-            pass
-
-    point(k, "tail0")
-    complete("D")
-    complete("d")
-    store_ff(k, 1)
-    store_head(k)
-    point(k, "tail1")
-    complete("C")
-    store_qkv(k, 1)
-    store_out(k, 1)
-    point(k, "tail2")
-    complete("B")
-    store_out(k, 0)
-    point(k, "tail3")
-    complete("b")
-    store_ff(k, 0)
-    point(k, "tail4")
-    complete("A")
-    store_rest(k)
-    complete("a")
-    store_qkv(k, 0)
+            store_ready(k)
+    store_ready(k)
     lane = lanes((8, 128))
     k.stat[0] = jnp.where(lane == 0, k.sq, jnp.where(lane == 1, k.loss, 0.0))
     me = g * 16 + k.s
@@ -1398,7 +1402,7 @@
     "ids", "targets", "lengths", "w_qkv", "w_out", "w_up", "w_down", "embed", "head", "gains",
 )
 OUT_NAMES = ("g_qkv", "g_out", "g_up", "g_down", "g_embed", "g_head", "g_gains", "stats")
-SEMS = 200
+SEMS = 168
 
 
 def scratch_shapes():

time: 212 us -> 187 us (0.88)
  Pallas kernels: 210 us -> 186 us
    pallas_call x1, Pallas kernels: 206 us -> 181 us  [on_device_fast(): pl.pallas_call(kernel, name='step', out_shape=shard_shapes + [jax.ShapeDt...]
where the time goes in v4:
time: 187 us; the launch traced here: 186 us
  Pallas kernels  186 us (99%)
    pallas_call x1, Pallas kernels, on_device_fast(): pl.pallas_call(kernel, name='step', out_shape=shard_shapes + [jax.ShapeDt...  181 us
    pallas_call x1, Pallas kernels, on_device_fast(): pl.pallas_call(update_kernel, name='update', out_shape=shard_shapes * 3 +...  4.71 us

profile of v4, /device:TPU:0, one launch (start us, length us, event | category | flops | bytes accessed | tf_op | source)
XLA Modules:
  0.0 186.5 jit_solution(13984345265058160645)
XLA Ops:
  0.7 180.9 %step.1 = (f32[2,16,1536]{2,1,0:T(8,128)}, f32[2,16,512]{2,1,0:T(8,128)}, f32[2,16,2048]{2,1,0:T(8,128)}, f32[2,64,512]{2,1,0:T(8,128)}, f32[8,512]{1,0:T(8,128)...) custom-call(s32[1,144]{1,0:T(1,128)} %refs_0_.1, s32[1,144]{1,0:T(1,128)} %refs_1_.1, s32[1,8]{1,0:T(1,128)} %refs_2_.1, ...), custom_call_target="tpu_custom_call" | custom-call | tf_op jit(solution)/shard_map/step/pallas_call | solution.py:1497
  181.6 4.7 %update.1 = (f32[2,16,1536]{2,1,0:T(8,128)}, f32[2,16,512]{2,1,0:T(8,128)}, f32[2,16,2048]{2,1,0:T(8,128)}, f32[2,64,512]{2,1,0:T(8,128)}, f32[8,512]{1,0:T(8,12...) custom-call(f32[8,128]{1,0:T(8,128)} %get-tuple-element.54.refs_0_, ...), custom_call_target="tpu_custom_call" | custom-call | tf_op jit(solution)/shard_map/update/pallas_call | solution.py:1508

commit v5 on v4

--- a/solution.py
+++ b/solution.py
@@ -393,42 +393,47 @@
 MESH = pl.DeviceIdType.MESH
 D = 512
 
-EG, LAYER0, LAYER_ROWS = 0, 16, 192
+EG, LAYER0, LAYER_ROWS = 0, -32, 192
 QKV, OUT, UP, DOWN = 0, 48, 64, 128
 HEAD = LAYER0 + 2 * LAYER_ROWS
 ROWS = HEAD + 16
 PIECES = {
-    "A": (0, 16, 32),
-    "a": (32, 48, 64),
-    "B": (64, 96, 144),
-    "b": (144, 176, 208),
-    "C": (208, 240, 272),
-    "D": (272, 304, 336),
-    "d": (336, 384, 416),
+    "A": (0, 16, 16),
+    "B": (16, 32, 64),
+    "E": (64, 80, 96),
+    "b": (96, 128, 160),
+    "C": (160, 192, 224),
+    "D": (224, 256, 288),
+    "d": (288, 320, 336),
+    "h": (336, 352, 368),
 }
+Z_LAST, Z_FIRST = "h", "h"
 SCHEDULE = {
-    "start": "AaBAaA",
-    "packed": "CabABaC",
-    "f0_sent": "bB",
-    "f0_take": "d",
-    "f0_got": "DbC",
-    "f0_part0": "B",
-    "f0_part1": "DbdC",
-    "f0_rim": "D",
-    "f1_sent": "d",
-    "f1_part0": "Dd",
-    "b1_ff": "D",
+    "start": "BAbhBEAh",
+    "heads": "dBAEbBCE",
+    "f0_heads": "DAb",
+    "f0_mid0": "C",
+    "f0_part0": "dE",
+    "f0_part1": "Cbh",
+    "f0_home": "D",
+    "f0_rim": "dC",
+    "f1_sent": "D",
+    "f1_got": "dh",
+    "f1_part0": "D",
+    "b1_ff": "d",
     "b1_sent": "dD",
-    "b1_sums": "D",
-    "b1_rim": "dC",
-    "b0_ff": "CBb",
-    "b0_sent": "BD",
-    "b0_part1": "C",
-    "b0_sums": "CBd",
-    "b0_home": "b",
-    "b0_kv": "B",
-    "b0_end": "AAdbaab",
-    "tail": "AaAa",
+    "b1_sums": "hDhd",
+    "b1_rim": "CDC",
+    "b0_ff": "BDB",
+    "b0_sent": "bCEd",
+    "b0_mid1": "E",
+    "b0_part1": "B",
+    "b0_keys1": "b",
+    "b0_mid0": "C",
+    "b0_part0": "h",
+    "b0_keys0": "B",
+    "b0_end": "E",
+    "tail": "AbAEbh",
 }
 
 
@@ -546,12 +551,12 @@
         setattr(k, name, ref)
     k.sems = refs[-1]
     for name in PER_LAYER:
-        setattr(k, name, [getattr(k, name + "0"), getattr(k, name + "1")])
+        setattr(k, name, [getattr(k, name + "0", None), getattr(k, name + "1")])
     k.hold = []
     for layer in range(2):
         hold = Bag()
         for name in HELD:
-            setattr(hold, name, getattr(k, "h_" + name + str(layer)))
+            setattr(hold, name, getattr(k, "h_" + name + str(layer), None))
         k.hold.append(hold)
     g = lax.axis_index("dp")
     s = lax.axis_index("seq")
@@ -580,7 +585,13 @@
     gains = jnp.concatenate([gains, jnp.zeros((3, 256), F32)], axis=0)
     gains = jnp.concatenate([jnp.where(g == 0, gains, 0.0), jnp.where(g == 1, gains, 0.0)], axis=0)
     own[EG : EG + 16, 256:512] = low(gains)
+    k.columns[0:1, 0:144] = k.ids[...].astype(F32)
+    k.columns[1:2, 0:144] = k.targets[...].astype(F32)
+    pack_heads(k)
     pack_layer(k, own, 0)
+    pack_layer(k, own, 1)
+    own[HEAD : HEAD + 16, 0:256] = low(k.head[...])
+    own[HEAD : HEAD + 16, 256:512] = jnp.zeros((16, 256), LOW)
     with scope("barrier"):
         pl.semaphore_wait(barrier, 31)
     k.gathers = {name: gather_piece(k, name, *rows) for name, rows in PIECES.items()}
@@ -588,16 +599,14 @@
     k.made, k.summed, k.stored = set(), set(), set()
     k.flushed, k.sq = [], jnp.zeros((1, 1), F32)
     point(k, "start")
-    own[HEAD : HEAD + 16, 0:256] = low(k.head[...])
-    own[HEAD : HEAD + 16, 256:512] = jnp.zeros((16, 256), LOW)
-    pack_layer(k, own, 1)
-    point(k, "packed")
+    spread_heads(k)
+    point(k, "heads")
     forward_backward(k)
     finish_grads(k)
 
 
 def point(k, name):
-    coming = name[0] in "spf"
+    coming = name[0] in "sphf"
     for piece in SCHEDULE.get(name, ""):
         next((k.gathers if coming else k.reduces)[piece], None)
         if not coming:
@@ -608,17 +617,104 @@
     return [name for name, (r0, _, r1) in PIECES.items() if r0 < rows.stop and r1 > rows.start]
 
 
+def pair_kv(keys, vals):
+    left = lanes(keys.shape) < 64
+    return jnp.where(left, keys, roll64(vals)), jnp.where(left, roll64(keys), vals)
+
+
+def pack_heads(k):
+    row, lane = lax.broadcasted_iota(jnp.int32, (16, 128), 0), lanes((16, 128))
+    ids = jnp.zeros((16, 128), F32)
+    for j in range(3):
+        part = pltpu.roll(k.columns[0:8, :], (64 - 48 * j) % 256, 1)[0:1, 0:128]
+        ids = jnp.where((row == j) & (lane >= 64) & (lane < 112), part, ids)
+    for pair in range(4):
+        query = k.w_qkv[0, :, 128 * pair : 128 * pair + 128]
+        keys = k.w_qkv[0, :, 512 + 128 * pair : 640 + 128 * pair]
+        vals = k.w_qkv[0, :, 1024 + 128 * pair : 1152 + 128 * pair]
+        for odd, kv in enumerate(pair_kv(keys, vals)):
+            k.headout[2 * pair + odd, :, 0:128] = low(jnp.where(lane < 64, roll64(query) if odd else query, ids))
+            k.headout[2 * pair + odd, :, 128:256] = low(kv)
+
+
+def around(k, source, target, sent, got):
+    for n in range(1, 16):
+        c = lax.rem(k.s + n, 16)
+        remote(source(c), target(k.s), sent, got, (k.g, c)).start()
+
+
+def spread_heads(k):
+    mine = k.g * 16 + k.s
+    k.wbox[mine] = k.headout[lax.rem(k.s, 8)]
+    k.head_sems = [sem(k), sem(k)]
+    around(k, lambda c: k.headout.at[lax.rem(c, 8)], lambda c: k.wbox.at[k.g * 16 + c], *k.head_sems)
+
+
+def take_heads(k):
+    with scope("heads"):
+        for semaphore in k.head_sems:
+            drain(semaphore, k.wbox.at[pl.ds(0, 15)])
+    share = k.wbox.at[pl.ds(16 * k.g, 16)]
+    return Stage(k, share, [(share, share, k.dev(1 - k.g, k.z, k.y, k.x))])
+
+
+def block_tables(k, b):
+    cos_b, sin_b = k.cosb[pl.ds(b, 1), :], k.sinb[pl.ds(b, 1), :]
+    cos_r, sin_r = k.cos[0][...], k.sin[0][...]
+    return cos_b * cos_r - sin_b * sin_r, sin_b * cos_r + cos_b * sin_r
+
+
+def kv_tables(cosine, sine):
+    left = lanes(cosine.shape) < 64
+    return jnp.where(left, cosine, 1.0), jnp.where(left, sine, 0.0)
+
+
+def byte_rows(k):
+    need(k, EG)
+    packed = k.pk[:, :, :, :, EG : EG + 16, :].astype(F32).reshape(32, 16, 512)
+    gains = jnp.sum(packed[:, :, 256:512], axis=0)
+    k.gain[:, 0:256] = gains[0:8]
+    k.gain[:, 256:512] = gains[8:16]
+    table = jnp.concatenate(
+        [packed[:, 0:8, 0:256].reshape(256, 256), packed[:, 8:16, 0:256].reshape(256, 256)], axis=1
+    )
+    k.table[...] = table
+    unit, _ = norm_parts(table)
+    k.normed[...] = low(unit * k.gain[0:1, :])
+
+
+def head_rows(k):
+    group = k.s // 8
+    for b in range(16):
+        k.columns[16 + 4 * b : 20 + 4 * b, 0:128] = k.wbox[group * 16 + b].astype(F32)[0:4, 0:128]
+    columns = k.columns[...].T
+    weights = k.wbox[...].astype(F32).reshape(512, 256)
+    lane = lanes(weights.shape)
+    k.wh[...] = low(jnp.where((lane >= 64) & (lane < 128), 0.0, weights))
+    joined = dot(k.normed[...], k.wh[...])
+    high = low(joined)
+    rest = low(joined - high.astype(F32))
+    for b in range(16):
+        ids = [columns[64:112, 16 + 4 * b + j : 17 + 4 * b + j] for j in range(3)]
+        hot = byte_matrix(jnp.concatenate(ids, axis=0).astype(jnp.int32))
+        k.hot[b] = hot
+        rows = dot(hot, high) + dot(hot, rest)
+        cosine, sine = block_tables(k, b)
+        k.q0[b] = low(rotate_block(rows[:, 0:128], cosine, sine) * 0.125)
+        k.kv0[b] = low(rotate_block(rows[:, 128:256], *kv_tables(cosine, sine)))
+
+
 def pack_layer(k, own, layer):
     base = LAYER0 + layer * LAYER_ROWS
-    own[base + QKV : base + QKV + 16, :] = low(k.w_qkv[layer, :, 0:512])
-    for pair in range(4):
-        keys = k.w_qkv[layer, :, 512 + 128 * pair : 640 + 128 * pair]
-        vals = k.w_qkv[layer, :, 1024 + 128 * pair : 1152 + 128 * pair]
-        left = lanes(keys.shape) < 64
-        row = base + QKV + 16 + 16 * (pair // 2)
-        col = 256 * (pair % 2)
-        own[row : row + 16, col : col + 128] = low(jnp.where(left, keys, roll64(vals)))
-        own[row : row + 16, col + 128 : col + 256] = low(jnp.where(left, roll64(keys), vals))
+    if layer == 1:
+        own[base + QKV : base + QKV + 16, :] = low(k.w_qkv[layer, :, 0:512])
+        for pair in range(4):
+            keys = k.w_qkv[layer, :, 512 + 128 * pair : 640 + 128 * pair]
+            vals = k.w_qkv[layer, :, 1024 + 128 * pair : 1152 + 128 * pair]
+            row = base + QKV + 16 + 16 * (pair // 2)
+            for odd, kv in enumerate(pair_kv(keys, vals)):
+                col = 256 * (pair % 2) + 128 * odd
+                own[row : row + 16, col : col + 128] = low(kv)
     own[base + OUT : base + OUT + 16, :] = low(k.w_out[layer])
     for j in range(4):
         own[base + UP + 16 * j : base + UP + 16 * j + 16, :] = low(k.w_up[layer, :, 512 * j : 512 * j + 512])
@@ -646,9 +742,9 @@
 
 
 class Stage:
-    def __init__(self, k, total, moves):
-        self.total, self.sent, self.got = total, sem(k), sem(k)
-        start_all([remote(src, dst, self.sent, self.got, device) for src, dst, device in moves])
+    def __init__(self, k, total, moves, sent=None):
+        self.total, self.sent, self.got = total, sem(k) if sent is None else sent, sem(k)
+        start_all([remote(src, dst, self.sent, self.got, device) for src, dst, device in moves if src.shape[-2]])
 
     def wait(self):
         drain(self.got, self.total)
@@ -659,35 +755,46 @@
     g, z, y, x, dev, pk = k.g, k.z, k.y, k.x, k.dev, k.pk
     a, b, every = pl.ds(r0, rm - r0), pl.ds(rm, r1 - rm), pl.ds(r0, r1 - r0)
 
+    sent = sem(k)
+
     def stage(total, *moves):
-        return Stage(k, total, [(ref, ref, device) for ref, device in moves])
-
-    stages = (
-        lambda: stage(
-            pk.at[g, pl.ds(0, 3), y, x, every],
-            *[(pk.at[g, z, y, x, every], dev(g, lax.rem(z + n, 4), y, x)) for n in (2, 1, 3)],
-        ),
-        lambda: stage(
-            pk.at[g, :, y, x, every],
-            (pk.at[g, :, y, x, a], dev(g, z, 1 - y, x)),
-            (pk.at[g, :, y, x, b], dev(g, z, y, 1 - x)),
-        ),
-        lambda: stage(
-            pk.at[g, :, :, x, every],
-            (pk.at[g, :, :, x, a], dev(g, z, y, 1 - x)),
-            (pk.at[g, :, y, :, b], dev(g, z, 1 - y, x)),
-        ),
-        lambda: stage(pk.at[1 - g, :, :, :, every], (pk.at[g, :, :, :, every], dev(1 - g, z, y, x))),
-    )
-    waiting = None
-    for begin in stages:
-        if waiting is not None:
-            with scope(f"gw_{name}"):
-                waiting.wait()
-        waiting = begin()
+        return Stage(k, total, [(ref, ref, device) for ref, device in moves], sent)
+
+    def wait(waiting):
+        with scope(f"gw_{name}"):
+            waiting.wait()
+
+    planes = pl.ds(z, 1) if name in Z_LAST else pl.ds(0, 4)
+
+    def across():
+        waiting = stage(
+            pk.at[g, planes, y, x, every],
+            (pk.at[g, planes, y, x, a], dev(g, z, 1 - y, x)),
+            (pk.at[g, planes, y, x, b], dev(g, z, y, 1 - x)),
+        )
         yield
-    with scope(f"gw_{name}"):
-        waiting.wait()
+        wait(waiting)
+        waiting = stage(
+            pk.at[g, planes, :, x, every],
+            (pk.at[g, planes, :, x, a], dev(g, z, y, 1 - x)),
+            (pk.at[g, planes, y, :, b], dev(g, z, 1 - y, x)),
+        )
+        yield
+        wait(waiting)
+
+    def along():
+        def part(n):
+            return pk.at[g, n, :, :, every] if name in Z_LAST else pk.at[g, n, y, x, every]
+
+        waiting = stage(part(pl.ds(0, 3)), *[(part(z), dev(g, lax.rem(z + n, 4), y, x)) for n in (2, 1, 3)])
+        yield
+        wait(waiting)
+
+    for way in (across, along) if name in Z_LAST else (along, across):
+        yield from way()
+    waiting = stage(pk.at[1 - g, :, :, :, every], (pk.at[g, :, :, :, every], dev(1 - g, z, y, x)))
+    yield
+    wait(waiting)
     yield
 
 
@@ -802,16 +909,21 @@
     return v * cosine + swap32(v) * sine
 
 
-def rotary_tables(k, layer):
-    rows, _ = layer_sizes(layer)
+def rotary_tables(k):
     lane = lanes((1, 128))
     freqs = jnp.zeros((1, 128), F32)
     for i in range(32):
         freqs = jnp.where(lane % 32 == i, 10000.0 ** (-i / 32), freqs)
-    position = k.s * rows + lax.broadcasted_iota(jnp.int32, (rows, 1), 0)
-    angles = position.astype(F32) * freqs
-    k.cos[layer][...] = jnp.cos(angles)
-    k.sin[layer][...] = jnp.sin(angles) * jnp.where(lane % 64 < 32, -1.0, 1.0)
+    sign = jnp.where(lane % 64 < 32, -1.0, 1.0)
+    rows, short = layer_sizes(0)[0], layer_sizes(1)[0]
+    for cos, sin, count, first, step in (
+        (k.cos[0], k.sin[0], rows, 0, 1),
+        (k.cosb, k.sinb, 16, 0, rows),
+        (k.cos[1], k.sin[1], short, k.s * short, 1),
+    ):
+        angles = (first + step * lax.broadcasted_iota(jnp.int32, (count, 1), 0)).astype(F32) * freqs
+        cos[...] = jnp.cos(angles)
+        sin[...] = jnp.sin(angles) * sign
 
 
 def layer_sizes(layer):
@@ -826,7 +938,7 @@
     for first in (0, 2):
         @pl.loop(first, first + 2)
         def _(n):
-            body([part * 4 + n], 8 * (part + 1))
+            body([part * 4 + n], 8 * part + 4 + 2 * first)
 
         if between is not None and first == 0:
             between()
@@ -836,27 +948,39 @@
     return pieces[0] if len(pieces) == 1 else jnp.concatenate(pieces, axis=0)
 
 
-def masked_scores(q, kv, places):
+def masked_scores(q, kv, places, plain):
     scores = dot_nt(q, kv)
-    return jnp.where(lanes(scores.shape) <= places, scores, MASK_FILL)
+    plain = plain // 128 * 128
+    rest = scores[:, plain:]
+    rest = jnp.where(lanes(rest.shape) + plain <= places, rest, MASK_FILL)
+    return jnp.concatenate([scores[:, :plain], rest], axis=1) if plain else rest
 
 
 def stacked_queries(k, layer, items):
     rows, pad = layer_sizes(layer)
     blocks = [my_block(k, i) for i in items]
+    places = stack([b * rows + lax.broadcasted_iota(jnp.int32, (rows, 1), 0) for b in blocks])
+    if layer == 0:
+        return stack([k.q0[b] for b in blocks]), blocks, places
     q = stack([unpack_left(k.inbox[layer][b, 0:pad, :].astype(F32)[: rows // 2]) for b in blocks])
-    places = stack([b * rows + lax.broadcasted_iota(jnp.int32, (rows, 1), 0) for b in blocks])
     return low(q * 0.125), blocks, places
+
+
+def stacked_keys(k, layer, count):
+    rows, pad = layer_sizes(layer)
+    if layer == 0:
+        return k.kv0[0:count].reshape(count * rows, 128)
+    return k.inbox[layer][0:count, pad : pad + rows, :].reshape(count * rows, 128)
 
 
 def attention_forward(k, layer, part, post, between):
     rows, pad = layer_sizes(layer)
-    inbox, outbox, lse, keep = k.inbox[layer], k.abox[layer], k.lse[layer], k.att[layer]
+    outbox, lse, keep = k.abox[layer], k.lse[layer], k.att[layer]
 
     def body(items, count):
         q, blocks, places = stacked_queries(k, layer, items)
-        kv = inbox[0:count, pad : pad + rows, :].reshape(count * rows, 128)
-        scores = masked_scores(q, kv, places)
+        kv = stacked_keys(k, layer, count)
+        scores = masked_scores(q, kv, places, 0 if layer == 1 else (count - 4) * rows)
         top = jnp.max(scores, axis=-1, keepdims=True)
         prob = jnp.exp(scores - top)
         total = jnp.sum(prob, axis=-1, keepdims=True)
@@ -874,20 +998,24 @@
 
 def attention_backward(k, layer, part, post, between=None):
     rows, pad = layer_sizes(layer)
-    inbox, gradbox, lse, keep = k.inbox[layer], k.gbox[layer], k.lse[layer], k.att[layer]
+    gradbox, lse, keep = k.gbox[layer], k.lse[layer], k.att[layer]
     dkvt, outbox = k.dkvt[layer], k.dbox[layer]
 
     def body(items, count):
         q, blocks, places = stacked_queries(k, layer, items)
-        kv = inbox[0:count, pad : pad + rows, :].reshape(count * rows, 128)
+        kv = stacked_keys(k, layer, count)
         grad = stack([unpack_right(gradbox[b].astype(F32)[: rows // 2]) for b in blocks])
         delta = jnp.sum(grad * stack([keep[i] for i in items]), axis=-1, keepdims=True)
         grad = low(grad)
-        prob = jnp.exp(masked_scores(q, kv, places) - stack([lse[i] for i in items])[:, 0:1])
+        prob = jnp.exp(masked_scores(q, kv, places, 0 if layer == 1 else (count - 4) * rows) - stack([lse[i] for i in items])[:, 0:1])
         grad_prob = dot_nt(grad, kv)
         ds = low(prob * (grad_prob - delta))
         dq = dot(ds, kv) * 0.125
-        for n, (i, b) in enumerate(zip(items, blocks)):
+        if layer == 0:
+            cosine, sine = block_tables(k, blocks[0])
+            dq = rotate_block(jnp.where(lanes(dq.shape) < 64, dq, 0.0), cosine, -sine)
+            k.gbytes[:, 0:128] += dot_tn(k.hot[blocks[0]], low(dq))
+        for n, (i, b) in enumerate(zip(items, blocks) if layer == 1 else ()):
             outbox[i, 0 : rows // 2, :] = low(pack_left(dq[n * rows : (n + 1) * rows]))
             post.send(i, b)
         dkvt[:, 0 : count * rows] += dot_tn(q, ds) + dot_tn(grad, low(prob))
@@ -923,17 +1051,15 @@
             self.post.send(i, mine[i])
 
 
-def layer_ahead(k, layer, hidden):
+def send_rows(k, hidden):
+    layer = 1
     rows, pad = layer_sizes(layer)
     base = LAYER0 + layer * LAYER_ROWS
-    hold = k.hold[layer]
-    hold.hidden[...] = hidden
     unit, _ = norm_parts(hidden)
     normed = low(unit * k.gain[2 * layer : 2 * layer + 1, :])
-    hold.normed[...] = normed
+    k.hold[layer].normed[...] = normed
     cosine, sine = k.cos[layer][...], k.sin[layer][...]
-    left = lanes(cosine.shape) < 64
-    cos_kv, sin_kv = jnp.where(left, cosine, 1.0), jnp.where(left, sine, 0.0)
+    cos_kv, sin_kv = kv_tables(cosine, sine)
     sendbox = k.sendbox[layer]
     for part in range(3):
         joined = dot(normed, block(k, base + QKV + 16 * part))
@@ -948,24 +1074,38 @@
     inbox = k.inbox[layer]
     out = ToHeads(k, sendbox, inbox)
     out.send()
-    point(k, f"f{layer}_sent")
+    point(k, "f1_sent")
     sent, shared = sem(k), [sem(k), sem(k)]
-    mine, others = my_blocks(k), other_blocks(k)
+    mine = my_blocks(k)
     for part in range(2):
         if part == 1:
-            point(k, f"f{layer}_take")
+            point(k, "f1_take")
         with scope("take"):
             out.take(part)
         for b in mine[4 * part : 4 * part + 4]:
             ref = inbox.at[b, pl.ds(pad, rows)]
             remote(ref, ref, sent, shared[part], k.dev(1 - k.g, k.z, k.y, k.x)).start()
-    point(k, f"f{layer}_got")
+    point(k, "f1_got")
+    k.pending += [out.done, lambda: drain(sent, inbox.at[pl.ds(0, 8), pl.ds(pad, rows)])]
+    return shared
+
+
+def layer_ahead(k, layer, hidden):
+    rows, pad = layer_sizes(layer)
+    base = LAYER0 + layer * LAYER_ROWS
+    hold = k.hold[layer]
     home = k.home[layer]
+    if layer == 0:
+        point(k, "f0_got")
+        shared = []
+    else:
+        hold.hidden[...] = hidden
+        shared = send_rows(k, hidden)
     back = FromHeads(k, k.abox[layer], home)
     for part in range(2 - layer):
-        for half in range(2) if layer == 1 else [part]:
+        for semaphore in shared:
             with scope("share"):
-                drain(shared[half], inbox.at[pl.ds(0, 4), pl.ds(pad, rows)])
+                drain(semaphore, k.inbox[layer].at[pl.ds(0, 4), pl.ds(pad, rows)])
         with scope("attend"):
             attention_forward(k, layer, part, back, lambda: point(k, f"f0_mid{part}"))
         point(k, f"f{layer}_part{part}")
@@ -988,13 +1128,14 @@
         pre = dot(second, block(k, base + UP + 16 * j))
         hold.pre[:, 512 * j : 512 * j + 512] = pre
         hold.act[:, 512 * j : 512 * j + 512] = low(gelu(pre))
-    output = middle
     point(k, f"f{layer}_up")
-    for c in range(4):
-        output = output + dot(hold.act[:, 512 * c : 512 * c + 512], down_block(k, base + DOWN, c))
-    out.done()
+    need(k, base + DOWN, 64)
+    falls = k.pk[:, :, :, :, base + DOWN : base + DOWN + 64, :].reshape(2048, 512)
+    output = hold.middle[...] + dot(hold.act[...], falls)
     back.done()
-    drain(sent, inbox.at[pl.ds(0, 8), pl.ds(pad, rows)])
+    for done in k.pending:
+        done()
+    k.pending = []
     return output
 
 
@@ -1007,10 +1148,14 @@
     second = hold.second[...]
     for c in range(4):
         cols = slice(512 * c, 512 * c + 512)
-        put_down(k, base + DOWN, c, dot_tn(hold.act[:, cols], fall))
+        if layer == 1:
+            put_down(k, base + DOWN, c, dot_tn(hold.act[:, cols], fall))
         grad_act = dot_nt(fall, down_block(k, base + DOWN, c))
         grad_pre = low(grad_act * gelu_grad(hold.pre[:, cols]))
-        put_block(k, base + UP + 16 * c, dot_tn(second, grad_pre))
+        if layer == 1:
+            put_block(k, base + UP + 16 * c, dot_tn(second, grad_pre))
+        else:
+            hold.gpre[:, cols] = grad_pre
         grad_second = grad_second + dot_nt(grad_pre, block(k, base + UP + 16 * c))
     if layer == 1:
         point(k, "b1_ff")
@@ -1019,7 +1164,8 @@
     grad_middle = grad_out + grad_mid
     hold.middle[...] = grad_middle
     proj = low(grad_middle)
-    put_block(k, base + OUT, dot_tn(hold.flat[...], proj))
+    if layer == 1:
+        put_block(k, base + OUT, dot_tn(hold.flat[...], proj))
     grad_att = dot_nt(proj, block(k, base + OUT))
     gsend = k.gsend[layer]
     for n in range(4):
@@ -1029,43 +1175,38 @@
     out = ToHeads(k, gsend, k.gbox[layer])
     out.send()
     if layer == 0:
+        put_block(k, base + OUT, dot_tn(hold.flat[...], proj))
+        for c in range(4):
+            cols = slice(512 * c, 512 * c + 512)
+            put_down(k, base + DOWN, c, dot_tn(hold.act[:, cols], fall))
+            put_block(k, base + UP + 16 * c, dot_tn(second, hold.gpre[:, cols]))
         point(k, "b0_ff")
+    k.dkvt[layer][...] = jnp.zeros_like(k.dkvt[layer])
+    point(k, f"b{layer}_sent")
+    if layer == 0:
+        return head_grads(k, out)
     back = k.back[layer]
     home_q = FromHeads(k, k.dbox[layer], back)
     home_kv = FromHeads(k, k.kvbox[layer], k.kvback[layer])
-    k.dkvt[layer][...] = jnp.zeros_like(k.dkvt[layer])
-    point(k, f"b{layer}_sent")
-    sums = None
-    for part in reversed(range(2 - layer)):
-        with scope("take"):
-            for half in range(2) if layer == 1 else [part]:
-                out.take(half)
-        with scope("unattend"):
-            def between(part=part, sums=sums):
-                if sums is not None:
-                    sums.send()
-                point(k, f"b0_mid{part}")
-
-            attention_backward(k, layer, part, home_q, between)
-        sums = KeySums(k, layer, part, home_kv)
-        point(k, f"b{layer}_part{part}")
+    with scope("take"):
+        out.take(0)
+        out.take(1)
+    with scope("unattend"):
+        attention_backward(k, layer, 0, home_q)
+    sums = KeySums(k, layer, 0, home_kv)
+    point(k, "b1_part0")
     with scope("sums"):
         sums.send()
-    point(k, f"b{layer}_sums")
+    point(k, "b1_sums")
     with scope("home_q"):
         home_q.take()
     cosine, sine = k.cos[layer][...], k.sin[layer][...]
-    left = lanes(cosine.shape) < 64
-    cos_kv, sin_kv = jnp.where(left, cosine, 1.0), jnp.where(left, sine, 0.0)
-    normed = hold.normed[...]
-    grad_normed = jnp.zeros((rows, D), F32)
+    cos_kv, sin_kv = kv_tables(cosine, sine)
     for part in range(3):
         if part == 1:
-            if layer == 0:
-                point(k, "b0_q")
             with scope("home_kv"):
                 home_kv.take()
-            point(k, f"b{layer}_home")
+            point(k, "b1_home")
         for n in range(4):
             if part == 0:
                 piece = unpack_pair(
@@ -1076,42 +1217,95 @@
             else:
                 piece = k.kvback[layer][4 * part - 4 + n].astype(F32)
                 piece = rotate_block(piece, cos_kv, -sin_kv)
-            hold.gj[:, 128 * n : 128 * n + 128] = low(piece)
-        gj = hold.gj[...]
-        put_block(k, base + QKV + 16 * part, dot_tn(normed, gj))
+            hold.gj[:, 512 * part + 128 * n : 512 * part + 128 * n + 128] = low(piece)
+    grad_normed = jnp.zeros((rows, D), F32)
+    for part in range(3):
+        gj = hold.gj[:, 512 * part : 512 * part + 512]
         grad_normed = grad_normed + dot_nt(gj, block(k, base + QKV + 16 * part))
-    if layer == 0:
-        point(k, "b0_kv")
     gain = k.gain[2 * layer : 2 * layer + 1, :]
     grad_in, k.gain_grads[2 * layer] = norm_back(hold.hidden[...], gain, grad_normed)
-    out.done()
-    home_q.done()
-    home_kv.done()
-    if layer == 1:
-        point(k, "b1_end")
-    return hold.middle[...] + grad_in
-
-
-def byte_matrix(ids, half):
-    n = lanes((ids.shape[0], 512))
-    return low(jnp.where((n // 16 * 8 + n % 8 == ids) & (n // 8 % 2 == half), 1.0, 0.0))
+    return hold.middle[...] + grad_in, (out, home_q, home_kv)
+
+
+def head_grads(k, out):
+    own = dot_tn(byte_matrix(k.own_ids), low(k.hold[0].middle[...]))
+    k.tgrad[...] = own
+    k.gbytes[...] = jnp.zeros_like(k.gbytes)
+    for part in (1, 0):
+        with scope("take"):
+            out.take(part)
+        with scope("unattend"):
+            attention_backward(k, 0, part, None, lambda: point(k, f"b0_mid{part}"))
+        point(k, f"b0_part{part}")
+        with scope("keysums"):
+            sums = k.dkvt[0][:, 1152 * part : 1152 * part + 1152].T
+            for i in range(8):
+                cosine, sine = kv_tables(*block_tables(k, 8 * part + i))
+                k.gkv[144 * i : 144 * i + 144, :] = low(rotate_block(sums[144 * i : 144 * i + 144], cosine, -sine))
+            k.gbytes[:, 128:256] += dot_tn(k.hot[8 * part : 8 * part + 8].reshape(1152, 256), k.gkv[...])
+        point(k, f"b0_keys{part}")
+    gbytes = low(k.gbytes[...])
+    k.headgrad[...] = low(dot_tn(k.normed[...], gbytes)).reshape(32, 16, 256)
+    stage = Stage(
+        k,
+        k.headgot,
+        [(k.headgrad.at[pl.ds(16 * (1 - k.g), 16)], k.headgot, k.dev(1 - k.g, k.z, k.y, k.x))],
+    )
+    grad, k.gain_grads[0] = norm_back(k.table[...], k.gain[0:1, :], dot_nt(gbytes, k.wh[...]))
+    total = k.tgrad[...] + grad
+    total = jnp.concatenate([total[:, 0:256].reshape(32, 8, 256), total[:, 256:512].reshape(32, 8, 256)], axis=1)
+    k.gr[:, :, :, :, EG : EG + 16, 0:256] = low(total).reshape(2, 4, 2, 2, 16, 256)
+    return stage, (out,)
+
+
+def send_head_grads(k, stage):
+    with scope("headcore"):
+        stage.wait()
+    total = k.headgrad[pl.ds(16 * k.g, 16)].astype(F32) + k.headgot[...].astype(F32)
+    k.headsum[...] = low(total)
+    k.headback[k.s] = k.headsum[k.s]
+    k.head_sems = [sem(k), sem(k)]
+    around(k, lambda c: k.headsum.at[c], lambda c: k.headback.at[c], *k.head_sems)
+
+
+def store_heads(k):
+    with scope("headback"):
+        for semaphore in k.head_sems:
+            drain(semaphore, k.headback.at[pl.ds(0, 15)])
+    for pair in range(4):
+        even, odd = (k.headback[h].astype(F32) + k.headback[8 + h].astype(F32) for h in (2 * pair, 2 * pair + 1))
+        left = lanes((16, 128)) < 64
+        query = jnp.where(left, even[:, 0:128], roll64(odd[:, 0:128]))
+        keys, vals = pair_kv(even[:, 128:256], odd[:, 128:256])
+        for at, value in ((0, query), (512, keys), (1024, vals)):
+            square(k, value)
+            k.s_qkv[0, :, at + 128 * pair : at + 128 * pair + 128] = value
+    flush(k, "qkv", 0)
+
+
+def finish_back(k, posts):
+    for post in posts:
+        post.done()
+
+
+def byte_matrix(ids):
+    return low(jnp.where(lanes((ids.shape[0], 256)) == ids, 1.0, 0.0))
 
 
 def forward_backward(k):
     rows, short = 144, 48
-    need(k, EG)
-    gains = jnp.sum(k.pk[:, :, :, :, EG : EG + 16, 256:512].astype(F32).reshape(32, 16, 256), axis=0)
-    k.gain[:, 0:256] = gains[0:8]
-    k.gain[:, 256:512] = gains[8:16]
-    k.gain_grads = [None] * 5
-    table = k.pk[:, :, :, :, EG : EG + 16, 0:256].reshape(512, 256)
-    k.columns[0:1, 0:rows] = k.ids[...].astype(F32)
-    k.columns[1:2, 0:rows] = k.targets[...].astype(F32)
+    k.gain_grads, k.pending = [None] * 5, []
+    rotary_tables(k)
+    stage = take_heads(k)
+    point(k, "f0_heads")
+    byte_rows(k)
+    with scope("headcore"):
+        stage.wait()
+    with scope("headrows"):
+        head_rows(k)
     columns = k.columns[...].T
-    ids, targets = columns[0:rows, 0:1].astype(jnp.int32), columns[0:rows, 1:2].astype(jnp.int32)
-    for layer in range(2):
-        rotary_tables(k, layer)
-    first_in = jnp.concatenate([dot(byte_matrix(ids, 0), table), dot(byte_matrix(ids, 1), table)], axis=1)
+    k.own_ids, targets = columns[0:rows, 0:1].astype(jnp.int32), columns[0:rows, 1:2].astype(jnp.int32)
+    first_in = dot(byte_matrix(k.own_ids), low(k.table[...]))
     first = layer_ahead(k, 0, first_in)
     k.shift[8 : 8 + rows, :] = first
     rim = remote(
@@ -1172,7 +1366,7 @@
     grad_up, k.gain_grads[4] = norm_back(upsampled, gain, grad_final)
     k.up[...] = grad_up
     grad_short = exact(pool_matrix((short, rows), 0, 0), grad_up)
-    grad_pooled = layer_back(k, 1, grad_short)
+    grad_pooled, posts = layer_back(k, 1, grad_short)
     k.pool[0:short, :] = grad_pooled
     rim2 = remote(
         k.pool.at[pl.ds(0, 8)], k.pool.at[pl.ds(short, 8)], sem(k), sem(k), (k.g, lax.rem(k.s + 15, 16))
@@ -1182,6 +1376,10 @@
     def _():
         rim2.start()
 
+    for part in range(3):
+        gj = k.hold[1].gj[:, 512 * part : 512 * part + 512]
+        put_block(k, LAYER0 + LAYER_ROWS + QKV + 16 * part, dot_tn(k.hold[1].normed[...], gj))
+    finish_back(k, posts)
     point(k, "b1_rim")
 
     @pl.when(k.s < 15)
@@ -1200,11 +1398,7 @@
     j = lax.broadcasted_iota(jnp.int32, (rows, short + 8), 1)
     spread = jnp.where((t + 2 >= 3 * j) & (t + 2 < 3 * j + 3), 1.0, 0.0)
     grad_first = k.up[...] + exact(spread, k.pool[...] / 3.0)
-    grad_in = layer_back(k, 0, grad_first)
-    table_grad = dot_tn(byte_matrix(ids, 0), low(grad_in[:, 0:256])) + dot_tn(
-        byte_matrix(ids, 1), low(grad_in[:, 256:512])
-    )
-    k.gr[:, :, :, :, EG : EG + 16, 0:256] = low(table_grad).reshape(2, 4, 2, 2, 16, 256)
+    stage, posts = layer_back(k, 0, grad_first)
     fill = [jnp.zeros((3, 256), F32)]
     gains = jnp.concatenate(
         [v[:, 0:256] for v in k.gain_grads] + fill + [v[:, 256:512] for v in k.gain_grads] + fill, axis=0
@@ -1213,6 +1407,8 @@
     k.gr[:, :, :, :, EG : EG + 16, 256:512] = gains.reshape(2, 4, 2, 2, 16, 256)
     k.made.add(EG)
     point(k, "b0_end")
+    send_head_grads(k, stage)
+    finish_back(k, posts)
 
 
 def add_into(ref, other):
@@ -1223,8 +1419,9 @@
     g, z, y, x, dev, gr = k.g, k.z, k.y, k.x, k.dev, k.gr
     a, b, every = pl.ds(r0, rm - r0), pl.ds(rm, r1 - rm), pl.ds(r0, r1 - r0)
     assert k.made.issuperset(range(r0, r1, 16)), name
+    sent = sem(k)
     waiting = Stage(
-        k, k.rc.at[:, :, :, every], [(gr.at[1 - g, :, :, :, every], k.rc.at[:, :, :, every], dev(1 - g, z, y, x))]
+        k, k.rc.at[:, :, :, every], [(gr.at[1 - g, :, :, :, every], k.rc.at[:, :, :, every], dev(1 - g, z, y, x))], sent
     )
     yield
     with scope(f"rw_{name}"):
@@ -1237,47 +1434,76 @@
             place = (n // 4, lax.rem(n // 2, 2), lax.rem(n, 2), every)
             add_into(gr.at[(g,) + place], k.rc.at[place])
 
-    waiting = Stage(
-        k,
-        k.r2.at[:, :, every],
-        [
-            (gr.at[g, :, :, 1 - x, a], k.r2.at[:, :, a], dev(g, z, y, 1 - x)),
-            (gr.at[g, :, 1 - y, :, b], k.r2.at[:, :, b], dev(g, z, 1 - y, x)),
-        ],
-    )
-    yield
-    with scope(f"rw_{name}"):
-        waiting.wait()
-
-    @pl.loop(0, 8)
-    def _(n):
-        add_into(gr.at[g, n // 2, lax.rem(n, 2), x, a], k.r2.at[n // 2, lax.rem(n, 2), a])
-        add_into(gr.at[g, n // 2, y, lax.rem(n, 2), b], k.r2.at[n // 2, lax.rem(n, 2), b])
-
-    waiting = Stage(
-        k,
-        k.r1.at[:, every],
-        [
-            (gr.at[g, :, 1 - y, x, a], k.r1.at[:, a], dev(g, z, 1 - y, x)),
-            (gr.at[g, :, y, 1 - x, b], k.r1.at[:, b], dev(g, z, y, 1 - x)),
-        ],
-    )
-    yield
-    with scope(f"rw_{name}"):
-        waiting.wait()
-
-    @pl.loop(0, 4)
-    def _(n):
-        add_into(gr.at[g, n, y, x, every], k.r1.at[n, every])
-
-    moves = []
-    for n in (2, 1, 3):
-        to = lax.rem(z + n, 4)
-        moves.append((gr.at[g, to, y, x, every], k.rz.at[n - 1, every], dev(g, to, y, x)))
-    waiting = Stage(k, k.rz.at[:, every], moves)
-    yield
-    with scope(f"rw_{name}"):
-        waiting.wait()
+    def wait(waiting):
+        with scope(f"rw_{name}"):
+            waiting.wait()
+
+    last = name in Z_FIRST
+    planes, depth = (pl.ds(z, 1), 1) if last else (pl.ds(0, 4), 4)
+    slots = pl.ds(0, depth)
+
+    def plane(n):
+        return z if last else n
+
+    def across():
+        waiting = Stage(
+            k,
+            k.r2.at[slots, :, every],
+            [
+                (gr.at[g, planes, :, 1 - x, a], k.r2.at[slots, :, a], dev(g, z, y, 1 - x)),
+                (gr.at[g, planes, 1 - y, :, b], k.r2.at[slots, :, b], dev(g, z, 1 - y, x)),
+            ],
+            sent,
+        )
+        yield
+        wait(waiting)
+
+        @pl.loop(0, 2 * depth)
+        def _(n):
+            m, w = n // 2, lax.rem(n, 2)
+            add_into(gr.at[g, plane(m), w, x, a], k.r2.at[m, w, a])
+            if r1 > rm:
+                add_into(gr.at[g, plane(m), y, w, b], k.r2.at[m, w, b])
+
+        waiting = Stage(
+            k,
+            k.r1.at[slots, every],
+            [
+                (gr.at[g, planes, 1 - y, x, a], k.r1.at[slots, a], dev(g, z, 1 - y, x)),
+                (gr.at[g, planes, y, 1 - x, b], k.r1.at[slots, b], dev(g, z, y, 1 - x)),
+            ],
+            sent,
+        )
+        yield
+        wait(waiting)
+
+        @pl.loop(0, depth)
+        def _(n):
+            add_into(gr.at[g, plane(n), y, x, every], k.r1.at[n, every])
+
+    def along():
+        moves = []
+        for n in (2, 1, 3):
+            to = lax.rem(z + n, 4)
+            if last:
+                moves.append((gr.at[g, to, :, :, every], k.rl.at[n - 1], dev(g, to, y, x)))
+            else:
+                moves.append((gr.at[g, to, y, x, every], k.rz.at[n - 1, every], dev(g, to, y, x)))
+        waiting = Stage(k, k.rl if last else k.rz.at[:, every], moves, sent)
+        yield
+        wait(waiting)
+        if last:
+            for n in range(4):
+                ref = gr.at[g, z, n // 2, n % 2, every]
+                total = ref[...].astype(F32)
+                for slot in range(3):
+                    total = total + k.rl[slot, n // 2, n % 2].astype(F32)
+                ref[...] = low(total)
+
+    for way in (along, across) if last else (across, along):
+        yield from way()
+    if last:
+        k.rz[:, every] = jnp.zeros((3, r1 - r0, D), LOW)
     k.summed.update(range(r0, r1, 16))
     yield
 
@@ -1364,7 +1590,8 @@
     stores = [(range(EG, EG + 16), store_rest, ()), (range(HEAD, HEAD + 16), store_head, ())]
     for layer in range(2):
         base = LAYER0 + layer * LAYER_ROWS
-        stores.append((range(base + QKV, base + QKV + 48), store_qkv, (layer,)))
+        if layer == 1:
+            stores.append((range(base + QKV, base + QKV + 48), store_qkv, (layer,)))
         stores.append((range(base + OUT, base + OUT + 16), store_out, (layer,)))
         stores.append((range(base + UP, base + UP + 64), store_up, (layer,)))
         stores.append((range(base + DOWN, base + DOWN + 64), store_down, (layer,)))
@@ -1381,6 +1608,7 @@
         for _ in k.reduces[name]:
             store_ready(k)
     store_ready(k)
+    store_heads(k)
     lane = lanes((8, 128))
     k.stat[0] = jnp.where(lane == 0, k.sq, jnp.where(lane == 1, k.loss, 0.0))
     me = g * 16 + k.s
@@ -1402,7 +1630,12 @@
     "ids", "targets", "lengths", "w_qkv", "w_out", "w_up", "w_down", "embed", "head", "gains",
 )
 OUT_NAMES = ("g_qkv", "g_out", "g_up", "g_down", "g_embed", "g_head", "g_gains", "stats")
-SEMS = 168
+SEMS = 128
+
+
+LATER = (
+    "sendbox", "inbox", "dbox", "kvbox", "back", "kvback", "dkv", "dkv_out", "dkv_in", "h_hidden", "h_normed", "h_gj"
+)
 
 
 def scratch_shapes():
@@ -1413,12 +1646,30 @@
         "r2": ((4, 2, ROWS, D), LOW),
         "r1": ((4, ROWS, D), LOW),
         "rz": ((3, ROWS, D), LOW),
+        "rl": ((3, 2, 2, max([16] + [PIECES[n][2] - PIECES[n][0] for n in Z_FIRST]), D), LOW),
         "gain": ((8, D), F32),
         "shift": ((152, D), F32),
         "pool": ((56, D), F32),
         "up": ((144, D), F32),
         "stat": ((32, 8, 128), F32),
         "columns": ((128, 256), F32),
+        "headout": ((8, 16, 256), LOW),
+        "wbox": ((32, 16, 256), LOW),
+        "wh": ((D, 256), LOW),
+        "table": ((256, D), F32),
+        "normed": ((256, D), LOW),
+        "hot": ((16, 144, 256), LOW),
+        "q0": ((16, 144, 128), LOW),
+        "kv0": ((16, 144, 128), LOW),
+        "cosb": ((16, 128), F32),
+        "sinb": ((16, 128), F32),
+        "tgrad": ((256, D), F32),
+        "gbytes": ((256, 256), F32),
+        "gkv": ((1152, 128), LOW),
+        "headgrad": ((32, 16, 256), LOW),
+        "headgot": ((16, 16, 256), LOW),
+        "headsum": ((16, 16, 256), LOW),
+        "headback": ((16, 16, 256), LOW),
         "s_qkv": ((2, 16, 3 * D), F32),
         "s_out": ((2, 16, D), F32),
         "s_up": ((2, 16, 4 * D), F32),
@@ -1455,9 +1706,11 @@
             ("h_second", (rows, D), LOW),
             ("h_pre", (rows, 4 * D), F32),
             ("h_act", (rows, 4 * D), LOW),
-            ("h_gj", (rows, D), LOW),
+            ("h_gj", (rows, 3 * D), LOW),
+            ("h_gpre", (rows, 4 * D), LOW),
         ):
-            shapes[name + str(layer)] = (shape, kind)
+            if layer == 1 or name not in LATER:
+                shapes[name + str(layer)] = (shape, kind)
     return shapes
 
 
@@ -1466,7 +1719,7 @@
     "cos", "sin", "sendbox", "inbox", "abox", "home", "gsend", "gbox", "dbox", "back", "lse", "att", "dkvt", "dkv",
     "dkv_out", "dkv_in", "kvbox", "kvback",
 )
-HELD = ("hidden", "normed", "flat", "middle", "second", "pre", "act", "gj")
+HELD = ("hidden", "normed", "flat", "middle", "second", "pre", "act", "gj", "gpre")
 
 
 def update_kernel(*refs):

time: 187 us -> 159 us (0.85)
  Pallas kernels: 186 us -> 158 us
    pallas_call x1, Pallas kernels: 181 us -> 153 us  [on_device_fast(): pl.pallas_call(kernel, name='step', out_shape=shard_shapes + [jax.ShapeDt...]
where the time goes in v5:
time: 159 us
  Pallas kernels  158 us (99%)
    pallas_call x1, Pallas kernels, on_device_fast(): pl.pallas_call(kernel, name='step', out_shape=shard_shapes + [jax.ShapeDt...  153 us
    pallas_call x1, Pallas kernels, on_device_fast(): pl.pallas_call(update_kernel, name='update', out_shape=shard_shapes * 3 +...  4.71 us

profile of v5, /device:TPU:0, one launch (start us, length us, event | category | flops | bytes accessed | tf_op | source)
XLA Modules:
  0.0 159.0 jit_solution(12067514370181066576)
XLA Ops:
  0.7 153.4 %step.1 = (f32[2,16,1536]{2,1,0:T(8,128)}, f32[2,16,512]{2,1,0:T(8,128)}, f32[2,16,2048]{2,1,0:T(8,128)}, f32[2,64,512]{2,1,0:T(8,128)}, f32[8,512]{1,0:T(8,128)...) custom-call(s32[1,144]{1,0:T(1,128)} %refs_0_.1, s32[1,144]{1,0:T(1,128)} %refs_1_.1, s32[1,8]{1,0:T(1,128)} %refs_2_.1, ...), custom_call_target="tpu_custom_call" | custom-call | tf_op jit(solution)/shard_map/step/pallas_call | solution.py:1750
  154.1 4.7 %update.1 = (f32[2,16,1536]{2,1,0:T(8,128)}, f32[2,16,512]{2,1,0:T(8,128)}, f32[2,16,2048]{2,1,0:T(8,128)}, f32[2,64,512]{2,1,0:T(8,128)}, f32[8,512]{1,0:T(8,12...) custom-call(f32[8,128]{1,0:T(8,128)} %get-tuple-element.54.refs_0_, ...), custom_call_target="tpu_custom_call" | custom-call | tf_op jit(solution)/shard_map/update/pallas_call | solution.py:1761

commit v6 on v5

--- a/solution.py
+++ b/solution.py
@@ -395,8 +395,7 @@
 
 EG, LAYER0, LAYER_ROWS = 0, -32, 192
 QKV, OUT, UP, DOWN = 0, 48, 64, 128
-HEAD = LAYER0 + 2 * LAYER_ROWS
-ROWS = HEAD + 16
+ROWS = LAYER0 + 2 * LAYER_ROWS
 PIECES = {
     "A": (0, 16, 16),
     "B": (16, 32, 64),
@@ -404,36 +403,37 @@
     "b": (96, 128, 160),
     "C": (160, 192, 224),
     "D": (224, 256, 288),
-    "d": (288, 320, 336),
-    "h": (336, 352, 368),
+    "d": (288, 304, 320),
+    "h": (320, 336, 352),
 }
 Z_LAST, Z_FIRST = "h", "h"
 SCHEDULE = {
-    "start": "BAbhBEAh",
-    "heads": "dBAEbBCE",
-    "f0_heads": "DAb",
+    "start": "AbhBh",
+    "heads": "AbABCb",
+    "f0_heads": "EDAB",
+    "f0_got": "E",
     "f0_mid0": "C",
-    "f0_part0": "dE",
-    "f0_part1": "Cbh",
-    "f0_home": "D",
-    "f0_rim": "dC",
-    "f1_sent": "D",
-    "f1_got": "dh",
+    "f0_part0": "d",
+    "f0_mid1": "bE",
+    "f0_part1": "hCBE",
+    "f0_home": "d",
+    "f0_rim": "DCd",
+    "f1_sent": "Dh",
+    "f1_take": "d",
     "f1_part0": "D",
-    "b1_ff": "d",
-    "b1_sent": "dD",
-    "b1_sums": "hDhd",
-    "b1_rim": "CDC",
-    "b0_ff": "BDB",
-    "b0_sent": "bCEd",
-    "b0_mid1": "E",
-    "b0_part1": "B",
+    "b1_ff": "D",
+    "b1_sent": "hD",
+    "b1_part0": "d",
+    "b1_sums": "dDh",
+    "b1_rim": "CdC",
+    "b0_ff": "bhBDb",
+    "b0_sent": "EdC",
+    "b0_part1": "E",
     "b0_keys1": "b",
     "b0_mid0": "C",
-    "b0_part0": "h",
-    "b0_keys0": "B",
-    "b0_end": "E",
-    "tail": "AbAEbh",
+    "b0_part0": "B",
+    "b0_end": "AEb",
+    "tail": "ABEABh",
 }
 
 
@@ -580,18 +580,12 @@
 
     own = k.pk.at[g, z, y, x]
     own[EG : EG + 16, 0:256] = low(jnp.concatenate([k.embed[:, 0:256], k.embed[:, 256:512]], axis=0))
-    place = lanes((16, 256)) - 16 * s == lax.broadcasted_iota(jnp.int32, (16, 256), 0)
-    gains = exact(k.gains[...], jnp.where(place, 1.0, 0.0))
-    gains = jnp.concatenate([gains, jnp.zeros((3, 256), F32)], axis=0)
-    gains = jnp.concatenate([jnp.where(g == 0, gains, 0.0), jnp.where(g == 1, gains, 0.0)], axis=0)
-    own[EG : EG + 16, 256:512] = low(gains)
+    own[EG : EG + 16, 256:512] = low(k.head[...])
     k.columns[0:1, 0:144] = k.ids[...].astype(F32)
     k.columns[1:2, 0:144] = k.targets[...].astype(F32)
     pack_heads(k)
     pack_layer(k, own, 0)
     pack_layer(k, own, 1)
-    own[HEAD : HEAD + 16, 0:256] = low(k.head[...])
-    own[HEAD : HEAD + 16, 256:512] = jnp.zeros((16, 256), LOW)
     with scope("barrier"):
         pl.semaphore_wait(barrier, 31)
     k.gathers = {name: gather_piece(k, name, *rows) for name, rows in PIECES.items()}
@@ -624,10 +618,12 @@
 
 def pack_heads(k):
     row, lane = lax.broadcasted_iota(jnp.int32, (16, 128), 0), lanes((16, 128))
-    ids = jnp.zeros((16, 128), F32)
+    place = lanes((16, 128)) - 64 == lax.broadcasted_iota(jnp.int32, (16, 128), 0)
+    gains = exact(k.gains[...], jnp.where(place, 1.0, 0.0))
+    ids = jnp.concatenate([gains, jnp.zeros((3, 128), F32), jnp.zeros((8, 128), F32)], axis=0)
     for j in range(3):
         part = pltpu.roll(k.columns[0:8, :], (64 - 48 * j) % 256, 1)[0:1, 0:128]
-        ids = jnp.where((row == j) & (lane >= 64) & (lane < 112), part, ids)
+        ids = jnp.where((row == 8 + j) & (lane >= 64) & (lane < 112), part, ids)
     for pair in range(4):
         query = k.w_qkv[0, :, 128 * pair : 128 * pair + 128]
         keys = k.w_qkv[0, :, 512 + 128 * pair : 640 + 128 * pair]
@@ -669,14 +665,25 @@
     return jnp.where(left, cosine, 1.0), jnp.where(left, sine, 0.0)
 
 
+def lane_copies(shape, axis):
+    narrow = lax.broadcasted_iota(jnp.int32, shape, axis)
+    wide = lax.broadcasted_iota(jnp.int32, shape, 1 - axis)
+    return jnp.where(narrow - 64 == wide % 16, 1.0, 0.0)
+
+
+def device_lanes():
+    shape = (32, 8, 512)
+    return lanes(shape) // 16 == lax.broadcasted_iota(jnp.int32, shape, 0)
+
+
 def byte_rows(k):
     need(k, EG)
-    packed = k.pk[:, :, :, :, EG : EG + 16, :].astype(F32).reshape(32, 16, 512)
-    gains = jnp.sum(packed[:, :, 256:512], axis=0)
-    k.gain[:, 0:256] = gains[0:8]
-    k.gain[:, 256:512] = gains[8:16]
+    packed = k.pk[:, :, :, :, EG : EG + 16, 0:256].astype(F32).reshape(32, 16, 256)
+    gains = low(k.wbox[...].astype(F32)[:, 0:8, 0:128].reshape(256, 128))
+    gains = dot(gains, low(lane_copies((128, 512), 0))).reshape(32, 8, 512)
+    k.gain[...] = jnp.sum(jnp.where(device_lanes(), gains, 0.0), axis=0)
     table = jnp.concatenate(
-        [packed[:, 0:8, 0:256].reshape(256, 256), packed[:, 8:16, 0:256].reshape(256, 256)], axis=1
+        [packed[:, 0:8].reshape(256, 256), packed[:, 8:16].reshape(256, 256)], axis=1
     )
     k.table[...] = table
     unit, _ = norm_parts(table)
@@ -686,7 +693,7 @@
 def head_rows(k):
     group = k.s // 8
     for b in range(16):
-        k.columns[16 + 4 * b : 20 + 4 * b, 0:128] = k.wbox[group * 16 + b].astype(F32)[0:4, 0:128]
+        k.columns[16 + 4 * b : 20 + 4 * b, 0:128] = k.wbox[group * 16 + b].astype(F32)[8:12, 0:128]
     columns = k.columns[...].T
     weights = k.wbox[...].astype(F32).reshape(512, 256)
     lane = lanes(weights.shape)
@@ -1245,13 +1252,19 @@
             k.gbytes[:, 128:256] += dot_tn(k.hot[8 * part : 8 * part + 8].reshape(1152, 256), k.gkv[...])
         point(k, f"b0_keys{part}")
     gbytes = low(k.gbytes[...])
-    k.headgrad[...] = low(dot_tn(k.normed[...], gbytes)).reshape(32, 16, 256)
+    grad, k.gain_grads[0] = norm_back(k.table[...], k.gain[0:1, :], dot_nt(gbytes, k.wh[...]))
+    gains = jnp.concatenate(k.gain_grads + [jnp.zeros((3, D), F32)], axis=0)
+    gains = jnp.where(device_lanes(), jnp.broadcast_to(gains[None], (32, 8, 512)), 0.0).reshape(256, 512)
+    gains = dot(low(gains), low(lane_copies((512, 128), 1))).reshape(32, 8, 128)
+    gains = jnp.concatenate([gains, jnp.zeros((32, 8, 128), F32)], axis=1)
+    heads = dot_tn(k.normed[...], gbytes).reshape(32, 16, 256)
+    k.headgrad[:, :, 0:128] = low(heads[:, :, 0:128] + gains)
+    k.headgrad[:, :, 128:256] = low(heads[:, :, 128:256])
     stage = Stage(
         k,
         k.headgot,
         [(k.headgrad.at[pl.ds(16 * (1 - k.g), 16)], k.headgot, k.dev(1 - k.g, k.z, k.y, k.x))],
     )
-    grad, k.gain_grads[0] = norm_back(k.table[...], k.gain[0:1, :], dot_nt(gbytes, k.wh[...]))
     total = k.tgrad[...] + grad
     total = jnp.concatenate([total[:, 0:256].reshape(32, 8, 256), total[:, 256:512].reshape(32, 8, 256)], axis=1)
     k.gr[:, :, :, :, EG : EG + 16, 0:256] = low(total).reshape(2, 4, 2, 2, 16, 256)
@@ -1281,6 +1294,12 @@
             square(k, value)
             k.s_qkv[0, :, at + 128 * pair : at + 128 * pair + 128] = value
     flush(k, "qkv", 0)
+    gains = sum(k.headback[c].astype(F32)[0:8, 0:128] for c in range(16))
+    row, column = lax.broadcasted_iota(jnp.int32, (128, 16), 0), lax.broadcasted_iota(jnp.int32, (128, 16), 1)
+    gains = exact(gains, jnp.where(row - 64 == column, 1.0, 0.0))[0:5]
+    square(k, gains)
+    k.s_gains[...] = gains
+    flush(k, "gains")
 
 
 def finish_back(k, posts):
@@ -1298,9 +1317,9 @@
     rotary_tables(k)
     stage = take_heads(k)
     point(k, "f0_heads")
-    byte_rows(k)
     with scope("headcore"):
         stage.wait()
+    byte_rows(k)
     with scope("headrows"):
         head_rows(k)
     columns = k.columns[...].T
@@ -1342,8 +1361,7 @@
     gain = k.gain[4:5, :]
     unit, _ = norm_parts(upsampled)
     final = low(unit * gain)
-    need(k, HEAD)
-    head = k.pk[:, :, :, :, HEAD : HEAD + 16, 0:256].reshape(512, 256)
+    head = k.pk[:, :, :, :, EG : EG + 16, 256:512].reshape(512, 256)
     logits = dot(final, head)
     top = jnp.max(logits, axis=-1, keepdims=True)
     log_total = top + jnp.log(jnp.sum(jnp.exp(logits - top), axis=-1, keepdims=True))
@@ -1359,9 +1377,7 @@
         begin = begin + size
     k.loss = jnp.sum((log_total - picked) / length, axis=0, keepdims=True)
     grad_logits = low((jnp.exp(logits - log_total) - hot) / length)
-    k.gr[:, :, :, :, HEAD : HEAD + 16, 0:256] = low(dot_tn(final, grad_logits)).reshape(2, 4, 2, 2, 16, 256)
-    k.made.add(HEAD)
-    k.gr[:, :, :, :, HEAD : HEAD + 16, 256:512] = jnp.zeros((2, 4, 2, 2, 16, 256), LOW)
+    k.gr[:, :, :, :, EG : EG + 16, 256:512] = low(dot_tn(final, grad_logits)).reshape(2, 4, 2, 2, 16, 256)
     grad_final = dot_nt(grad_logits, head)
     grad_up, k.gain_grads[4] = norm_back(upsampled, gain, grad_final)
     k.up[...] = grad_up
@@ -1399,12 +1415,6 @@
     spread = jnp.where((t + 2 >= 3 * j) & (t + 2 < 3 * j + 3), 1.0, 0.0)
     grad_first = k.up[...] + exact(spread, k.pool[...] / 3.0)
     stage, posts = layer_back(k, 0, grad_first)
-    fill = [jnp.zeros((3, 256), F32)]
-    gains = jnp.concatenate(
-        [v[:, 0:256] for v in k.gain_grads] + fill + [v[:, 256:512] for v in k.gain_grads] + fill, axis=0
-    )
-    gains = jnp.broadcast_to(low(gains)[None], (32, 16, 256))
-    k.gr[:, :, :, :, EG : EG + 16, 256:512] = gains.reshape(2, 4, 2, 2, 16, 256)
     k.made.add(EG)
     point(k, "b0_end")
     send_head_grads(k, stage)
@@ -1565,29 +1575,18 @@
     flush(k, "down", layer)
 
 
-def store_head(k):
-    v = own_sum(k, HEAD, 16)[:, 0:256]
-    square(k, v)
-    k.s_head[...] = v
-    flush(k, "head")
-
-
 def store_rest(k):
     v = own_sum(k, EG, 16)
-    square(k, v[:, 0:256])
+    square(k, v)
     k.s_embed[:, 0:256] = v[0:8, 0:256]
     k.s_embed[:, 256:512] = v[8:16, 0:256]
-    gains = jnp.where(k.g == 0, v[0:8, 256:512], v[8:16, 256:512])
-    row, column = lax.broadcasted_iota(jnp.int32, (256, 16), 0), lax.broadcasted_iota(jnp.int32, (256, 16), 1)
-    gains = exact(gains, jnp.where(row - 16 * k.s == column, 1.0, 0.0))[0:5]
-    square(k, gains)
-    k.s_gains[...] = gains
+    k.s_head[...] = v[:, 256:512]
     flush(k, "embed")
-    flush(k, "gains")
+    flush(k, "head")
 
 
 def store_ready(k):
-    stores = [(range(EG, EG + 16), store_rest, ()), (range(HEAD, HEAD + 16), store_head, ())]
+    stores = [(range(EG, EG + 16), store_rest, ())]
     for layer in range(2):
         base = LAYER0 + layer * LAYER_ROWS
         if layer == 1:
@@ -1735,7 +1734,12 @@
     for i in order:
         drain(sems.at[i], held[i])
         gradient, master, first, second = (held[i][j] for j in range(4))
-        results = adam_update(master, gradient * clip, first, second, STEP_RATES[i], WEIGHT_DECAYS[i])
+        gradient = gradient * clip
+        first = BETA_ONE * first + (1.0 - BETA_ONE) * gradient
+        second = BETA_TWO * second + (1.0 - BETA_TWO) * gradient * gradient
+        step = first * (1.0 / (1.0 - BETA_ONE**STEP))
+        spread = jnp.sqrt(second * (1.0 / (1.0 - BETA_TWO**STEP))) + EPSILON
+        results = (master - STEP_RATES[i] * (step / spread + WEIGHT_DECAYS[i] * master), first, second)
         for j in range(3):
             made[i][j] = results[j]
         start_all([pltpu.make_async_copy(made[i].at[j], outs[7 * j + i], out_sems.at[i]) for j in range(3)])

time: 159 us -> 156 us (0.981)
  Pallas kernels: 158 us -> 155 us
    pallas_call x1, Pallas kernels: 153 us -> 150 us  [on_device_fast(): pl.pallas_call(kernel, name='step', out_shape=shard_shapes + [jax.ShapeDt...]
where the time goes in v6:
time: 156 us
  Pallas kernels  155 us (99%)
    pallas_call x1, Pallas kernels, on_device_fast(): pl.pallas_call(kernel, name='step', out_shape=shard_shapes + [jax.ShapeDt...  150 us
    pallas_call x1, Pallas kernels, on_device_fast(): pl.pallas_call(update_kernel, name='update', out_shape=shard_shapes * 3 +...  4.71 us

profile of v6, /device:TPU:0, one launch (start us, length us, event | category | flops | bytes accessed | tf_op | source)
XLA Modules:
  0.0 155.6 jit_solution(15502530852181163822)
XLA Ops:
  0.7 150.0 %step.1 = (f32[2,16,1536]{2,1,0:T(8,128)}, f32[2,16,512]{2,1,0:T(8,128)}, f32[2,16,2048]{2,1,0:T(8,128)}, f32[2,64,512]{2,1,0:T(8,128)}, f32[8,512]{1,0:T(8,128)...) custom-call(s32[1,144]{1,0:T(1,128)} %refs_0_.1, s32[1,144]{1,0:T(1,128)} %refs_1_.1, s32[1,8]{1,0:T(1,128)} %refs_2_.1, ...), custom_call_target="tpu_custom_call" | custom-call | tf_op jit(solution)/shard_map/step/pallas_call | solution.py:1754
  150.7 4.7 %update.1 = (f32[2,16,1536]{2,1,0:T(8,128)}, f32[2,16,512]{2,1,0:T(8,128)}, f32[2,16,2048]{2,1,0:T(8,128)}, f32[2,64,512]{2,1,0:T(8,128)}, f32[8,512]{1,0:T(8,12...) custom-call(f32[8,128]{1,0:T(8,128)} %get-tuple-element.54.refs_0_, ...), custom_call_target="tpu_custom_call" | custom-call | tf_op jit(solution)/shard_map/update/pallas_call | solution.py:1765

commit v7 on v6

--- a/solution.py
+++ b/solution.py
@@ -1,4 +1,3 @@
-import contextlib
 import functools
 
 import jax
@@ -407,33 +406,70 @@
     "h": (320, 336, 352),
 }
 Z_LAST, Z_FIRST = "h", "h"
+(
+    START,
+    HEADS,
+    F0_HEADS,
+    F0_GOT,
+    F0_MID0,
+    F0_MID1,
+    F0_PART0,
+    F0_PART1,
+    F0_HOME,
+    F0_UP,
+    F0_RIM,
+    F0_END,
+    F1_SENT,
+    F1_TAKE,
+    F1_GOT,
+    F1_PART0,
+    F1_HOME,
+    F1_OUT,
+    F1_UP,
+    B1_FF,
+    B1_SENT,
+    B1_PART0,
+    B1_SUMS,
+    B1_HOME,
+    B1_RIM,
+    B0_FF,
+    B0_SENT,
+    B0_MID0,
+    B0_MID1,
+    B0_PART0,
+    B0_PART1,
+    B0_KEYS0,
+    B0_KEYS1,
+    B0_END,
+    TAIL,
+) = range(35)
 SCHEDULE = {
-    "start": "AbhBh",
-    "heads": "AbABCb",
-    "f0_heads": "EDAB",
-    "f0_got": "E",
-    "f0_mid0": "C",
-    "f0_part0": "d",
-    "f0_mid1": "bE",
-    "f0_part1": "hCBE",
-    "f0_home": "d",
-    "f0_rim": "DCd",
-    "f1_sent": "Dh",
-    "f1_take": "d",
-    "f1_part0": "D",
-    "b1_ff": "D",
-    "b1_sent": "hD",
-    "b1_part0": "d",
-    "b1_sums": "dDh",
-    "b1_rim": "CdC",
-    "b0_ff": "bhBDb",
-    "b0_sent": "EdC",
-    "b0_part1": "E",
-    "b0_keys1": "b",
-    "b0_mid0": "C",
-    "b0_part0": "B",
-    "b0_end": "AEb",
-    "tail": "ABEABh",
+    START: "AbhBh",
+    HEADS: "AbABCb",
+    F0_HEADS: "EDAB",
+    F0_GOT: "E",
+    F0_MID0: "C",
+    F0_PART0: "d",
+    F0_MID1: "bE",
+    F0_PART1: "hCBE",
+    F0_HOME: "d",
+    F0_RIM: "DCd",
+    F1_SENT: "Dh",
+    F1_TAKE: "d",
+    F1_PART0: "D",
+    B1_FF: "D",
+    B1_SENT: "hD",
+    B1_PART0: "d",
+    B1_SUMS: "dDh",
+    B1_RIM: "CdC",
+    B0_FF: "bhBDb",
+    B0_SENT: "EdC",
+    B0_PART1: "E",
+    B0_KEYS1: "b",
+    B0_MID0: "C",
+    B0_PART0: "B",
+    B0_END: "AEb",
+    TAIL: "ABEABh",
 }
 
 
@@ -495,10 +531,6 @@
 
 class Bag:
     pass
-
-
-def scope(name):
-    return contextlib.nullcontext()
 
 
 def remote(src, dst, send, recv, device):
@@ -586,21 +618,20 @@
     pack_heads(k)
     pack_layer(k, own, 0)
     pack_layer(k, own, 1)
-    with scope("barrier"):
-        pl.semaphore_wait(barrier, 31)
+    pl.semaphore_wait(barrier, 31)
     k.gathers = {name: gather_piece(k, name, *rows) for name, rows in PIECES.items()}
     k.reduces = {name: reduce_piece(k, name, *rows) for name, rows in PIECES.items()}
     k.made, k.summed, k.stored = set(), set(), set()
     k.flushed, k.sq = [], jnp.zeros((1, 1), F32)
-    point(k, "start")
+    point(k, START)
     spread_heads(k)
-    point(k, "heads")
+    point(k, HEADS)
     forward_backward(k)
     finish_grads(k)
 
 
 def point(k, name):
-    coming = name[0] in "sphf"
+    coming = name < B1_FF
     for piece in SCHEDULE.get(name, ""):
         next((k.gathers if coming else k.reduces)[piece], None)
         if not coming:
@@ -647,9 +678,8 @@
 
 
 def take_heads(k):
-    with scope("heads"):
-        for semaphore in k.head_sems:
-            drain(semaphore, k.wbox.at[pl.ds(0, 15)])
+    for semaphore in k.head_sems:
+        drain(semaphore, k.wbox.at[pl.ds(0, 15)])
     share = k.wbox.at[pl.ds(16 * k.g, 16)]
     return Stage(k, share, [(share, share, k.dev(1 - k.g, k.z, k.y, k.x))])
 
@@ -768,8 +798,7 @@
         return Stage(k, total, [(ref, ref, device) for ref, device in moves], sent)
 
     def wait(waiting):
-        with scope(f"gw_{name}"):
-            waiting.wait()
+        waiting.wait()
 
     planes = pl.ds(z, 1) if name in Z_LAST else pl.ds(0, 4)
 
@@ -1081,18 +1110,17 @@
     inbox = k.inbox[layer]
     out = ToHeads(k, sendbox, inbox)
     out.send()
-    point(k, "f1_sent")
+    point(k, F1_SENT)
     sent, shared = sem(k), [sem(k), sem(k)]
     mine = my_blocks(k)
     for part in range(2):
         if part == 1:
-            point(k, "f1_take")
-        with scope("take"):
-            out.take(part)
+            point(k, F1_TAKE)
+        out.take(part)
         for b in mine[4 * part : 4 * part + 4]:
             ref = inbox.at[b, pl.ds(pad, rows)]
             remote(ref, ref, sent, shared[part], k.dev(1 - k.g, k.z, k.y, k.x)).start()
-    point(k, "f1_got")
+    point(k, F1_GOT)
     k.pending += [out.done, lambda: drain(sent, inbox.at[pl.ds(0, 8), pl.ds(pad, rows)])]
     return shared
 
@@ -1103,7 +1131,7 @@
     hold = k.hold[layer]
     home = k.home[layer]
     if layer == 0:
-        point(k, "f0_got")
+        point(k, F0_GOT)
         shared = []
     else:
         hold.hidden[...] = hidden
@@ -1111,16 +1139,13 @@
     back = FromHeads(k, k.abox[layer], home)
     for part in range(2 - layer):
         for semaphore in shared:
-            with scope("share"):
-                drain(semaphore, k.inbox[layer].at[pl.ds(0, 4), pl.ds(pad, rows)])
-        with scope("attend"):
-            attention_forward(k, layer, part, back, lambda: point(k, f"f0_mid{part}"))
-        point(k, f"f{layer}_part{part}")
-    with scope("home"):
-        back.take()
-    point(k, f"f{layer}_home")
+            drain(semaphore, k.inbox[layer].at[pl.ds(0, 4), pl.ds(pad, rows)])
+        attention_forward(k, layer, part, back, lambda: point(k, (F0_MID0, F0_MID1)[part]))
+        point(k, (F0_PART0, F0_PART1)[part] if layer == 0 else F1_PART0)
+    back.take()
+    point(k, (F0_HOME, F1_HOME)[layer])
     if layer == 1:
-        point(k, "f1_out")
+        point(k, F1_OUT)
     for n in range(4):
         pair = unpack_pair(
             home[2 * n].astype(F32)[: rows // 2], home[2 * n + 1].astype(F32)[: rows // 2]
@@ -1135,7 +1160,7 @@
         pre = dot(second, block(k, base + UP + 16 * j))
         hold.pre[:, 512 * j : 512 * j + 512] = pre
         hold.act[:, 512 * j : 512 * j + 512] = low(gelu(pre))
-    point(k, f"f{layer}_up")
+    point(k, (F0_UP, F1_UP)[layer])
     need(k, base + DOWN, 64)
     falls = k.pk[:, :, :, :, base + DOWN : base + DOWN + 64, :].reshape(2048, 512)
     output = hold.middle[...] + dot(hold.act[...], falls)
@@ -1165,7 +1190,7 @@
             hold.gpre[:, cols] = grad_pre
         grad_second = grad_second + dot_nt(grad_pre, block(k, base + UP + 16 * c))
     if layer == 1:
-        point(k, "b1_ff")
+        point(k, B1_FF)
     gain = k.gain[2 * layer + 1 : 2 * layer + 2, :]
     grad_mid, k.gain_grads[2 * layer + 1] = norm_back(hold.middle[...], gain, grad_second)
     grad_middle = grad_out + grad_mid
@@ -1187,33 +1212,28 @@
             cols = slice(512 * c, 512 * c + 512)
             put_down(k, base + DOWN, c, dot_tn(hold.act[:, cols], fall))
             put_block(k, base + UP + 16 * c, dot_tn(second, hold.gpre[:, cols]))
-        point(k, "b0_ff")
+        point(k, B0_FF)
     k.dkvt[layer][...] = jnp.zeros_like(k.dkvt[layer])
-    point(k, f"b{layer}_sent")
+    point(k, (B0_SENT, B1_SENT)[layer])
     if layer == 0:
         return head_grads(k, out)
     back = k.back[layer]
     home_q = FromHeads(k, k.dbox[layer], back)
     home_kv = FromHeads(k, k.kvbox[layer], k.kvback[layer])
-    with scope("take"):
-        out.take(0)
-        out.take(1)
-    with scope("unattend"):
-        attention_backward(k, layer, 0, home_q)
+    out.take(0)
+    out.take(1)
+    attention_backward(k, layer, 0, home_q)
     sums = KeySums(k, layer, 0, home_kv)
-    point(k, "b1_part0")
-    with scope("sums"):
-        sums.send()
-    point(k, "b1_sums")
-    with scope("home_q"):
-        home_q.take()
+    point(k, B1_PART0)
+    sums.send()
+    point(k, B1_SUMS)
+    home_q.take()
     cosine, sine = k.cos[layer][...], k.sin[layer][...]
     cos_kv, sin_kv = kv_tables(cosine, sine)
     for part in range(3):
         if part == 1:
-            with scope("home_kv"):
-                home_kv.take()
-            point(k, "b1_home")
+            home_kv.take()
+            point(k, B1_HOME)
         for n in range(4):
             if part == 0:
                 piece = unpack_pair(
@@ -1239,18 +1259,15 @@
     k.tgrad[...] = own
     k.gbytes[...] = jnp.zeros_like(k.gbytes)
     for part in (1, 0):
-        with scope("take"):
-            out.take(part)
-        with scope("unattend"):
-            attention_backward(k, 0, part, None, lambda: point(k, f"b0_mid{part}"))
-        point(k, f"b0_part{part}")
-        with scope("keysums"):
-            sums = k.dkvt[0][:, 1152 * part : 1152 * part + 1152].T
-            for i in range(8):
-                cosine, sine = kv_tables(*block_tables(k, 8 * part + i))
-                k.gkv[144 * i : 144 * i + 144, :] = low(rotate_block(sums[144 * i : 144 * i + 144], cosine, -sine))
-            k.gbytes[:, 128:256] += dot_tn(k.hot[8 * part : 8 * part + 8].reshape(1152, 256), k.gkv[...])
-        point(k, f"b0_keys{part}")
+        out.take(part)
+        attention_backward(k, 0, part, None, lambda: point(k, (B0_MID0, B0_MID1)[part]))
+        point(k, (B0_PART0, B0_PART1)[part])
+        sums = k.dkvt[0][:, 1152 * part : 1152 * part + 1152].T
+        for i in range(8):
+            cosine, sine = kv_tables(*block_tables(k, 8 * part + i))
+            k.gkv[144 * i : 144 * i + 144, :] = low(rotate_block(sums[144 * i : 144 * i + 144], cosine, -sine))
+        k.gbytes[:, 128:256] += dot_tn(k.hot[8 * part : 8 * part + 8].reshape(1152, 256), k.gkv[...])
+        point(k, (B0_KEYS0, B0_KEYS1)[part])
     gbytes = low(k.gbytes[...])
     grad, k.gain_grads[0] = norm_back(k.table[...], k.gain[0:1, :], dot_nt(gbytes, k.wh[...]))
     gains = jnp.concatenate(k.gain_grads + [jnp.zeros((3, D), F32)], axis=0)
@@ -1272,8 +1289,7 @@
 
 
 def send_head_grads(k, stage):
-    with scope("headcore"):
-        stage.wait()
+    stage.wait()
     total = k.headgrad[pl.ds(16 * k.g, 16)].astype(F32) + k.headgot[...].astype(F32)
     k.headsum[...] = low(total)
     k.headback[k.s] = k.headsum[k.s]
@@ -1282,9 +1298,8 @@
 
 
 def store_heads(k):
-    with scope("headback"):
-        for semaphore in k.head_sems:
-            drain(semaphore, k.headback.at[pl.ds(0, 15)])
+    for semaphore in k.head_sems:
+        drain(semaphore, k.headback.at[pl.ds(0, 15)])
     for pair in range(4):
         even, odd = (k.headback[h].astype(F32) + k.headback[8 + h].astype(F32) for h in (2 * pair, 2 * pair + 1))
         left = lanes((16, 128)) < 64
@@ -1316,12 +1331,10 @@
     k.gain_grads, k.pending = [None] * 5, []
     rotary_tables(k)
     stage = take_heads(k)
-    point(k, "f0_heads")
-    with scope("headcore"):
-        stage.wait()
+    point(k, F0_HEADS)
+    stage.wait()
     byte_rows(k)
-    with scope("headrows"):
-        head_rows(k)
+    head_rows(k)
     columns = k.columns[...].T
     k.own_ids, targets = columns[0:rows, 0:1].astype(jnp.int32), columns[0:rows, 1:2].astype(jnp.int32)
     first_in = dot(byte_matrix(k.own_ids), low(k.table[...]))
@@ -1335,7 +1348,7 @@
     def _():
         rim.start()
 
-    point(k, "f0_rim")
+    point(k, F0_RIM)
 
     @pl.when(k.s > 0)
     def _():
@@ -1355,7 +1368,7 @@
         return jnp.where((t >= 3 * j) & (t < 3 * j + 3), 1.0, 0.0)
 
     pooled = exact(pool_matrix((short, rows + 8), 6, 0), k.shift[...]) / 3.0
-    point(k, "f0_end")
+    point(k, F0_END)
     short_out = layer_ahead(k, 1, pooled)
     upsampled = k.shift[8 : 8 + rows, :] + exact(pool_matrix((rows, short), 0, 1), short_out)
     gain = k.gain[4:5, :]
@@ -1396,7 +1409,7 @@
         gj = k.hold[1].gj[:, 512 * part : 512 * part + 512]
         put_block(k, LAYER0 + LAYER_ROWS + QKV + 16 * part, dot_tn(k.hold[1].normed[...], gj))
     finish_back(k, posts)
-    point(k, "b1_rim")
+    point(k, B1_RIM)
 
     @pl.when(k.s < 15)
     def _():
@@ -1416,7 +1429,7 @@
     grad_first = k.up[...] + exact(spread, k.pool[...] / 3.0)
     stage, posts = layer_back(k, 0, grad_first)
     k.made.add(EG)
-    point(k, "b0_end")
+    point(k, B0_END)
     send_head_grads(k, stage)
     finish_back(k, posts)
 
@@ -1434,19 +1447,16 @@
         k, k.rc.at[:, :, :, every], [(gr.at[1 - g, :, :, :, every], k.rc.at[:, :, :, every], dev(1 - g, z, y, x))], sent
     )
     yield
-    with scope(f"rw_{name}"):
+    waiting.wait()
+
+
+    @pl.loop(0, 16)
+    def _(n):
+        place = (n // 4, lax.rem(n // 2, 2), lax.rem(n, 2), every)
+        add_into(gr.at[(g,) + place], k.rc.at[place])
+
+    def wait(waiting):
         waiting.wait()
-
-    with scope("radd"):
-
-        @pl.loop(0, 16)
-        def _(n):
-            place = (n // 4, lax.rem(n // 2, 2), lax.rem(n, 2), every)
-            add_into(gr.at[(g,) + place], k.rc.at[place])
-
-    def wait(waiting):
-        with scope(f"rw_{name}"):
-            waiting.wait()
 
     last = name in Z_FIRST
     planes, depth = (pl.ds(z, 1), 1) if last else (pl.ds(0, 4), 4)
@@ -1602,7 +1612,7 @@
 
 def finish_grads(k):
     g = k.g
-    point(k, "tail")
+    point(k, TAIL)
     for name in PIECES:
         for _ in k.reduces[name]:
             store_ready(k)
@@ -1618,9 +1628,8 @@
         t = lax.rem(me + i, 32)
         remote(k.stat.at[0], k.stat.at[i], sent, got, (t // 16, lax.rem(t, 16))).start()
 
-    with scope("stats"):
-        drain(got, k.stat.at[pl.ds(1, 31)])
-        drain(sent, k.stat.at[pl.ds(1, 31)])
+    drain(got, k.stat.at[pl.ds(1, 31)])
+    drain(sent, k.stat.at[pl.ds(1, 31)])
     k.stats[...] = jnp.sum(k.stat[...], axis=0)
     wait_all(k.flushed)
 

time: 156 us -> 156 us (level)
  no operation moved by 1% of the time
where the time goes in v7:
time: 156 us
  Pallas kernels  155 us (99%)
    pallas_call x1, Pallas kernels, on_device_fast(): pl.pallas_call(kernel, name='step', out_shape=shard_shapes + [jax.ShapeDt...  150 us
    pallas_call x1, Pallas kernels, on_device_fast(): pl.pallas_call(update_kernel, name='update', out_shape=shard_shapes * 3 +...  4.71 us

profile of v7, /device:TPU:0, one launch (start us, length us, event | category | flops | bytes accessed | tf_op | source)
XLA Modules:
  0.0 155.6 jit_solution(15502530852181163822)
XLA Ops:
  0.7 150.0 %step.1 = (f32[2,16,1536]{2,1,0:T(8,128)}, f32[2,16,512]{2,1,0:T(8,128)}, f32[2,16,2048]{2,1,0:T(8,128)}, f32[2,64,512]{2,1,0:T(8,128)}, f32[8,512]{1,0:T(8,128)...) custom-call(s32[1,144]{1,0:T(1,128)} %refs_0_.1, s32[1,144]{1,0:T(1,128)} %refs_1_.1, s32[1,8]{1,0:T(1,128)} %refs_2_.1, ...), custom_call_target="tpu_custom_call" | custom-call | tf_op jit(solution)/shard_map/step/pallas_call | solution.py:1763
  150.7 4.7 %update.1 = (f32[2,16,1536]{2,1,0:T(8,128)}, f32[2,16,512]{2,1,0:T(8,128)}, f32[2,16,2048]{2,1,0:T(8,128)}, f32[2,64,512]{2,1,0:T(8,128)}, f32[8,512]{1,0:T(8,12...) custom-call(f32[8,128]{1,0:T(8,128)} %get-tuple-element.54.refs_0_, ...), custom_call_target="tpu_custom_call" | custom-call | tf_op jit(solution)/shard_map/update/pallas_call | solution.py:1774
